TPU v7x, 32 devices: a whole 2x2x4 slice. The times are simulated.
32 devices in a mesh: gx: 16 (over z, y, core), az: 2 (over x).
Axes of the slice: x: 2, y: 2, z: 4, core: 2. Of those that a mesh axis runs over, the one named last changes fastest.
Arguments:
- state: float32 [5, 256, 256, 512], P(None, 'gx', 'az'), as said below
- sponge_level: int32 [256, 256, 512], P('gx', 'az'), may hold values from 0 to 3
- inv_dx: float32 [256], P('gx'), may hold values from 1 to 8
- inv_dr: float32 [512], replicated, may hold values from 1 to 8
- target: float32 [5, 512], replicated, may hold values from -4 to 4
- cutoff: int32 [32], replicated, may hold values from 2 to 32, as said below
Outputs:
- section_state: float32 [5, 256, 256, 512], P(None, 'gx', 'az')
Inputs may be any that keep to these rules, and one draw needn't show every extreme that they name: `cutoff`: every value from 2 to 32 may occur; both ends occur on some cycle. `state`: density lies between 0.7 and 1.3 and pressure is positive.
All inputs are finite; a program needn't handle non-finite values.
Results may differ from a plain program's by a relative error of at most 0.0003.
Values sent between devices are 32-bit elements; how exact they have to be, the bound alone decides.
No kernel may reach another device: no remote copies, remote signals or barrier semaphores. Data moves between devices by JAX's collectives and lax.ppermute only.
A program may use at most 320 MiB of HBM per device.

v0:
```python
import jax
import jax.numpy as jnp
from jax import lax
from jax.sharding import PartitionSpec as P

NT = 256
CYCLE = 32


gas_factor = 0.4
time_step = 0.02
sponge_rate = 4.0


def extended(cells, sides, width, closed):
    for axis, dim in sides:
        count = lax.axis_size(axis)
        ends = count if closed else count - 1
        head = lax.slice_in_dim(cells, 0, width, axis=dim)
        tail = lax.slice_in_dim(cells, cells.shape[dim] - width, cells.shape[dim], axis=dim)
        cells = jnp.concatenate(
            [
                lax.ppermute(tail, axis, [(i, (i + 1) % count) for i in range(ends)]),
                cells,
                lax.ppermute(head, axis, [((i + 1) % count, i) for i in range(ends)]),
            ],
            axis=dim,
        )
    return cells


def cycle_radius(length):
    return 1.0 + 4.0 * jnp.arange(length, dtype=jnp.float32) / length


def flux_parts(fields, radius):
    density = fields[0]
    axial_momentum = fields[1]
    radial_momentum = fields[2]
    swirl_momentum = fields[3]
    energy = fields[4]
    axial_speed = axial_momentum / density
    radial_speed = radial_momentum / density
    swirl_speed = swirl_momentum / density
    pressure = gas_factor * (
        energy
        - 0.5
        * (
            axial_momentum * axial_speed
            + radial_momentum * radial_speed
            + swirl_momentum * swirl_speed
        )
    )
    enthalpy = energy + pressure
    axial_flux = jnp.stack(
        [
            axial_momentum,
            axial_momentum * axial_speed + pressure,
            radial_momentum * axial_speed,
            swirl_momentum * axial_speed,
            enthalpy * axial_speed,
        ]
    )
    radial_flux = radius * jnp.stack(
        [
            radial_momentum,
            axial_momentum * radial_speed,
            radial_momentum * radial_speed + pressure,
            swirl_momentum * radial_speed,
            enthalpy * radial_speed,
        ]
    )
    swirl_flux = jnp.stack(
        [
            swirl_momentum,
            axial_momentum * swirl_speed,
            radial_momentum * swirl_speed,
            swirl_momentum * swirl_speed + pressure,
            enthalpy * swirl_speed,
        ]
    )
    press_source = (pressure + swirl_momentum * swirl_speed) / radius
    turn_source = -(radial_momentum * swirl_speed) / radius
    return (axial_flux, radial_flux, swirl_flux, press_source, turn_source)


def mode_tables(mode_count, length):
    wave_number = (
        jnp.arange(mode_count, dtype=jnp.int32)[:, None]
        * jnp.arange(length, dtype=jnp.int32)[None, :]
    )
    phase_angle = 2.0 * jnp.pi / length * (wave_number % length).astype(jnp.float32)
    return (jnp.cos(phase_angle), jnp.sin(phase_angle))


def mode_weights(mode_count, length, cycle_cut):
    wave_number = jnp.arange(mode_count, dtype=jnp.int32)[:, None]
    mode_scale = jnp.where(wave_number == 0, 1.0, 2.0) / length
    return jnp.where(wave_number <= cycle_cut[None, :], mode_scale, 0.0).astype(jnp.float32)


def forward(values_block, cosine, sine):
    forward_cos = jnp.einsum("itr,kt->ikr", values_block, cosine, precision=lax.Precision.HIGHEST)
    forward_sin = jnp.einsum("itr,kt->ikr", values_block, sine, precision=lax.Precision.HIGHEST)
    return (forward_cos, forward_sin)


def inverse(coef_cos, coef_sin, weights, cosine, sine):
    first_part = jnp.einsum(
        "ikr,kt->itr", coef_cos * weights[None], cosine, precision=lax.Precision.HIGHEST
    )
    second_part = jnp.einsum(
        "ikr,kt->itr", coef_sin * weights[None], sine, precision=lax.Precision.HIGHEST
    )
    return first_part + second_part


def body(state, sponge_level, inv_dx, inv_dr, target, cutoff):
    planes = state.shape[1]
    columns = state.shape[2]
    cycles_all = state.shape[3]
    radius = cycle_radius(cycles_all)
    axial_flux, radial_flux, swirl_flux, press_source, turn_source = flux_parts(state, radius)
    axial_wide = extended(axial_flux, (("gx", 1),), 1, False)
    swirl_wide = extended(swirl_flux, (("az", 2),), 1, True)
    axial_term = (axial_wide[:, 2:] - axial_wide[:, :-2]) * (0.5 * inv_dx)[None, :, None, None]
    radial_pad = jnp.pad(radial_flux, ((0, 0), (0, 0), (0, 0), (1, 1)))
    radial_term = (radial_pad[..., 2:] - radial_pad[..., :-2]) * (0.5 * inv_dr / radius)
    swirl_term = (swirl_wide[:, :, 2:] - swirl_wide[:, :, :-2]) * (NT / (4.0 * jnp.pi) / radius)
    tendency = -(axial_term + radial_term + swirl_term)
    zero_field = jnp.zeros_like(press_source)
    tendency = tendency + jnp.stack([zero_field, zero_field, press_source, turn_source, zero_field])
    tendency = tendency - sponge_rate * sponge_level.astype(jnp.float32)[None] * (
        state - target[:, None, None, :]
    )
    updated = state + time_step * tendency
    inner_block = updated[..., :CYCLE].reshape(5 * planes, columns, CYCLE)
    mode_count = NT // 8 + 1
    cosine, sine = mode_tables(mode_count, NT)
    position = lax.axis_index("az")
    cycle_share = CYCLE // lax.axis_size("az")
    cycle_cut = lax.dynamic_slice_in_dim(cutoff, position * cycle_share, cycle_share, 0)
    weights = mode_weights(mode_count, NT, cycle_cut)
    coef_cos, coef_sin = forward(
        lax.all_to_all(inner_block, "az", split_axis=2, concat_axis=1, tiled=True), cosine, sine
    )
    turned = inverse(coef_cos, coef_sin, weights, cosine, sine)
    filtered = lax.all_to_all(turned, "az", split_axis=1, concat_axis=2, tiled=True)
    filtered = filtered.reshape(5, planes, columns, CYCLE)
    return jnp.concatenate([filtered, updated[..., CYCLE:]], axis=3)


def solution(mesh):
    return jax.shard_map(
        body,
        mesh=mesh,
        in_specs=(P(None, "gx", "az", None), P("gx", "az", None), P("gx"), P(), P(), P()),
        out_specs=P(None, "gx", "az", None),
        check_vma=False,
    )
```

profile of v0, /device:TPU:1, one launch (start us, length us, event | category | flops | bytes accessed | tf_op | source)
XLA Modules:
  0.0 385.1 jit_solution(15511459593013660546)
XLA Ops:
  0.0 20.6 %copy.38 = f32[5,16,128,512]{2,3,1,0:T(8,128)} copy(f32[5,16,128,512]{3,2,1,0:T(8,128)} %param.6) | data formatting | bytes 41943040 | tf_op args[0]
  20.6 4.6 %slice_dynamic-update-slice_fusion.1 = f32[5,16,128,512]{2,3,1,0:T(8,128)} fusion(f32[5,16,128,512]{2,3,1,0:T(8,128)} %copy.38), kind=kLoop, calls=%fused_computation.37 | loop fusion | bytes 8388608
  25.2 7.7 %multiply_dynamic-update-slice_fusion.4 = (f32[5,16,128,512]{2,3,1,0:T(8,128)}, f32[1,16,128,512]{2,3,1,0:T(8,128)S(1)}) fusion(f32[5,16,128,512]{2,3,1,0:T(8,128)} %slice_dynamic-update-slice_fusion.1, f32[5,16,128,512]{2,3,1,0:T(8,128)} %copy.38), kind=kLoop, calls=%fused_computation.24 | loop fusion | flops 2097152 | bytes 20971520
  32.8 16.2 %add_dynamic-update-slice_fusion = (f32[5,16,128,512]{2,3,1,0:T(8,128)}, f32[1,16,128,512]{2,3,1,0:T(8,128)}, f32[1,16,128,512]{2,3,1,0:T(8,128)}, f32[1,16,128,512]{2,3,1,0:T(8,128)}, f32[5,16,128,512]{2,3,1,0:T(8,128)}) fusion(f32[5,16,128,512]{2,3,1,0:T(8,128)} %get-tuple-element.9, f32[1,16,128,512]{2,3,1,0:T(8,128)S(1)} %get-tuple-element.10, ...), kind=kLoop, calls=%fused_computation.23 | loop fusion | flops 11534335 | bytes 46137344
  49.0 11.1 %multiply_dynamic-update-slice_fusion.3 = (f32[5,16,128,512]{2,3,1,0:T(8,128)}, f32[5,16,128,512]{2,3,1,0:T(8,128)}, f32[5,16,128,512]{2,3,1,0:T(8,128)}) fusion(f32[5,16,128,512]{2,3,1,0:T(8,128)} %get-tuple-element.5, f32[1,16,128,512]{2,3,1,0:T(8,128)} %copy-done.1, f32[5,16,128,512]{2,3,1,0:T(8,128)} %copy.38, f32[5,16,128,512]{2,3,1,0:T(8,128)} %get-tuple-element.25, ...), kind=kLoop, calls=%fused_computation.22 | loop fusion | flops 2097151 | bytes 29360128
  60.1 5.9 %fusion.11 = f32[5,16,128,512]{2,3,1,0:T(8,128)} fusion(f32[5,16,128,512]{2,3,1,0:T(8,128)} %get-tuple-element.20, f32[1,16,128,512]{2,3,1,0:T(8,128)} %get-tuple-element.8, f32[5,16,128,512]{2,3,1,0:T(8,128)} %copy.38), kind=kLoop, calls=%fused_computation.43 | loop fusion | flops 1048576 | bytes 12582912
  66.1 12.3 %add_dynamic-update-slice_fusion.1 = (f32[5,16,128,512]{2,3,1,0:T(8,128)}, f32[5,16,128,512]{2,3,1,0:T(8,128)}) fusion(f32[5,16,128,512]{2,3,1,0:T(8,128)} %get-tuple-element.19, f32[1,16,128,512]{2,3,1,0:T(8,128)} %get-tuple-element.6, f32[1,16,128,512]{2,3,1,0:T(8,128)} %get-tuple-element.7, f32[5,16,128,512]{2,3,1,0:T(8,128)} %copy.38, ...), kind=kLoop, calls=%fused_computation.28 | loop fusion | flops 4194304 | bytes 29360128
  78.4 6.1 %multiply_dynamic-update-slice_fusion.7 = f32[5,16,128,512]{2,3,1,0:T(8,128)} fusion(f32[5,16,128,512]{2,3,1,0:T(8,128)} %get-tuple-element.16, f32[1,16,128,512]{2,3,1,0:T(8,128)} %get-tuple-element.7, f32[5,16,128,512]{2,3,1,0:T(8,128)} %copy.38), kind=kLoop, calls=%fused_computation.27 | loop fusion | flops 1048576 | bytes 12582912
  84.5 6.0 %multiply_dynamic-update-slice_fusion.6 = f32[5,16,128,512]{2,3,1,0:T(8,128)} fusion(f32[5,16,128,512]{2,3,1,0:T(8,128)} %multiply_dynamic-update-slice_fusion.7, f32[1,16,128,512]{2,3,1,0:T(8,128)} %get-tuple-element.7, f32[5,16,128,512]{2,3,1,0:T(8,128)} %copy.38), kind=kLoop, calls=%fused_computation.26 | loop fusion | flops 1048576 | bytes 12582912
  90.5 15.0 %broadcast_divide_fusion = (f32[1,16,128,512]{2,3,1,0:T(8,128)}, f32[5,16,128,512]{2,3,1,0:T(8,128)}, f32[1,16,128,512]{2,3,1,0:T(8,128)}, f32[5,16,128,512]{2,3,1,0:T(8,128)}, f32[5,16,128,512]{2,3,1,0:T(8,128)}) fusion(f32[512]{0:T(512)S(1)} %multiply_add_fusion, f32[1,16,128,512]{2,3,1,0:T(8,128)} %get-tuple-element.6, ...), kind=kLoop, calls=%fused_computation.41 | loop fusion | flops 10485760 | bytes 50333696 | tf_op jit(solution)/shard_map/div | solution.py:82
  105.5 31.8 %fusion.68 = (f32[5,16,1,512]{2,3,1,0:T(8,128)}, f32[5,16,1,512]{2,3,1,0:T(8,128)}) fusion(f32[5,16,128,512]{2,3,1,0:T(8,128)} %get-tuple-element.12), kind=kLoop, calls=%fused_computation.97 | loop fusion | bytes 655360 | tf_op jit(solution)/shard_map/slice | solution.py:19
  137.2 11.4 %copy.32 = f32[5,16,1,512]{3,1,2,0:T(8,128)S(1)} copy(f32[5,16,1,512]{2,3,1,0:T(8,128)} %get-tuple-element.23) | data formatting | bytes 327680 | tf_op jit(solution)/shard_map/slice | solution.py:19
  150.8 11.6 %copy.34 = f32[5,16,1,512]{3,1,2,0:T(8,128)S(1)} copy(f32[5,16,1,512]{2,3,1,0:T(8,128)} %get-tuple-element.24) | data formatting | bytes 327680 | tf_op jit(solution)/shard_map/slice | solution.py:20
  172.3 4.7 %convert_multiply_fusion = f32[16,128,512]{2,1,0:T(8,128)} fusion(s32[16,128,512]{2,1,0:T(8,128)} %param.7), kind=kLoop, calls=%fused_computation.17 | loop fusion | flops 2097152 | bytes 8388608 | tf_op jit(solution)/shard_map/mul | solution.py:133
  177.0 5.3 %copy.36 = f32[16,128,512]{1,2,0:T(8,128)} copy(f32[16,128,512]{2,1,0:T(8,128)} %convert_multiply_fusion) | data formatting | bytes 8388608 | tf_op jit(solution)/shard_map/mul | solution.py:133
  182.4 16.0 %broadcast_multiply_fusion = f32[5,16,128,512]{2,3,1,0:T(8,128)} fusion(f32[5,16,128,512]{2,3,1,0:T(8,128)} %get-tuple-element.14, f32[512]{0:T(512)S(1)} %multiply_add_fusion), kind=kLoop, calls=%fused_computation.16 | loop fusion | flops 5242880 | bytes 41945088 | tf_op jit(solution)/shard_map/mul | solution.py:64
  198.4 9.8 %copy.33 = f32[5,16,1,512]{2,3,1,0:T(8,128)} copy(f32[5,16,1,512]{3,1,2,0:T(8,128)S(1)} %collective-permute-done.2) | data formatting | bytes 327680 | tf_op jit(solution)/shard_map/ppermute | solution.py:25
  208.2 9.7 %copy.35 = f32[5,16,1,512]{2,3,1,0:T(8,128)} copy(f32[5,16,1,512]{3,1,2,0:T(8,128)S(1)} %collective-permute-done.3) | data formatting | bytes 327680 | tf_op jit(solution)/shard_map/ppermute | solution.py:23
  217.9 69.9 %fusion.7 = f32[5,16,128,512]{2,3,1,0:T(8,128)} fusion(f32[5,16,128,512]{2,3,1,0:T(8,128)} %copy.38, f32[5,16,128,512]{2,3,1,0:T(8,128)} %get-tuple-element.12, f32[5,16,1,512]{2,3,1,0:T(8,128)} %copy.35, f32[5,16,1,512]{2,3,1,0:T(8,128)} %copy.33, f32[5,16,128,512]{2,3,1,0:T(8,128)} %get-tuple-element.15, f32[5,1,128,512]{2,3,1,0:T(8,128)S(1)} %collective-permute-done.1, ...), kind=kLoop, calls=%fused_computation.8 | loop fusion | flops 115343360 | bytes 120404072 | tf_op jit(solution)/shard_map/add | solution.py:136
  295.1 15.9 %all-to-all-done = f32[80,128,32]{1,0,2:T(8,128)S(1)} async-done(((f32[80,128,32]{1,0,2:T(8,128)}), f32[80,128,32]{1,0,2:T(8,128)S(1)}, u32[]{:S(2)}, u32[]{:S(2)}) %all-to-all-start) | async-done | bytes 1310752 | tf_op jit(solution)/shard_map/all_to_all | solution.py:145
  323.0 15.1 %slice.82 = f32[5,16,128,480]{2,3,1,0:T(8,128)} slice(f32[5,16,128,512]{2,3,1,0:T(8,128)} %fusion.7), slice={[0:5], [0:16], [0:128], [32:512]} | slice | bytes 39321600 | tf_op jit(solution)/shard_map/slice | solution.py:150
  338.1 9.5 %all-to-all-done.1 = f32[80,256,16]{0,2,1:T(8,128)S(1)} async-done(((f32[80,256,16]{0,2,1:T(8,128)}), f32[80,256,16]{0,2,1:T(8,128)S(1)}, u32[]{:S(2)}, u32[]{:S(2)}) %all-to-all-start.1) | async-done | bytes 1310752 | tf_op jit(solution)/shard_map/all_to_all | solution.py:148
  349.2 15.2 %pad_maximum_fusion.4 = f32[5,16,128,512]{2,3,1,0:T(8,128)} fusion(f32[5,16,128,480]{2,3,1,0:T(8,128)} %slice.82, f32[5,16,128,32]{2,3,1,0:T(8,128)S(1)} %bitcast.43), kind=kLoop, calls=%fused_computation.15 | loop fusion | flops 5242880 | bytes 41943040 | tf_op jit(solution)/shard_map/concatenate | solution.py:150
  364.4 20.7 %copy.47 = f32[5,16,128,512]{3,2,1,0:T(8,128)} copy(f32[5,16,128,512]{2,3,1,0:T(8,128)} %pad_maximum_fusion.4) | data formatting | bytes 41943040 | tf_op jit(solution)/shard_map/concatenate | solution.py:150
  (41 shorter events, 33.1 us)
Async XLA Ops:
  32.8 16.2 %copy-start.1 = (f32[1,16,128,512]{2,3,1,0:T(8,128)}, f32[1,16,128,512]{2,3,1,0:T(8,128)S(1)}, u32[]{:S(2)}) copy-start(f32[1,16,128,512]{2,3,1,0:T(8,128)S(1)} %get-tuple-element.10) | copy-start | bytes 12582916
  78.4 12.0 %copy-start = (f32[1,16,128,512]{2,3,1,0:T(8,128)S(1)}, f32[1,16,128,512]{2,3,1,0:T(8,128)}, u32[]{:S(2)}) copy-start(f32[1,16,128,512]{2,3,1,0:T(8,128)} %get-tuple-element.7) | copy-start | bytes 12582916
  137.2 35.0 %copy-start.3 = (f32[512]{0:T(512)S(1)}, f32[512]{0:T(512)}, u32[]{:S(2)}) copy-start(f32[512]{0:T(512)} %param.9) | copy-start | bytes 6148
  148.7 49.7 %collective-permute-start.2 = (f32[5,16,1,512]{3,1,2,0:T(8,128)S(1)}, f32[5,16,1,512]{3,1,2,0:T(8,128)S(1)}, u32[]{:S(2)}, u32[]{:S(2)}) collective-permute-start(f32[5,16,1,512]{3,1,2,0:T(8,128)S(1)} %copy.32), channel_id=1, source_target_pairs={{1,0},{0,1},{3,2},{2,3},{5,4},{4,5},{7,6},{6,7},{9,8},{8,9},{11,10... | collective-permute-start | bytes 491528 | tf_op jit(solution)/shard_map/ppermute | solution.py:25
  162.4 45.8 %collective-permute-start.3 = (f32[5,16,1,512]{3,1,2,0:T(8,128)S(1)}, f32[5,16,1,512]{3,1,2,0:T(8,128)S(1)}, u32[]{:S(2)}, u32[]{:S(2)}) collective-permute-start(f32[5,16,1,512]{3,1,2,0:T(8,128)S(1)} %copy.34), channel_id=1, source_target_pairs={{0,1},{1,0},{2,3},{3,2},{4,5},{5,4},{6,7},{7,6},{8,9},{9,8},{10,11... | collective-permute-start | bytes 491528 | tf_op jit(solution)/shard_map/ppermute | solution.py:23
  165.9 52.0 %collective-permute-start = (f32[5,1,128,512]{2,3,1,0:T(8,128)}, f32[5,1,128,512]{2,3,1,0:T(8,128)S(1)}, u32[]{:S(2)}, u32[]{:S(2)}) collective-permute-start(f32[5,1,128,512]{2,3,1,0:T(8,128)} %get-tuple-element.21), channel_id=1, source_target_pairs={{2,0},{4,2},{6,4},{8,6},{10,8},{12,10},{14,12},{16,14},{18,16},{20... | collective-permute-start | bytes 3932168 | tf_op jit(solution)/shard_map/ppermute | solution.py:25
  168.7 49.2 %collective-permute-start.1 = (f32[5,1,128,512]{2,3,1,0:T(8,128)}, f32[5,1,128,512]{2,3,1,0:T(8,128)S(1)}, u32[]{:S(2)}, u32[]{:S(2)}) collective-permute-start(f32[5,1,128,512]{2,3,1,0:T(8,128)} %get-tuple-element.22), channel_id=1, source_target_pairs={{0,2},{2,4},{4,6},{6,8},{8,10},{10,12},{12,14},{14,16},{16,18},{18... | collective-permute-start | bytes 3932168 | tf_op jit(solution)/shard_map/ppermute | solution.py:23
  182.4 16.0 %copy-start.4 = (f32[16]{0:T(128)S(1)}, f32[16]{0:T(128)}, u32[]{:S(2)}) copy-start(f32[16]{0:T(128)} %param.8) | copy-start | bytes 196
  198.4 19.5 %copy-start.2 = (f32[5,512]{1,0:T(8,128)S(1)}, f32[5,512]{1,0:T(8,128)}, u32[]{:S(2)}) copy-start(f32[5,512]{1,0:T(8,128)} %param.10) | copy-start | bytes 30724
  217.9 77.0 %copy-start.5 = (s32[32]{0:T(128)S(1)}, s32[32]{0:T(128)}, u32[]{:S(2)}) copy-start(s32[32]{0:T(128)} %param.11) | copy-start | bytes 388
  291.0 19.9 %all-to-all-start = ((f32[80,128,32]{1,0,2:T(8,128)}), f32[80,128,32]{1,0,2:T(8,128)S(1)}, u32[]{:S(2)}, u32[]{:S(2)}) async-start(f32[80,128,32]{1,0,2:T(8,128)} %copy.39), calls=%async_computation | async-start | bytes 2621440 | tf_op jit(solution)/shard_map/all_to_all | solution.py:145
  319.2 28.3 %all-to-all-start.1 = ((f32[80,256,16]{0,2,1:T(8,128)}), f32[80,256,16]{0,2,1:T(8,128)S(1)}, u32[]{:S(2)}, u32[]{:S(2)}) async-start(f32[80,256,16]{0,2,1:T(8,128)} %copy.44), calls=%async_computation.1 | async-start | bytes 4194304 | tf_op jit(solution)/shard_map/all_to_all | solution.py:148
where the time goes:
time: 388 us; the launch traced here: 385 us
  other arithmetic  186 us (48%)
  local copies, waits for them, and re-layouts  151 us (39%)
  waiting for transfers between devices  25.3 us (7%)
  starting transfers between devices  16.2 us (4%)
  matrix products  6.34 us (2%)
    add x1, other arithmetic, body(): updated = state + time_step * tendency  69.9 us
    unnamed x7, other arithmetic  65.3 us
    slice x3, local copies, waits for them, and re-layouts, extended(): head = lax.slice_in_dim(cells, 0, width, axis=dim)  46.6 us
    unnamed x14, local copies, waits for them, and re-layouts  25.2 us
    concatenate x1, local copies, waits for them, and re-layouts, body(): return jnp.concatenate([filtered, updated[..., CYCLE:]], axis=3)  20.7 us
    mul x1, other arithmetic, flux_parts(): radius * jnp.stack([radial_momentum, axial_momentum * radial_speed, radia...  16 us
    all_to_all x1, waiting for transfers between devices, body(): lax.all_to_all(inner_block, 'az', split_axis=2, concat_axis=1, tiled=True)  15.9 us
    concatenate x1, other arithmetic, body(): return jnp.concatenate([filtered, updated[..., CYCLE:]], axis=3)  15.2 us
  transfers between devices with their start and end apart: 6, of which 2 were waited for; matrix products, arithmetic and copies ran while one was open for 20% of the time, Pallas kernels for 0%

commit v1 on v0

v1 whole, which is shorter than its diff:
```python
import functools
import math

import jax
import jax.numpy as jnp
import ml_dtypes
import numpy as np
from jax import lax
from jax.experimental import pallas as pl
from jax.experimental.pallas import tpu as pltpu
from jax.sharding import PartitionSpec as P

CYCLE = 32
LANES = 128
PACK = LANES // CYCLE

gas_factor = 0.4
time_step = 0.02
sponge_rate = 4.0

VMEM_LIMIT = 56 * 1024 * 1024


def params(steps=1):
    return pltpu.CompilerParams(
        dimension_semantics=("arbitrary",) * steps, vmem_limit_bytes=VMEM_LIMIT
    )


def reciprocal(x):
    guess = pl.reciprocal(x, approx=True)
    return guess * (2.0 - x * guess)


def products(q):
    density, m, n, s, energy = q
    inverse = reciprocal(density)
    u, v, w = m * inverse, n * inverse, s * inverse
    mu, nv, sw = m * u, n * v, s * w
    pressure = gas_factor * energy - (0.5 * gas_factor) * (mu + nv + sw)
    return u, v, w, mu, nv, sw, pressure, energy + pressure


def axial_flux(q):
    u, _, _, mu, _, _, pressure, enthalpy = products(q)
    return (q[1], mu + pressure, q[2] * u, q[3] * u, enthalpy * u)


def swirl_flux(q):
    _, _, w, _, _, sw, pressure, enthalpy = products(q)
    return (q[3], q[1] * w, q[2] * w, sw + pressure, enthalpy * w)


def all_fluxes(q):
    u, v, w, mu, nv, sw, pressure, enthalpy = products(q)
    mv, mw, nw = q[1] * v, q[1] * w, q[2] * w
    axial = (q[1], mu + pressure, mv, mw, enthalpy * u)
    radial = (q[2], mv, nv + pressure, nw, enthalpy * v)
    swirl = (q[3], mw, nw, sw + pressure, enthalpy * w)
    return axial, radial, swirl


def fill_rows(rows_ref, inv_dr, cycles, columns):
    width = rows_ref.shape[-1]
    cycle = lax.broadcasted_iota(jnp.int32, (8, width), 1)
    spacing = 4.0 / cycles
    radius = 1.0 + spacing * cycle.astype(jnp.float32)
    inverse = 1.0 / radius
    half = (0.5 * time_step) * jnp.broadcast_to(inv_dr, (8, width)) * inverse
    rows_ref[0] = jnp.where(cycle == cycles - 1, 0.0, half * (radius + spacing))
    rows_ref[1] = jnp.where(cycle == 0, 0.0, half * (radius - spacing))
    rows_ref[2] = (time_step * columns / (4.0 * math.pi)) * inverse


def base_update(q, level, target, factors, radial, swirl, columns):
    up, down, around = factors
    width = q[0].shape[-1]
    sponge = level.astype(jnp.float32) * (time_step * sponge_rate)
    scaled = [around * flux for flux in swirl]
    source = 4.0 * math.pi / columns
    result = []
    for f in range(5):
        ahead = pltpu.roll(radial[f], width - 1, 1)
        behind = pltpu.roll(radial[f], 1, 1)
        value = q[f] - sponge * (q[f] - target[f]) - (up * ahead - down * behind)
        if f == 2:
            value = value + source * scaled[3]
        if f == 3:
            value = value - source * scaled[2]
        result.append(value)
    return result, scaled


def outer_kernel(odd_ref, state_ref, flux_ref, packed_ref):
    block = pl.program_id(0)
    flux = axial_flux([state_ref[f, 0] for f in range(5)])
    lane = lax.broadcasted_iota(jnp.int32, packed_ref.shape[1:], 1)
    for f in range(5):
        flux_ref[f] = flux[f]
        turned = pltpu.roll(flux[f][:, :LANES], block * CYCLE, 1)
        packed_ref[f] = jnp.where(lane // CYCLE == block, turned, packed_ref[f])


def outer_plane(odd, state):
    _, planes, columns, cycles = state.shape
    rows = columns // PACK
    return pl.pallas_call(
        outer_kernel,
        grid_spec=pltpu.PrefetchScalarGridSpec(
            num_scalar_prefetch=1,
            grid=(PACK,),
            in_specs=[pl.BlockSpec((5, 1, rows, cycles), lambda b, odd: (0, odd[0] * (planes - 1), b, 0))],
            out_specs=[
                pl.BlockSpec((5, rows, cycles), lambda b, odd: (0, b, 0)),
                pl.BlockSpec((5, rows, LANES), lambda b, odd: (0, 0, 0)),
            ],
        ),
        out_shape=[
            jax.ShapeDtypeStruct((5, columns, cycles), jnp.float32),
            jax.ShapeDtypeStruct((5, rows, LANES), jnp.float32),
        ],
        compiler_params=params(),
        name="outer_plane",
    )(odd, state)


def inner_kernel(odd_ref, state_ref, first_ref, last_ref, flux_ref, edge_ref):
    flux = axial_flux([state_ref[f, 0] for f in range(5)])
    for f in range(5):
        flux_ref[f] = flux[f]
    low = swirl_flux([last_ref[f, :, 7, :] for f in range(5)])
    high = swirl_flux([first_ref[f, :, 0, :] for f in range(5)])
    for f in range(5):
        edge_ref[0, f] = low[f]
        edge_ref[1, f] = high[f]


def inner_plane(odd, state):
    _, planes, columns, cycles = state.shape
    steps = planes // 8
    rows = columns // steps
    return pl.pallas_call(
        inner_kernel,
        grid_spec=pltpu.PrefetchScalarGridSpec(
            num_scalar_prefetch=1,
            grid=(steps,),
            in_specs=[
                pl.BlockSpec((5, 1, rows, cycles), lambda b, odd: (0, (1 - odd[0]) * (planes - 1), b, 0)),
                pl.BlockSpec((5, 8, 8, cycles), lambda b, odd: (0, b, 0, 0)),
                pl.BlockSpec((5, 8, 8, cycles), lambda b, odd: (0, b, columns // 8 - 1, 0)),
            ],
            out_specs=[
                pl.BlockSpec((5, rows, cycles), lambda b, odd: (0, b, 0)),
                pl.BlockSpec((2, 5, 8, cycles), lambda b, odd: (0, 0, b, 0)),
            ],
        ),
        out_shape=[
            jax.ShapeDtypeStruct((5, columns, cycles), jnp.float32),
            jax.ShapeDtypeStruct((2, 5, planes, cycles), jnp.float32),
        ],
        compiler_params=params(),
        name="inner_plane",
    )(odd, state, state, state)


def modes_kernel(
    odd_ref, scale_ref, state_ref, before_ref, after_ref, level_ref, inv_dr_ref, target_ref, near_ref, far_ref,
    table_ref, edge_ref, out_ref, rows_ref, axial_ref, swirl_ref, base_ref, split_ref, total_ref,
    *, cycles, cells, chunk,
):
    step = pl.program_id(0)
    steps = pl.num_programs(0)
    columns = state_ref.shape[2]
    odd = odd_ref[0]
    far_rows = far_ref.shape[1]

    @pl.when(step == 0)
    def _():
        fill_rows(rows_ref, inv_dr_ref[...], cycles, cells)
        for f in range(5):
            for i in range(PACK):
                swirl_ref[i, f, 0:8] = jnp.zeros((8, LANES), jnp.float32)
                swirl_ref[i, f, columns + 8 : columns + 16] = jnp.zeros((8, LANES), jnp.float32)

    def load(ref, plane, start):
        return [ref[f, plane, pl.ds(start, chunk), :] for f in range(5)]

    def halo(slot, use_near):
        for f in range(5):
            for b in range(PACK):
                away = far_ref[f]
                away = away if b == 0 else pltpu.roll(away, LANES - b * CYCLE, 1)
                near = near_ref[f, b * far_rows : (b + 1) * far_rows]
                axial_ref[slot, f, b * far_rows : (b + 1) * far_rows] = jnp.where(use_near, near, away)

    def neighbour(slot, ref):
        def one(c, _):
            start = pl.multiple_of(c * chunk, chunk)
            flux = axial_flux(load(ref, 0, start))
            for f in range(5):
                axial_ref[slot, f, pl.ds(start, chunk)] = flux[f]
            return 0

        lax.fori_loop(0, columns // chunk, one, 0)

    pl.when(step == 0)(lambda: halo(0, odd == 1))
    pl.when(step > 0)(lambda: neighbour(0, before_ref))
    pl.when(step == steps - 1)(lambda: halo(PACK + 1, odd == 0))
    pl.when(step < steps - 1)(lambda: neighbour(PACK + 1, after_ref))

    def wide(rows):
        return jnp.broadcast_to(rows[None], (chunk // 8, 8, LANES)).reshape(chunk, LANES)

    def first(c, _):
        start = pl.multiple_of(c * chunk, chunk)
        factors = [wide(rows_ref[k]) for k in range(3)]
        target = [jnp.broadcast_to(target_ref[f : f + 1], (chunk, LANES)) for f in range(5)]
        for i in range(PACK):
            q = load(state_ref, i, start)
            axial, radial, swirl = all_fluxes(q)
            level = level_ref[i, pl.ds(start, chunk), :]
            base, scaled = base_update(q, level, target, factors, radial, swirl, cells)
            for f in range(5):
                axial_ref[i + 1, f, pl.ds(start, chunk)] = axial[f]
                swirl_ref[i, f, pl.ds(start + 8, chunk)] = scaled[f]
                base_ref[i, f, pl.ds(start, chunk)] = base[f]
        return 0

    lax.fori_loop(0, columns // chunk, first, 0)

    lane = lax.broadcasted_iota(jnp.int32, (chunk, LANES), 1)

    def packed(parts, rows):
        result = parts[0]
        for i in range(1, PACK):
            result = jnp.where(lane[:rows] // CYCLE == i, pltpu.roll(parts[i], i * CYCLE, 1), result)
        return result

    factor = [(0.5 * time_step) * scale_ref[step * PACK + i] for i in range(PACK)]
    for f in range(5):
        total = jnp.zeros((8, LANES), jnp.float32)
        for c in range(columns // chunk):
            start = c * chunk
            parts = []
            for i in range(PACK):
                value = base_ref[i, f, start : start + chunk]
                value = value - factor[i] * (
                    axial_ref[i + 2, f, start : start + chunk] - axial_ref[i, f, start : start + chunk]
                )
                value = value + (
                    swirl_ref[i, f, start + 7 : start + 7 + chunk] - swirl_ref[i, f, start + 9 : start + 9 + chunk]
                )
                parts.append(value)
            value = packed(parts, chunk)
            high = value.astype(jnp.bfloat16)
            split_ref[f, start : start + chunk] = high
            split_ref[f, columns + start : columns + start + chunk] = (value - high.astype(jnp.float32)).astype(
                jnp.bfloat16
            )
            total = total + value.reshape(chunk // 8, 8, LANES).sum(axis=0)
        sums = jnp.dot(table_ref[...], split_ref[f], preferred_element_type=jnp.float32)
        half = sums.shape[0] // 2
        start_row = packed([swirl_ref[i, f, 8:16] for i in range(PACK)], 8)[0:1]
        end_row = packed([swirl_ref[i, f, columns : columns + 8] for i in range(PACK)], 8)[7:8]
        group = step * 5 + f
        out_ref[pl.ds(pl.multiple_of(group * half, half), half), :] = (
            sums[:half] + sums[half:] + (edge_ref[1] * end_row - edge_ref[0] * start_row)
        )
        mean = total.sum(axis=0, keepdims=True) + (end_row - start_row)
        out_ref[pl.ds(steps * 5 * half + group, 1), :] = mean


def mode_rows(planes, half):
    groups = 5 * planes // PACK
    return groups * half + -(-groups // 8) * 8


def inner_modes(odd, scale, state, sponge, inv_dr, target, near, far, table, edge, cells):
    _, planes, columns, cycles = state.shape
    half = table.shape[0] // 2
    chunk = min(32, columns)
    rows = mode_rows(planes, half)
    whole = lambda *shape: pl.BlockSpec(shape, lambda g, odd: (0,) * len(shape))
    return pl.pallas_call(
        functools.partial(modes_kernel, cycles=cycles, cells=cells, chunk=chunk),
        grid_spec=pltpu.PrefetchScalarGridSpec(
            num_scalar_prefetch=1,
            grid=(planes // PACK,),
            in_specs=[
                pl.BlockSpec(memory_space=pltpu.SMEM),
                pl.BlockSpec((5, PACK, columns, LANES), lambda g, odd: (0, g, 0, 0)),
                pl.BlockSpec((5, 1, columns, LANES), lambda g, odd: (0, jnp.maximum(g * PACK - 1, 0), 0, 0)),
                pl.BlockSpec(
                    (5, 1, columns, LANES), lambda g, odd: (0, jnp.minimum(g * PACK + PACK, planes - 1), 0, 0)
                ),
                pl.BlockSpec((PACK, columns, LANES), lambda g, odd: (g, 0, 0)),
                whole(1, LANES),
                whole(5, LANES),
                whole(5, columns, LANES),
                whole(5, columns // PACK, LANES),
                whole(*table.shape),
                whole(*edge.shape),
            ],
            out_specs=whole(rows, LANES),
            scratch_shapes=[
                pltpu.VMEM((3, 8, LANES), jnp.float32),
                pltpu.VMEM((PACK + 2, 5, columns, LANES), jnp.float32),
                pltpu.VMEM((PACK, 5, columns + 16, LANES), jnp.float32),
                pltpu.VMEM((PACK, 5, columns, LANES), jnp.float32),
                pltpu.VMEM((5, 2 * columns, LANES), jnp.bfloat16),
                pltpu.VMEM((8, LANES), jnp.float32),
            ],
        ),
        out_shape=jax.ShapeDtypeStruct((rows, LANES), jnp.float32),
        compiler_params=params(),
        name="inner_modes",
    )(odd, scale, state, state, state, sponge, inv_dr, target, near, far, table, edge)


def update_kernel(
    odd_ref, scale_ref, state_ref, level_ref, inv_dr_ref, target_ref, near_ref, halo_ref, out_ref,
    rows_ref, axial_ref, swirl_ref, base_ref, *, cells, chunk,
):
    step = pl.program_id(0)
    planes = pl.num_programs(0) - 1
    columns, cycles = state_ref.shape[2:]
    tiles = cycles // LANES
    odd = odd_ref[0]

    @pl.when(step == 0)
    def _():
        fill_rows(rows_ref, inv_dr_ref[...], cycles, cells)

    def lanes(value, tile):
        return value[:, tile * LANES : (tile + 1) * LANES]

    def finish(c, axial_of):
        start = pl.multiple_of(c * chunk, chunk)
        factor = (0.5 * time_step) * scale_ref[step - 1]
        parity = lax.rem(step + 1, 2)
        for f in range(5):
            ahead = factor * axial_of(f)
            for tile in range(tiles):
                value = lanes(base_ref[f, pl.ds(start, chunk), :], tile) - lanes(ahead, tile)
                value = value + (
                    swirl_ref[parity, f, tile, pl.ds(start + 7, chunk)]
                    - swirl_ref[parity, f, tile, pl.ds(start + 9, chunk)]
                )
                out_ref[f, 0, pl.ds(start, chunk), tile * LANES : (tile + 1) * LANES] = value

    def compute(c, beginning):
        start = pl.multiple_of(c * chunk, chunk)
        q = [state_ref[f, 0, pl.ds(start, chunk), :] for f in range(5)]
        axial, radial, swirl = all_fluxes(q)
        if not beginning:
            finish(c, lambda f: axial[f])
        factor = (0.5 * time_step) * scale_ref[step]
        target = [jnp.broadcast_to(target_ref[f : f + 1], (chunk, cycles)) for f in range(5)]
        base, scaled = base_update(
            q, level_ref[0, pl.ds(start, chunk), :], target, [rows_ref[k] for k in range(3)], radial, swirl, cells
        )
        parity = lax.rem(step, 2)
        for f in range(5):
            if beginning:
                behind = jnp.where(odd == 1, near_ref[f, pl.ds(start, chunk), :], 0.0)
            else:
                behind = axial_ref[f, pl.ds(start, chunk), :]
            base_ref[f, pl.ds(start, chunk), :] = base[f] + factor * behind
            axial_ref[f, pl.ds(start, chunk), :] = axial[f]
            for tile in range(tiles):
                swirl_ref[parity, f, tile, pl.ds(start + 8, chunk)] = lanes(scaled[f], tile)
        return 0

    @pl.when(step < planes)
    def _():
        parity = lax.rem(step, 2)
        around = rows_ref[2][0:1]
        for f in range(5):
            low = around * halo_ref[0, f, pl.ds(step, 1), :]
            high = around * halo_ref[1, f, pl.ds(step, 1), :]
            for tile in range(tiles):
                swirl_ref[parity, f, tile, 7:8] = lanes(low, tile)
                swirl_ref[parity, f, tile, columns + 8 : columns + 9] = lanes(high, tile)

    count = columns // chunk

    def loop(body):
        lax.fori_loop(0, count, body, 0)

    pl.when(step == 0)(lambda: loop(lambda c, _: compute(c, True)))
    pl.when(jnp.logical_and(step > 0, step < planes))(lambda: loop(lambda c, _: compute(c, False)))

    def last(c, _):
        start = pl.multiple_of(c * chunk, chunk)
        finish(c, lambda f: jnp.where(odd == 0, near_ref[f, pl.ds(start, chunk), :], 0.0))
        return 0

    pl.when(step == planes)(lambda: loop(last))


def bulk_update(odd, scale, state, sponge, inv_dr, target, near, halo, cells):
    _, planes, columns, cycles = state.shape
    whole = lambda *shape: pl.BlockSpec(shape, lambda g, odd: (0,) * len(shape))
    return pl.pallas_call(
        functools.partial(update_kernel, cells=cells, chunk=8),
        grid_spec=pltpu.PrefetchScalarGridSpec(
            num_scalar_prefetch=1,
            grid=(planes + 1,),
            in_specs=[
                pl.BlockSpec(memory_space=pltpu.SMEM),
                pl.BlockSpec((5, 1, columns, cycles), lambda g, odd: (0, jnp.minimum(g, planes - 1), 0, 0)),
                pl.BlockSpec((1, columns, cycles), lambda g, odd: (jnp.minimum(g, planes - 1), 0, 0)),
                whole(1, cycles),
                whole(5, cycles),
                whole(5, columns, cycles),
                whole(2, 5, planes, cycles),
            ],
            out_specs=pl.BlockSpec((5, 1, columns, cycles), lambda g, odd: (0, jnp.maximum(g - 1, 0), 0, 0)),
            scratch_shapes=[
                pltpu.VMEM((3, 8, cycles), jnp.float32),
                pltpu.VMEM((5, columns, cycles), jnp.float32),
                pltpu.VMEM((2, 5, cycles // LANES, columns + 16, LANES), jnp.float32),
                pltpu.VMEM((5, columns, cycles), jnp.float32),
            ],
        ),
        out_shape=jax.ShapeDtypeStruct(state.shape, jnp.float32),
        compiler_params=params(),
        name="bulk_update",
    )(odd, scale, state, sponge, inv_dr, target, near, halo)


def filter_kernel(cutoff_ref, table_ref, *refs, cells):
    *sums, state_ref, out_ref, split_ref = refs
    step = pl.program_id(0)
    steps = pl.num_programs(0)
    half = table_ref.shape[1] // 4
    count = half // 2
    columns = out_ref.shape[2]
    mode = lax.broadcasted_iota(jnp.int32, (half, LANES), 0)
    mode = jnp.where(mode >= count, mode - count, mode) + 1
    weight = jnp.where(mode <= cutoff_ref[...], 2.0 / cells, 0.0)
    lane = lax.broadcasted_iota(jnp.int32, (columns, LANES), 1)
    for f in range(5):
        group = step * 5 + f
        rows = pl.ds(pl.multiple_of(group * half, half), half)
        coefficient = sums[0][rows, :]
        mean = sums[0][pl.ds(steps * 5 * half + group, 1), :]
        for other in sums[1:]:
            coefficient = coefficient + other[rows, :]
            mean = mean + other[pl.ds(steps * 5 * half + group, 1), :]
        coefficient = coefficient * weight
        high = coefficient.astype(jnp.bfloat16)
        low = (coefficient - high.astype(jnp.float32)).astype(jnp.bfloat16)
        for k in range(2):
            split_ref[f, 2 * k * half : (2 * k + 1) * half] = high
            split_ref[f, (2 * k + 1) * half : (2 * k + 2) * half] = low
        values = jnp.dot(table_ref[...], split_ref[f], preferred_element_type=jnp.float32) + mean * (1.0 / cells)
        for i in range(PACK):
            turned = values if i == 0 else pltpu.roll(values, LANES - i * CYCLE, 1)
            out_ref[f, i] = jnp.where(lane < CYCLE, turned, state_ref[f, i])


def put_filtered(cutoff, table, sums, updated, cells):
    _, planes, columns, cycles = updated.shape
    whole = lambda *shape: pl.BlockSpec(shape, lambda g: (0,) * len(shape))
    block = pl.BlockSpec((5, PACK, columns, LANES), lambda g: (0, g, 0, 0))
    return pl.pallas_call(
        functools.partial(filter_kernel, cells=cells),
        grid=(planes // PACK,),
        in_specs=[whole(1, LANES), whole(*table.shape)] + [whole(*part.shape) for part in sums] + [block],
        out_specs=block,
        scratch_shapes=[pltpu.VMEM((5, table.shape[1], LANES), jnp.bfloat16)],
        out_shape=jax.ShapeDtypeStruct(updated.shape, jnp.float32),
        input_output_aliases={2 + len(sums): 0},
        compiler_params=params(),
        name="put_filtered",
    )(cutoff, table, *sums, updated)


def finish_kernel(odd_ref, scale_ref, flux_ref, state_ref, out_ref):
    odd = odd_ref[0]
    planes = scale_ref.shape[0]
    factor = (0.5 * time_step) * scale_ref[odd * (planes - 1)]
    factor = jnp.where(odd == 1, -factor, factor)
    lane = lax.broadcasted_iota(jnp.int32, out_ref.shape[2:], 1)
    for f in range(5):
        out_ref[f, 0] = state_ref[f, 0] + jnp.where(lane < CYCLE, 0.0, factor * flux_ref[f])


def finish_plane(odd, scale, flux, updated):
    _, planes, columns, cycles = updated.shape
    rows = columns // 4
    block = pl.BlockSpec((5, 1, rows, cycles), lambda b, odd: (0, odd[0] * (planes - 1), b, 0))
    return pl.pallas_call(
        finish_kernel,
        grid_spec=pltpu.PrefetchScalarGridSpec(
            num_scalar_prefetch=1,
            grid=(4,),
            in_specs=[
                pl.BlockSpec(memory_space=pltpu.SMEM),
                pl.BlockSpec((5, rows, cycles), lambda b, odd: (0, b, 0)),
                block,
            ],
            out_specs=block,
        ),
        out_shape=jax.ShapeDtypeStruct(updated.shape, jnp.float32),
        input_output_aliases={3: 0},
        compiler_params=params(),
        name="finish_plane",
    )(odd, scale, flux, updated)


def mode_tables(cells, sectors):
    columns = cells // sectors
    mode = np.arange(1, cells // 8 + 1)

    def waves(cell):
        angle = 2.0 * np.pi / cells * ((mode[:, None] * cell[None, :]) % cells)
        return np.concatenate([np.cos(angle), np.sin(angle)])

    forward, inverse, edge = [], [], []
    for sector in range(sectors):
        wave = waves(sector * columns + np.arange(columns))
        high = wave.astype(ml_dtypes.bfloat16)
        low = (wave - high.astype(np.float64)).astype(ml_dtypes.bfloat16)
        forward.append(np.block([[high, high], [low, low]]))
        inverse.append(np.concatenate([high.T, high.T, low.T, low.T], axis=1))
        ends = waves(np.array([sector * columns - 1, (sector + 1) * columns]) % cells)
        edge.append(np.broadcast_to(ends.T[:, :, None], (2, ends.shape[0], LANES)))
    return np.stack(forward), np.stack(inverse), np.stack(edge).astype(np.float32)


def body(forward, inverse, edge, cells, state, sponge_level, inv_dx, inv_dr, target, cutoff):
    sectors = lax.axis_size("az")
    rows = lax.axis_size("gx")
    sector = lax.axis_index("az")
    odd = jnp.reshape(lax.rem(lax.axis_index("gx"), 2), (1,)).astype(jnp.int32)
    cycles = state.shape[3]
    inv_dr = inv_dr.reshape(1, cycles)
    cutoff = jnp.tile(cutoff, PACK).reshape(1, LANES)
    pick = lambda table: lax.dynamic_index_in_dim(table, sector, 0, False)

    near_pairs = [(i ^ 1, i) for i in range(rows) if i ^ 1 < rows]
    far_pairs = [(i, i + 1) for i in range(1, rows - 1, 2)] + [(i + 1, i) for i in range(1, rows - 1, 2)]
    shifted = lambda part, by: lax.ppermute(part, "az", [(i, (i + by) % sectors) for i in range(sectors)])

    far_flux, far_packed = outer_plane(odd, state)
    far_packed = lax.ppermute(far_packed, "gx", far_pairs)
    far_flux = lax.ppermute(far_flux, "gx", far_pairs)
    near_flux, edges = inner_plane(odd, state)
    near_flux = lax.ppermute(near_flux, "gx", near_pairs)
    if sectors == 2:
        halo = shifted(edges, 1)
    else:
        halo = jnp.stack([shifted(edges[0], 1), shifted(edges[1], sectors - 1)])
    sums = inner_modes(
        odd, inv_dx, state, sponge_level, inv_dr, target, near_flux, far_packed, pick(forward), pick(edge), cells
    )
    others = [shifted(sums, by) for by in range(1, sectors)]
    updated = bulk_update(odd, inv_dx, state, sponge_level, inv_dr, target, near_flux, halo, cells)
    updated = put_filtered(cutoff, pick(inverse), [sums, *others], updated, cells)
    return finish_plane(odd, inv_dx, far_flux, updated)


def solution(mesh):
    def whole(state, sponge_level, inv_dx, inv_dr, target, cutoff):
        cells = state.shape[2]
        tables = mode_tables(cells, mesh.shape["az"])
        mapped = jax.shard_map(
            functools.partial(body, *(jnp.asarray(table) for table in tables), cells),
            mesh=mesh,
            in_specs=(P(None, "gx", "az", None), P("gx", "az", None), P("gx"), P(), P(), P()),
            out_specs=P(None, "gx", "az", None),
            check_vma=False,
        )
        return mapped(state, sponge_level, inv_dx, inv_dr, target, cutoff)

    return whole
```

time: 388 us -> 119 us (0.31)
  other arithmetic: 186 us -> 0 us
  local copies, waits for them, and re-layouts: 151 us -> 6.27 us
  Pallas kernels: 0 us -> 65.2 us
  waiting for transfers between devices: 25.3 us -> 38 us
  starting transfers between devices: 16.2 us -> 8.01 us
  matrix products: 6.34 us -> 0 us
    slice x6 -> x0, local copies, waits for them, and re-layouts: 74.7 us -> none  [the longest x3 46.6 us: extended(): head = lax.slice_in_dim(cells, 0, width, axis=dim)]
    add x2 -> x0, other arithmetic: 69.9 us -> none  [the longest x1 69.9 us: body(): updated = state + time_step * tendency]
    unnamed x7 -> x0, other arithmetic: 65.3 us -> none
    pallas_call x0 -> x6, Pallas kernels: none -> 65.2 us  [the longest x1 37.6 us: bulk_update(): pl.pallas_call(functools.partial(update_kernel, cells=cells, chunk=8), gr...]
    ppermute x4 -> x5, waiting for transfers between devices: 0.01 us -> 38 us  [the longest x1 27.4 us: body(): far_packed = lax.ppermute(far_packed, 'gx', far_pairs)]
    all_to_all x2 -> x0, waiting for transfers between devices: 25.3 us -> none  [the longest x1 15.9 us: body(): lax.all_to_all(inner_block, 'az', split_axis=2, concat_axis=1, tiled=True)]
    unnamed x14 -> x20, local copies, waits for them, and re-layouts: 25.2 us -> 3.75 us
    concatenate x1 -> x0, local copies, waits for them, and re-layouts: 20.7 us -> none  [body(): return jnp.concatenate([filtered, updated[..., CYCLE:]], axis=3)]
  transfers between devices with their start and end apart: 6 -> 5, of which waited for: 2 -> 2; matrix products, arithmetic and copies ran while one was open for 20% -> 2% of each run, Pallas kernels for 0% -> 50%
where the time goes in v1:
time: 119 us; the launch traced here: 118 us
  Pallas kernels  65.2 us (55%)
  waiting for transfers between devices  38 us (32%)
  starting transfers between devices  8.01 us (7%)
  local copies, waits for them, and re-layouts  6.27 us (5%)
    pallas_call x1, Pallas kernels, bulk_update(): pl.pallas_call(functools.partial(update_kernel, cells=cells, chunk=8), gr...  37.6 us
    ppermute x1, waiting for transfers between devices, body(): far_packed = lax.ppermute(far_packed, 'gx', far_pairs)  27.4 us
    ppermute x2, waiting for transfers between devices, body(): lax.ppermute(part, 'az', [(i, (i + by) % sectors) for i in range(sectors)])  10.6 us
    pallas_call x1, Pallas kernels, inner_modes(): pl.pallas_call(functools.partial(modes_kernel, cycles=cycles, cells=cells...  10.3 us
    pallas_call x1, Pallas kernels, put_filtered(): pl.pallas_call(functools.partial(filter_kernel, cells=cells), grid=(plane...  6.63 us
    ppermute x1, starting transfers between devices, body(): far_flux = lax.ppermute(far_flux, 'gx', far_pairs)  4.52 us
    pallas_call x1, Pallas kernels, outer_plane(): pl.pallas_call(outer_kernel, grid_spec=pltpu.PrefetchScalarGridSpec(num_s...  3.76 us
    unnamed x20, local copies, waits for them, and re-layouts  3.75 us
  transfers between devices with their start and end apart: 5, of which 2 were waited for; matrix products, arithmetic and copies ran while one was open for 2% of the time, Pallas kernels for 50%

profile of v1, /device:TPU:1, one launch (start us, length us, event | category | flops | bytes accessed | tf_op | source)
XLA Modules:
  0.0 117.5 jit_solution(4808822917198048594)
XLA Ops:
  0.0 3.2 %inner_plane.1 = (f32[5,128,512]{2,1,0:T(8,128)}, f32[2,5,16,512]{3,2,1,0:T(8,128)}) custom-call(s32[1]{0:T(128)} %bitcast.odd_ref, f32[5,16,128,512]{3,2,1,0:T(8,128)} %state_ref.7, f32[5,16,128,512]{3,2,1,0:T(8,128)} %state_ref.7, f32[5,16,128,512]{3,2,1,0:T(8,128)} %state_ref.7), custom_call_target="tpu_custom_call" | custom-call | tf_op jit(solution)/shard_map/inner_plane/pallas_call | solution.py:142
  3.2 0.1 collective-permute-start.1
  3.3 3.8 %outer_plane.1 = (f32[5,128,512]{2,1,0:T(8,128)}, f32[5,32,128]{2,1,0:T(8,128)}) custom-call(s32[1]{0:T(128)} %bitcast.odd_ref, f32[5,16,128,512]{3,2,1,0:T(8,128)} %state_ref.7), custom_call_target="tpu_custom_call" | custom-call | tf_op jit(solution)/shard_map/outer_plane/pallas_call | solution.py:107
  7.1 4.5 %collective-permute-start = (f32[5,128,512]{2,1,0:T(8,128)}, f32[5,128,512]{2,1,0:T(8,128)S(1)}, u32[]{:S(2)}, u32[]{:S(2)}) collective-permute-start(f32[5,128,512]{2,1,0:T(8,128)} %get-tuple-element.9), channel_id=1, source_target_pairs={{2,4},{6,8},{10,12},{14,16},{18,20},{22,24},{26,28},{4,2},{8,6},{1... | collective-permute-start | bytes 3932168 | tf_op jit(solution)/shard_map/ppermute | solution.py:549
  11.6 1.9 %collective-permute-start.2 = (f32[5,32,128]{2,1,0:T(8,128)}, f32[5,32,128]{2,1,0:T(8,128)S(1)}, u32[]{:S(2)}, u32[]{:S(2)}) collective-permute-start(f32[5,32,128]{2,1,0:T(8,128)} %get-tuple-element.11), channel_id=1, source_target_pairs={{2,4},{6,8},{10,12},{14,16},{18,20},{22,24},{26,28},{4,2},{8,6},{1... | collective-permute-start | bytes 245768 | tf_op jit(solution)/shard_map/ppermute | solution.py:548
  13.5 0.6 dynamic-slice_bitcast_fusion.1.table_ref
  14.2 0.6 dynamic-slice_bitcast_fusion.edge_ref
  14.8 27.4 %collective-permute-done.2.far_ref = f32[5,32,128]{2,1,0:T(8,128)S(1)} collective-permute-done((f32[5,32,128]{2,1,0:T(8,128)}, f32[5,32,128]{2,1,0:T(8,128)S(1)}, u32[]{:S(2)}, u32[]{:S(2)}) %collective-permute-start.2) | collective-permute-done | bytes 81952 | tf_op jit(solution)/shard_map/ppermute | solution.py:548
  42.2 0.0 collective-permute-done.1.near_ref
  42.2 0.6 copy-done.4
  42.9 0.5 copy-done
  43.3 10.3 %inner_modes.1.refs_0_ = f32[1304,128]{1,0:T(8,128)} custom-call(s32[1]{0:T(128)} %bitcast.odd_ref, f32[16]{0:T(128)} %scale_ref.5, f32[5,16,128,512]{3,2,1,0:T(8,128)} %state_ref.7, f32[5,16,128,512]{3,2,1,0:T(8,128)} %state_ref.7, f32[5,16,128,512]{3,2,1,0:T(8,128)} %state_ref.7, s32[16,128,512]{2,1,0:T(8,128)} %level_ref.3, f32[1,512]{1,0:T(1,128)} %bitcast.8, ...), custom_call_target="tpu_custom_call" | custom-call | tf_op jit(solution)/shard_map/inner_modes/pallas_call | solution.py:284
  53.6 1.2 %collective-permute-start.3 = (f32[1304,128]{1,0:T(8,128)}, f32[1304,128]{1,0:T(8,128)S(1)}, u32[]{:S(2)}, u32[]{:S(2)}) collective-permute-start(f32[1304,128]{1,0:T(8,128)} %inner_modes.1.refs_0_), channel_id=1, source_target_pairs={{0,1},{1,0},{2,3},{3,2},{4,5},{5,4},{6,7},{7,6},{8,9},{9,8},{10,11... | collective-permute-start | bytes 2002952 | tf_op jit(solution)/shard_map/ppermute | solution.py:545
  54.8 0.3 collective-permute-start.4
  55.1 0.6 reshape_tile.3.cutoff_ref
  55.7 0.6 dynamic-slice_bitcast_fusion.2.table_ref
  56.4 10.6 %collective-permute-done.4.halo_ref = f32[2,5,16,512]{3,2,1,0:T(8,128)S(1)} collective-permute-done((f32[2,5,16,512]{3,2,1,0:T(8,128)S(1)}, f32[2,5,16,512]{3,2,1,0:T(8,128)S(1)}, u32[]{:S(2)}, u32[]{:S(2)}) %collective-permute-start.4) | collective-permute-done | bytes 327712 | tf_op jit(solution)/shard_map/ppermute | solution.py:545
  66.9 0.7 copy-done.3
  67.7 37.6 %bulk_update.1.refs_2_ = f32[5,16,128,512]{3,2,1,0:T(8,128)} custom-call(s32[1]{0:T(128)} %bitcast.odd_ref, f32[16]{0:T(128)} %scale_ref.5, f32[5,16,128,512]{3,2,1,0:T(8,128)} %state_ref.7, s32[16,128,512]{2,1,0:T(8,128)} %level_ref.3, f32[1,512]{1,0:T(1,128)} %bitcast.9, f32[5,512]{1,0:T(8,128)} %target_ref.3, f32[5,128,512]{2,1,0:T(8,128)} %copy-done, ...), custom_call_target="tpu_custom_call" | custom-call | tf_op jit(solution)/shard_map/bulk_update/pallas_call | solution.py:404
  105.2 0.8 copy-done.2
  106.1 6.6 %put_filtered.1.state_ref = f32[5,16,128,512]{3,2,1,0:T(8,128)} custom-call(s32[1,128]{1,0:T(1,128)} %reshape_tile.3.cutoff_ref, bf16[128,256]{1,0:T(8,128)(2,1)} %dynamic-slice_bitcast_fusion.2.table_ref, f32[1304,128]{1,0:T(8,128)} %inner_modes.1.refs_0_, f32[1304,128]{1,0:T(8,128)} %copy-done.2, ...), custom_call_target="tpu_custom_call", output_to_operand_aliasing={{}: (4, {})} | custom-call | tf_op jit(solution)/shard_map/put_filtered/pallas_call | solution.py:467
  112.7 0.0 collective-permute-done.flux_ref
  112.7 1.1 copy-done.1
  113.8 3.7 %finish_plane.1 = f32[5,16,128,512]{3,2,1,0:T(8,128)} custom-call(s32[1]{0:T(128)} %bitcast.odd_ref, f32[16]{0:T(128)} %scale_ref.5, f32[5,128,512]{2,1,0:T(8,128)} %copy-done.1, f32[5,16,128,512]{3,2,1,0:T(8,128)} %put_filtered.1.state_ref), custom_call_target="tpu_custom_call", output_to_operand_aliasing={{}: (3, {})} | custom-call | tf_op jit(solution)/shard_map/finish_plane/pallas_call | solution.py:494
  (17 shorter events, 0.0 us)
Async XLA Ops:
  3.2 10.3 %copy-start.7 = (bf16[2,128,256]{2,1,0:T(8,128)(2,1)S(1)}, bf16[2,128,256]{2,1,0:T(8,128)(2,1)}, u32[]{:S(2)}) copy-start(bf16[2,128,256]{2,1,0:T(8,128)(2,1)} %constant.30.clone) | copy-start | bytes 393220
  3.2 11.0 %copy-start.6 = (f32[2,2,64,128]{3,2,1,0:T(8,128)S(1)}, f32[2,2,64,128]{3,2,1,0:T(8,128)}, u32[]{:S(2)}) copy-start(f32[2,2,64,128]{3,2,1,0:T(8,128)} %constant.31.clone) | copy-start | bytes 393220
  3.2 39.0 %collective-permute-start.1 = (f32[5,128,512]{2,1,0:T(8,128)}, f32[5,128,512]{2,1,0:T(8,128)S(1)}, u32[]{:S(2)}, u32[]{:S(2)}) collective-permute-start(f32[5,128,512]{2,1,0:T(8,128)} %get-tuple-element.10), channel_id=1, source_target_pairs={{2,0},{0,2},{6,4},{4,6},{10,8},{8,10},{14,12},{12,14},{18,16},{16,... | collective-permute-start | bytes 3932168 | tf_op jit(solution)/shard_map/ppermute | solution.py:551
  7.1 105.6 %collective-permute-start = (f32[5,128,512]{2,1,0:T(8,128)}, f32[5,128,512]{2,1,0:T(8,128)S(1)}, u32[]{:S(2)}, u32[]{:S(2)}) collective-permute-start(f32[5,128,512]{2,1,0:T(8,128)} %get-tuple-element.9), channel_id=1, source_target_pairs={{2,4},{6,8},{10,12},{14,16},{18,20},{22,24},{26,28},{4,2},{8,6},{1... | collective-permute-start | bytes 3932168 | tf_op jit(solution)/shard_map/ppermute | solution.py:549
  11.6 30.6 %collective-permute-start.2 = (f32[5,32,128]{2,1,0:T(8,128)}, f32[5,32,128]{2,1,0:T(8,128)S(1)}, u32[]{:S(2)}, u32[]{:S(2)}) collective-permute-start(f32[5,32,128]{2,1,0:T(8,128)} %get-tuple-element.11), channel_id=1, source_target_pairs={{2,4},{6,8},{10,12},{14,16},{18,20},{22,24},{26,28},{4,2},{8,6},{1... | collective-permute-start | bytes 245768 | tf_op jit(solution)/shard_map/ppermute | solution.py:548
  42.2 0.6 copy-start.4
  42.2 1.1 copy-start
  43.3 11.5 %copy-start.9 = (f32[2,5,16,512]{3,2,1,0:T(8,128)S(1)}, f32[2,5,16,512]{3,2,1,0:T(8,128)}, u32[]{:S(2)}) copy-start(f32[2,5,16,512]{3,2,1,0:T(8,128)} %get-tuple-element.12) | copy-start | bytes 983044
  43.3 11.8 %copy-start.8 = (s32[32]{0:T(128)S(1)}, s32[32]{0:T(128)}, u32[]{:S(2)}) copy-start(s32[32]{0:T(128)} %param.14) | copy-start | bytes 388
  43.3 12.4 %copy-start.5 = (bf16[2,128,256]{2,1,0:T(8,128)(2,1)S(1)}, bf16[2,128,256]{2,1,0:T(8,128)(2,1)}, u32[]{:S(2)}) copy-start(bf16[2,128,256]{2,1,0:T(8,128)(2,1)} %constant.32.clone) | copy-start | bytes 393220
  53.6 51.6 %collective-permute-start.3 = (f32[1304,128]{1,0:T(8,128)}, f32[1304,128]{1,0:T(8,128)S(1)}, u32[]{:S(2)}, u32[]{:S(2)}) collective-permute-start(f32[1304,128]{1,0:T(8,128)} %inner_modes.1.refs_0_), channel_id=1, source_target_pairs={{0,1},{1,0},{2,3},{3,2},{4,5},{5,4},{6,7},{7,6},{8,9},{9,8},{10,11... | collective-permute-start | bytes 2002952 | tf_op jit(solution)/shard_map/ppermute | solution.py:545
  54.8 12.1 %collective-permute-start.4 = (f32[2,5,16,512]{3,2,1,0:T(8,128)S(1)}, f32[2,5,16,512]{3,2,1,0:T(8,128)S(1)}, u32[]{:S(2)}, u32[]{:S(2)}) collective-permute-start(f32[2,5,16,512]{3,2,1,0:T(8,128)S(1)} %copy-done.9), channel_id=1, source_target_pairs={{0,1},{1,0},{2,3},{3,2},{4,5},{5,4},{6,7},{7,6},{8,9},{9,8},{10,11... | collective-permute-start | bytes 983048 | tf_op jit(solution)/shard_map/ppermute | solution.py:545
  66.9 0.7 copy-start.3
  105.2 0.8 copy-start.2
  112.7 1.1 copy-start.1

commit v2 on v1

v2 whole, which is shorter than its diff:
```python
import functools
import math

import jax
import jax.numpy as jnp
import ml_dtypes
import numpy as np
from jax import lax
from jax.experimental import pallas as pl
from jax.experimental.pallas import tpu as pltpu
from jax.sharding import PartitionSpec as P

CYCLE = 32
LANES = 128
PACK = LANES // CYCLE

gas_factor = 0.4
time_step = 0.02
sponge_rate = 4.0

MIB = 1024 * 1024


def params(steps, limit):
    return pltpu.CompilerParams(
        dimension_semantics=("arbitrary",) * steps, vmem_limit_bytes=limit * MIB
    )


def resident(x):
    return pltpu.with_memory_space_constraint(x, pltpu.VMEM)


VMEM_SPEC = pl.BlockSpec(memory_space=pltpu.VMEM)
SMEM_SPEC = pl.BlockSpec(memory_space=pltpu.SMEM)
HBM_SPEC = pl.BlockSpec(memory_space=pl.ANY)


def products(q):
    density, m, n, s, energy = q
    inverse = pltpu.reciprocal(density, approx=True)
    u, v, w = m * inverse, n * inverse, s * inverse
    mu, nv, sw = m * u, n * v, s * w
    pressure = gas_factor * energy - (0.5 * gas_factor) * (mu + nv + sw)
    return u, v, w, mu, nv, sw, pressure, energy + pressure


def axial_flux(q):
    u, _, _, mu, _, _, pressure, enthalpy = products(q)
    return (q[1], mu + pressure, q[2] * u, q[3] * u, enthalpy * u)


def swirl_flux(q):
    _, _, w, _, _, sw, pressure, enthalpy = products(q)
    return (q[3], q[1] * w, q[2] * w, sw + pressure, enthalpy * w)


def all_fluxes(q):
    u, v, w, mu, nv, sw, pressure, enthalpy = products(q)
    mv, mw, nw = q[1] * v, q[1] * w, q[2] * w
    axial = (q[1], mu + pressure, mv, mw, enthalpy * u)
    radial = (q[2], mv, nv + pressure, nw, enthalpy * v)
    swirl = (q[3], mw, nw, sw + pressure, enthalpy * w)
    return axial, radial, swirl


def fill_rows(rows_ref, inv_dr, start, cycles, cells):
    width = rows_ref.shape[-1]
    cycle = lax.broadcasted_iota(jnp.int32, (8, width), 1) + start
    spacing = 4.0 / cycles
    radius = 1.0 + spacing * cycle.astype(jnp.float32)
    inverse = 1.0 / radius
    half = (0.5 * time_step) * jnp.broadcast_to(inv_dr, (8, width)) * inverse
    rows_ref[0] = jnp.where(cycle == start + width - 1, 0.0, half * (radius + spacing))
    rows_ref[1] = jnp.where(cycle == 0, 0.0, half * (radius - spacing))
    rows_ref[2] = (time_step * cells / (4.0 * math.pi)) * inverse


def base_update(q, sponge, target, ahead, behind, up, down, scaled, cells):
    source = 4.0 * math.pi / cells
    result = []
    for f in range(5):
        value = q[f] - sponge * (q[f] - target[f]) - (up * ahead[f] - down * behind[f])
        if f == 2:
            value = value + source * scaled[3]
        if f == 3:
            value = value - source * scaled[2]
        result.append(value)
    return result


def outer_kernel(odd_ref, state_ref, flux_ref, packed_ref):
    step = pl.program_id(0)
    rows = packed_ref.shape[1]
    blocks = state_ref.shape[2] // rows
    flux = axial_flux([state_ref[f, 0] for f in range(5)])
    lane = lax.broadcasted_iota(jnp.int32, packed_ref.shape[1:], 1)
    for f in range(5):
        flux_ref[f, pl.ds(pl.multiple_of(step * state_ref.shape[2], 8), state_ref.shape[2])] = flux[f]
        for i in range(blocks):
            block = step * blocks + i
            turned = pltpu.roll(flux[f][i * rows : (i + 1) * rows, :LANES], block * CYCLE, 1)
            packed_ref[f] = jnp.where(lane // CYCLE == block, turned, packed_ref[f])


def outer_plane(odd, state):
    _, planes, columns, cycles = state.shape
    steps = 2
    return pl.pallas_call(
        outer_kernel,
        grid_spec=pltpu.PrefetchScalarGridSpec(
            num_scalar_prefetch=1,
            grid=(steps,),
            in_specs=[
                pl.BlockSpec((5, 1, columns // steps, cycles), lambda b, odd: (0, odd[0] * (planes - 1), b, 0))
            ],
            out_specs=[VMEM_SPEC, VMEM_SPEC],
        ),
        out_shape=[
            pltpu.VMEM((5, columns, cycles), jnp.float32),
            pltpu.VMEM((5, columns // PACK, LANES), jnp.float32),
        ],
        compiler_params=params(1, 8),
        name="outer_plane",
    )(odd, state)


def inner_kernel(odd_ref, state_ref, first_ref, last_ref, flux_ref, edge_ref):
    step = pl.program_id(0)
    rows = state_ref.shape[2]
    flux = axial_flux([state_ref[f, 0] for f in range(5)])
    for f in range(5):
        flux_ref[f, pl.ds(pl.multiple_of(step * rows, 8), rows)] = flux[f]
    low = swirl_flux([last_ref[f, :, 7, :] for f in range(5)])
    high = swirl_flux([first_ref[f, :, 0, :] for f in range(5)])
    planes = pl.ds(pl.multiple_of(step * 8, 8), 8)
    for f in range(5):
        edge_ref[0, f, planes] = low[f]
        edge_ref[1, f, planes] = high[f]


def inner_plane(odd, state):
    _, planes, columns, cycles = state.shape
    steps = planes // 8
    return pl.pallas_call(
        inner_kernel,
        grid_spec=pltpu.PrefetchScalarGridSpec(
            num_scalar_prefetch=1,
            grid=(steps,),
            in_specs=[
                pl.BlockSpec((5, 1, columns // steps, cycles), lambda b, odd: (0, (1 - odd[0]) * (planes - 1), b, 0)),
                pl.BlockSpec((5, 8, 8, cycles), lambda b, odd: (0, b, 0, 0)),
                pl.BlockSpec((5, 8, 8, cycles), lambda b, odd: (0, b, columns // 8 - 1, 0)),
            ],
            out_specs=[VMEM_SPEC, VMEM_SPEC],
        ),
        out_shape=[
            pltpu.VMEM((5, columns, cycles), jnp.float32),
            pltpu.VMEM((2, 5, planes, cycles), jnp.float32),
        ],
        compiler_params=params(1, 12),
        name="inner_plane",
    )(odd, state, state, state)


def modes_kernel(
    place_ref, scale_ref, state_ref, before_ref, after_ref, level_ref, inv_dr_ref, target_ref, table_ref, edge_ref,
    near_ref, far_ref, sums_ref, tile_ref, behind_ref, rows_ref, axial_ref, swirl_ref, base_ref, split_ref,
    *, cycles, cells, chunk,
):
    step = pl.program_id(0)
    steps = pl.num_programs(0)
    columns = state_ref.shape[2]
    odd = place_ref[0]
    far_rows = far_ref.shape[1]

    @pl.when(step == 0)
    def _():
        fill_rows(rows_ref, inv_dr_ref[...], 0, cycles, cells)
        for f in range(5):
            for i in range(PACK):
                swirl_ref[i, f, 0:8] = jnp.zeros((8, LANES), jnp.float32)
                swirl_ref[i, f, columns + 8 : columns + 16] = jnp.zeros((8, LANES), jnp.float32)

    def load(ref, plane, start):
        return [ref[f, plane, pl.ds(start, chunk), :] for f in range(5)]

    def halo(slot, use_near):
        for f in range(5):
            for b in range(PACK):
                away = far_ref[f]
                away = away if b == 0 else pltpu.roll(away, LANES - b * CYCLE, 1)
                near = near_ref[f, b * far_rows : (b + 1) * far_rows, :LANES]
                axial_ref[slot, f, b * far_rows : (b + 1) * far_rows] = jnp.where(
                    use_near, near, jnp.where(lane[:far_rows] < CYCLE, away, 0.0)
                )

    def neighbour(slot, ref):
        def one(c, _):
            start = pl.multiple_of(c * chunk, chunk)
            flux = axial_flux(load(ref, 0, start))
            for f in range(5):
                axial_ref[slot, f, pl.ds(start, chunk)] = flux[f]
            return 0

        lax.fori_loop(0, columns // chunk, one, 0, unroll=True)

    lane = lax.broadcasted_iota(jnp.int32, (chunk, LANES), 1)
    pl.when(step == 0)(lambda: halo(0, odd == 1))
    pl.when(step > 0)(lambda: neighbour(0, before_ref))
    pl.when(step == steps - 1)(lambda: halo(PACK + 1, odd == 0))
    pl.when(step < steps - 1)(lambda: neighbour(PACK + 1, after_ref))

    def wide(row):
        return jnp.broadcast_to(row[None], (chunk // 8, 8, LANES)).reshape(chunk, LANES)

    def first(c, _):
        start = pl.multiple_of(c * chunk, chunk)
        up, down, around = [wide(rows_ref[k]) for k in range(3)]
        target = [jnp.broadcast_to(target_ref[f : f + 1], (chunk, LANES)) for f in range(5)]
        for i in range(PACK):
            q = load(state_ref, i, start)
            axial, radial, swirl = all_fluxes(q)
            sponge = level_ref[i, pl.ds(start, chunk), :].astype(jnp.float32) * (time_step * sponge_rate)
            scaled = [around * flux for flux in swirl]
            ahead = [pltpu.roll(flux, LANES - 1, 1) for flux in radial]
            behind = [pltpu.roll(flux, 1, 1) for flux in radial]
            base = base_update(q, sponge, target, ahead, behind, up, down, scaled, cells)
            plane = step * PACK + i
            for f in range(5):
                behind_ref[f, plane, pl.ds(start, chunk)] = behind[f]
                axial_ref[i + 1, f, pl.ds(start, chunk)] = axial[f]
                swirl_ref[i, f, pl.ds(start + 8, chunk)] = scaled[f]
                base_ref[i, f, pl.ds(start, chunk)] = base[f]
        return 0

    lax.fori_loop(0, columns // chunk, first, 0, unroll=True)

    def packed(parts, rows):
        result = parts[0]
        for i in range(1, PACK):
            result = jnp.where(lane[:rows] // CYCLE == i, pltpu.roll(parts[i], i * CYCLE, 1), result)
        return result

    factor = [(0.5 * time_step) * scale_ref[step * PACK + i] for i in range(PACK)]
    for f in range(5):
        total = jnp.zeros((8, LANES), jnp.float32)
        for c in range(columns // chunk):
            start = c * chunk
            parts = []
            for i in range(PACK):
                value = base_ref[i, f, start : start + chunk]
                value = value - factor[i] * (
                    axial_ref[i + 2, f, start : start + chunk] - axial_ref[i, f, start : start + chunk]
                )
                inside = value + (
                    swirl_ref[i, f, start + 7 : start + 7 + chunk] - swirl_ref[i, f, start + 9 : start + 9 + chunk]
                )
                tile_ref[f, step * PACK + i, start : start + chunk] = inside
                parts.append(inside)
            value = packed(parts, chunk)
            high = value.astype(jnp.bfloat16)
            split_ref[f, start : start + chunk] = high
            split_ref[f, columns + start : columns + start + chunk] = (value - high.astype(jnp.float32)).astype(
                jnp.bfloat16
            )
            total = total + value.reshape(chunk // 8, 8, LANES).sum(axis=0)
        sums = jnp.dot(table_ref[0], split_ref[f], preferred_element_type=jnp.float32)
        half = sums.shape[0] // 2
        start_row = packed([swirl_ref[i, f, 8:16] for i in range(PACK)], 8)[0:1]
        end_row = packed([swirl_ref[i, f, columns : columns + 8] for i in range(PACK)], 8)[7:8]
        group = step * 5 + f
        sums_ref[pl.ds(pl.multiple_of(group * half, half), half), :] = (
            sums[:half] + sums[half:] + (edge_ref[0, 1] * end_row - edge_ref[0, 0] * start_row)
        )
        mean = total.sum(axis=0, keepdims=True) + (end_row - start_row)
        sums_ref[pl.ds(steps * 5 * half + group, 1), :] = mean


def mode_rows(planes, half):
    groups = 5 * planes // PACK
    return groups * half + -(-groups // 8) * 8


def inner_modes(place, scale, state, sponge, inv_dr, target, table, edge, near, far, cells):
    _, planes, columns, cycles = state.shape
    half = table.shape[1] // 2
    chunk = min(32, columns)
    whole = lambda *shape: pl.BlockSpec(shape, lambda g, place: (0,) * len(shape))
    tile = pltpu.VMEM((5, planes, columns, LANES), jnp.float32)
    return pl.pallas_call(
        functools.partial(modes_kernel, cycles=cycles, cells=cells, chunk=chunk),
        grid_spec=pltpu.PrefetchScalarGridSpec(
            num_scalar_prefetch=1,
            grid=(planes // PACK,),
            in_specs=[
                SMEM_SPEC,
                pl.BlockSpec((5, PACK, columns, LANES), lambda g, place: (0, g, 0, 0)),
                pl.BlockSpec((5, 1, columns, LANES), lambda g, place: (0, jnp.maximum(g * PACK - 1, 0), 0, 0)),
                pl.BlockSpec(
                    (5, 1, columns, LANES), lambda g, place: (0, jnp.minimum(g * PACK + PACK, planes - 1), 0, 0)
                ),
                pl.BlockSpec((PACK, columns, LANES), lambda g, place: (g, 0, 0)),
                whole(1, LANES),
                whole(5, LANES),
                pl.BlockSpec((1,) + table.shape[1:], lambda g, place: (place[1], 0, 0)),
                pl.BlockSpec((1,) + edge.shape[1:], lambda g, place: (place[1], 0, 0, 0)),
                VMEM_SPEC,
                VMEM_SPEC,
            ],
            out_specs=[VMEM_SPEC, VMEM_SPEC, VMEM_SPEC],
            scratch_shapes=[
                pltpu.VMEM((3, 8, LANES), jnp.float32),
                pltpu.VMEM((PACK + 2, 5, columns, LANES), jnp.float32),
                pltpu.VMEM((PACK, 5, columns + 16, LANES), jnp.float32),
                pltpu.VMEM((PACK, 5, columns, LANES), jnp.float32),
                pltpu.VMEM((5, 2 * columns, LANES), jnp.bfloat16),
            ],
        ),
        out_shape=[pltpu.VMEM((mode_rows(planes, half), LANES), jnp.float32), tile, tile],
        compiler_params=params(1, 20),
        name="inner_modes",
    )(place, scale, state, state, state, sponge, inv_dr, target, table, edge, resident(near), resident(far))


IN_SLOTS = 3
OUT_SLOTS = 2


def update_kernel(
    place_ref, scale_ref, inv_dr_ref, target_ref, near_ref, halo_ref, behind_ref, state_ref, level_ref,
    out_ref, ahead_ref, rows_ref, fields_ref, levels_ref, result_ref, axial_even_ref, axial_odd_ref, swirl_even_ref,
    swirl_odd_ref, base_ref, field_sem, level_sem, result_sem, *, cells, chunk, unroll,
):
    axial_refs = (axial_even_ref, axial_odd_ref)
    swirl_refs = (swirl_even_ref, swirl_odd_ref)
    planes, columns, cycles = level_ref.shape
    tiles = cycles // LANES - 1
    odd = place_ref[0]
    rest = pl.ds(LANES, cycles - LANES)
    lane = lax.broadcasted_iota(jnp.int32, (chunk, LANES), 1)

    def fetch(plane):
        slot = lax.rem(plane, IN_SLOTS)
        return (
            pltpu.make_async_copy(state_ref.at[:, plane, :, rest], fields_ref.at[slot], field_sem.at[slot]),
            pltpu.make_async_copy(level_ref.at[plane, :, rest], levels_ref.at[slot], level_sem.at[slot]),
        )

    def store(plane):
        slot = lax.rem(plane, OUT_SLOTS)
        return pltpu.make_async_copy(result_ref.at[slot], out_ref.at[:, plane, :, rest], result_sem.at[slot])

    for plane in range(IN_SLOTS):
        for copy in fetch(plane):
            copy.start()

    fill_rows(rows_ref, inv_dr_ref[:, LANES:], LANES, cycles, cells)

    def wide(k, tile):
        row = rows_ref[k, :, tile * LANES : (tile + 1) * LANES]
        return jnp.broadcast_to(row[None], (chunk // 8, 8, LANES)).reshape(chunk, LANES)

    def outside(c, use):
        rows = pl.ds(pl.multiple_of(c * chunk, chunk), chunk)
        return [[jnp.where(use, near_ref[f, rows, (k + 1) * LANES : (k + 2) * LANES], 0.0) for f in range(5)] for k in range(tiles)]

    def before(c, _):
        axial = outside(c, odd == 1)
        for k in range(tiles):
            for f in range(5):
                axial_odd_ref[f, k, pl.ds(pl.multiple_of(c * chunk, chunk), chunk)] = axial[k][f]
        return 0

    lax.fori_loop(0, columns // chunk, before, 0)

    def finish(plane, parity, start, k, axial):
        rows = pl.ds(start, chunk)
        factor = (0.5 * time_step) * scale_ref[jnp.maximum(plane - 1, 0)]
        axial_ref, swirl_ref = axial_refs[parity], swirl_refs[1 - parity]
        slot = lax.rem(plane + OUT_SLOTS - 1, OUT_SLOTS)
        for f in range(5):
            value = base_ref[f, k, rows] - factor * (axial[f] - axial_ref[f, k, rows])
            value = value + (
                swirl_ref[f, k, pl.ds(start + 7, chunk)] - swirl_ref[f, k, pl.ds(start + 9, chunk)]
            )
            result_ref[slot, f, rows, k * LANES : (k + 1) * LANES] = value

    def one_chunk(plane, parity, c):
        start = pl.multiple_of(c * chunk, chunk)
        rows = pl.ds(start, chunk)
        slot = lax.rem(plane, IN_SLOTS)

        def open_tile(k):
            q = [fields_ref[slot, f, rows, k * LANES : (k + 1) * LANES] for f in range(5)]
            axial, radial, swirl = all_fluxes(q)
            ahead = [pltpu.roll(flux, LANES - 1, 1) for flux in radial]
            behind = [pltpu.roll(flux, 1, 1) for flux in radial]
            return q, axial, swirl, ahead, behind

        def close_tile(k, last, this, following):
            q, axial, swirl, ahead, behind = this
            if following is not None:
                ahead = [jnp.where(lane == LANES - 1, following[3][f], ahead[f]) for f in range(5)]
            if last is not None:
                first = last[4]
            else:
                first = [behind_ref[f, plane, rows] for f in range(5)]
                for f in range(5):
                    ahead_ref[f, plane, rows] = this[3][f]
            behind = [jnp.where(lane == 0, first[f], behind[f]) for f in range(5)]
            sponge = levels_ref[slot, rows, k * LANES : (k + 1) * LANES].astype(jnp.float32) * (
                time_step * sponge_rate
            )
            target = [
                jnp.broadcast_to(target_ref[f : f + 1, (k + 1) * LANES : (k + 2) * LANES], (chunk, LANES))
                for f in range(5)
            ]
            around = wide(2, k)
            scaled = [around * flux for flux in swirl]
            base = base_update(q, sponge, target, ahead, behind, wide(0, k), wide(1, k), scaled, cells)
            finish(plane, parity, start, k, axial)
            for f in range(5):
                base_ref[f, k, rows] = base[f]
                axial_refs[parity][f, k, rows] = axial[f]
                swirl_refs[parity][f, k, pl.ds(start + 8, chunk)] = scaled[f]

        opened = [open_tile(0)]
        for k in range(tiles):
            if k + 1 < tiles:
                opened.append(open_tile(k + 1))
            close_tile(
                k, opened[k - 1] if k else None, opened[k], opened[k + 1] if k + 1 < tiles else None
            )

    def one_plane(plane, parity):
        for copy in fetch(plane):
            copy.wait()
        for f in range(5):
            for side, row in ((0, 7), (1, columns + 8)):
                edge = halo_ref[side, f, pl.ds(plane, 1), :]
                for k in range(tiles):
                    around = rows_ref[2, 0:1, k * LANES : (k + 1) * LANES]
                    swirl_refs[parity][f, k, row : row + 1] = around * edge[:, (k + 1) * LANES : (k + 2) * LANES]
        pl.when(plane > OUT_SLOTS)(lambda: store(plane - 1 - OUT_SLOTS).wait())

        def step(c, _):
            one_chunk(plane, parity, c)
            return 0

        lax.fori_loop(0, columns // chunk, step, 0, unroll=unroll)
        pl.when(plane > 0)(lambda: store(plane - 1).start())

        @pl.when(plane + IN_SLOTS < planes)
        def _():
            for copy in fetch(plane + IN_SLOTS):
                copy.start()

    def two_planes(pair, _):
        for parity in range(2):
            one_plane(2 * pair + parity, parity)
        return 0

    lax.fori_loop(0, planes // 2, two_planes, 0)
    store(planes - 1 - OUT_SLOTS).wait()

    def last(c, _):
        start = pl.multiple_of(c * chunk, chunk)
        axial = outside(c, odd == 0)
        for k in range(tiles):
            finish(planes, 0, start, k, axial[k])
        return 0

    lax.fori_loop(0, columns // chunk, last, 0)
    store(planes - 1).start()
    for plane in range(planes - OUT_SLOTS, planes):
        store(plane).wait()


def bulk_update(place, scale, state, sponge, inv_dr, target, near, halo, behind, cells, chunk=8, unroll=16):
    _, planes, columns, cycles = state.shape
    tiles = cycles // LANES - 1
    width = cycles - LANES
    return pl.pallas_call(
        functools.partial(update_kernel, cells=cells, chunk=chunk, unroll=unroll),
        in_specs=[SMEM_SPEC, SMEM_SPEC, VMEM_SPEC, VMEM_SPEC, VMEM_SPEC, VMEM_SPEC, VMEM_SPEC, HBM_SPEC, HBM_SPEC],
        out_specs=[HBM_SPEC, VMEM_SPEC],
        scratch_shapes=[
            pltpu.VMEM((3, 8, width), jnp.float32),
            pltpu.VMEM((IN_SLOTS, 5, columns, width), jnp.float32),
            pltpu.VMEM((IN_SLOTS, columns, width), jnp.int32),
            pltpu.VMEM((OUT_SLOTS, 5, columns, width), jnp.float32),
            pltpu.VMEM((5, tiles, columns, LANES), jnp.float32),
            pltpu.VMEM((5, tiles, columns, LANES), jnp.float32),
            pltpu.VMEM((5, tiles, columns + 16, LANES), jnp.float32),
            pltpu.VMEM((5, tiles, columns + 16, LANES), jnp.float32),
            pltpu.VMEM((5, tiles, columns, LANES), jnp.float32),
            pltpu.SemaphoreType.DMA((IN_SLOTS,)),
            pltpu.SemaphoreType.DMA((IN_SLOTS,)),
            pltpu.SemaphoreType.DMA((OUT_SLOTS,)),
        ],
        out_shape=[
            jax.ShapeDtypeStruct(state.shape, jnp.float32),
            pltpu.VMEM((5, planes, columns, LANES), jnp.float32),
        ],
        compiler_params=pltpu.CompilerParams(vmem_limit_bytes=20 * MIB),
        name="bulk_update",
    )(place, scale, inv_dr, target, resident(near), resident(halo), resident(behind), state, sponge)


def filter_kernel(
    place_ref, cutoff_ref, table_ref, inv_dr_ref, tile_ref, ahead_ref, halo_ref, *refs, cells, cycles
):
    *sums, state_ref, out_ref, split_ref = refs
    step = pl.program_id(0)
    steps = pl.num_programs(0)
    half = table_ref.shape[2] // 4
    count = half // 2
    columns = out_ref.shape[2]
    mode = lax.broadcasted_iota(jnp.int32, (half, LANES), 0)
    mode = jnp.where(mode >= count, mode - count, mode) + 1
    cut = jnp.concatenate([cutoff_ref[...]] * PACK, axis=1)
    weight = jnp.where(mode <= cut, 2.0 / cells, 0.0)
    lane = lax.broadcasted_iota(jnp.int32, (columns, LANES), 1)
    spacing = 4.0 / cycles
    edge = 1.0 + spacing * (LANES - 1)
    up = (0.5 * time_step) * inv_dr_ref[...] * ((edge + spacing) / edge)
    up = jnp.where(lane == LANES - 1, up, 0.0)
    cycle = lax.broadcasted_iota(jnp.int32, (1, LANES), 1)
    around = (time_step * cells / (4.0 * math.pi)) / (1.0 + spacing * cycle.astype(jnp.float32))
    around = jnp.where(cycle < CYCLE, 0.0, around)
    for f in range(5):
        group = step * 5 + f
        rows = pl.ds(pl.multiple_of(group * half, half), half)
        coefficient = sums[0][rows, :]
        mean = sums[0][pl.ds(steps * 5 * half + group, 1), :]
        for other in sums[1:]:
            coefficient = coefficient + other[rows, :]
            mean = mean + other[pl.ds(steps * 5 * half + group, 1), :]
        coefficient = coefficient * weight
        high = coefficient.astype(jnp.bfloat16)
        low = (coefficient - high.astype(jnp.float32)).astype(jnp.bfloat16)
        for k in range(2):
            split_ref[f, 2 * k * half : (2 * k + 1) * half] = high
            split_ref[f, (2 * k + 1) * half : (2 * k + 2) * half] = low
        values = jnp.dot(table_ref[0], split_ref[f], preferred_element_type=jnp.float32) + mean * (1.0 / cells)
        for i in range(PACK):
            turned = values if i == 0 else pltpu.roll(values, LANES - i * CYCLE, 1)
            plane = step * PACK + i
            out_ref[f, i] = jnp.where(lane < CYCLE, turned, tile_ref[f, plane] - up * ahead_ref[f, plane])
            low = halo_ref[0, f, pl.ds(plane, 1), :][:, :LANES]
            high = halo_ref[1, f, pl.ds(plane, 1), :][:, :LANES]
            out_ref[f, i, 0:1] = out_ref[f, i, 0:1] + around * low
            out_ref[f, i, columns - 1 : columns] = out_ref[f, i, columns - 1 : columns] - around * high


def put_filtered(place, cutoff, table, inv_dr, tile, ahead, halo, sums, updated, cells):
    _, planes, columns, cycles = updated.shape
    return pl.pallas_call(
        functools.partial(filter_kernel, cells=cells, cycles=cycles),
        grid_spec=pltpu.PrefetchScalarGridSpec(
            num_scalar_prefetch=1,
            grid=(planes // PACK,),
            in_specs=[
                pl.BlockSpec(cutoff.shape, lambda g, place: (0, 0)),
                pl.BlockSpec((1,) + table.shape[1:], lambda g, place: (place[1], 0, 0)),
                pl.BlockSpec((1, LANES), lambda g, place: (0, 0)),
                VMEM_SPEC,
                VMEM_SPEC,
                VMEM_SPEC,
            ]
            + [VMEM_SPEC] * len(sums)
            + [HBM_SPEC],
            out_specs=pl.BlockSpec((5, PACK, columns, LANES), lambda g, place: (0, g, 0, 0)),
            scratch_shapes=[pltpu.VMEM((5, table.shape[2], LANES), jnp.bfloat16)],
        ),
        out_shape=jax.ShapeDtypeStruct(updated.shape, jnp.float32),
        input_output_aliases={7 + len(sums): 0},
        compiler_params=params(1, 12),
        name="put_filtered",
    )(place, cutoff, table, inv_dr, resident(tile), resident(ahead), resident(halo),
      *(resident(part) for part in sums), updated)


def finish_kernel(place_ref, scale_ref, flux_ref, state_ref, out_ref):
    odd = place_ref[0]
    planes = scale_ref.shape[0]
    rows = out_ref.shape[2]
    factor = (0.5 * time_step) * scale_ref[odd * (planes - 1)]
    factor = jnp.where(odd == 1, -factor, factor)
    lane = lax.broadcasted_iota(jnp.int32, out_ref.shape[2:], 1)
    start = pl.multiple_of(pl.program_id(0) * rows, 8)
    for f in range(5):
        out_ref[f, 0] = state_ref[f, 0] + jnp.where(lane < CYCLE, 0.0, factor * flux_ref[f, pl.ds(start, rows)])


def finish_plane(place, scale, flux, updated):
    _, planes, columns, cycles = updated.shape
    steps = 2
    block = pl.BlockSpec((5, 1, columns // steps, cycles), lambda b, place: (0, place[0] * (planes - 1), b, 0))
    return pl.pallas_call(
        finish_kernel,
        grid_spec=pltpu.PrefetchScalarGridSpec(
            num_scalar_prefetch=1,
            grid=(steps,),
            in_specs=[SMEM_SPEC, VMEM_SPEC, block],
            out_specs=block,
        ),
        out_shape=jax.ShapeDtypeStruct(updated.shape, jnp.float32),
        input_output_aliases={3: 0},
        compiler_params=params(1, 12),
        name="finish_plane",
    )(place, scale, resident(flux), updated)


def mode_tables(cells, sectors):
    columns = cells // sectors
    mode = np.arange(1, cells // 8 + 1)

    def waves(cell):
        angle = 2.0 * np.pi / cells * ((mode[:, None] * cell[None, :]) % cells)
        return np.concatenate([np.cos(angle), np.sin(angle)])

    forward, inverse, edge = [], [], []
    for sector in range(sectors):
        wave = waves(sector * columns + np.arange(columns))
        high = wave.astype(ml_dtypes.bfloat16)
        low = (wave - high.astype(np.float64)).astype(ml_dtypes.bfloat16)
        forward.append(np.block([[high, high], [low, low]]))
        inverse.append(np.concatenate([high.T, high.T, low.T, low.T], axis=1))
        ends = waves(np.array([sector * columns - 1, (sector + 1) * columns]) % cells)
        edge.append(np.broadcast_to(ends.T[:, :, None], (2, ends.shape[0], LANES)))
    return np.stack(forward), np.stack(inverse), np.stack(edge).astype(np.float32)


def body(forward, inverse, edge, cells, state, sponge_level, inv_dx, inv_dr, target, cutoff):
    sectors = lax.axis_size("az")
    rows = lax.axis_size("gx")
    place = jnp.stack([lax.rem(lax.axis_index("gx"), 2), lax.axis_index("az")]).astype(jnp.int32)
    cycles = state.shape[3]
    inv_dr = inv_dr.reshape(1, cycles)
    cutoff = cutoff.reshape(1, CYCLE)

    near_pairs = [(i ^ 1, i) for i in range(rows) if i ^ 1 < rows]
    far_pairs = [(i, i + 1) for i in range(1, rows - 1, 2)] + [(i + 1, i) for i in range(1, rows - 1, 2)]
    shifted = lambda part, by: lax.ppermute(part, "az", [(i, (i + by) % sectors) for i in range(sectors)])

    far_flux, far_packed = outer_plane(place, state)
    far_packed = lax.ppermute(far_packed, "gx", far_pairs)
    far_flux = lax.ppermute(far_flux, "gx", far_pairs)
    near_flux, edges = inner_plane(place, state)
    near_flux = lax.ppermute(near_flux, "gx", near_pairs)
    if sectors == 2:
        halo = shifted(edges, 1)
    else:
        halo = jnp.stack([shifted(edges[0], 1), shifted(edges[1], sectors - 1)])
    sums, tile, behind = inner_modes(
        place, inv_dx, state, sponge_level, inv_dr, target, forward, edge, near_flux, far_packed, cells
    )
    others = [shifted(sums, by) for by in range(1, sectors)]
    updated, ahead = bulk_update(
        place, inv_dx, state, sponge_level, inv_dr, target, near_flux, halo, behind, cells
    )
    updated = put_filtered(place, cutoff, inverse, inv_dr, tile, ahead, halo, [sums, *others], updated, cells)
    return finish_plane(place, inv_dx, far_flux, updated)


def solution(mesh):
    def whole(state, sponge_level, inv_dx, inv_dr, target, cutoff):
        cells = state.shape[2]
        tables = mode_tables(cells, mesh.shape["az"])
        mapped = jax.shard_map(
            functools.partial(body, *(jnp.asarray(table) for table in tables), cells),
            mesh=mesh,
            in_specs=(P(None, "gx", "az", None), P("gx", "az", None), P("gx"), P(), P(), P()),
            out_specs=P(None, "gx", "az", None),
            check_vma=False,
        )
        return mapped(state, sponge_level, inv_dx, inv_dr, target, cutoff)

    return whole
```

time: 119 us -> 100 us (0.84)
  Pallas kernels: 65.2 us -> 38.1 us
  local copies, waits for them, and re-layouts: 6.27 us -> 12.5 us
  waiting for transfers between devices: 38 us -> 40 us
    pallas_call x2, Pallas kernels: 44.2 us -> 23.8 us  [the longest x1 19.3 us: bulk_update(): pl.pallas_call(functools.partial(update_kernel, cells=cells, chunk=chunk,...]
    unnamed x20, local copies, waits for them, and re-layouts: 3.75 us -> 12.5 us
    pallas_call x1, Pallas kernels: 3.76 us -> 1.02 us  [outer_plane(): pl.pallas_call(outer_kernel, grid_spec=pltpu.PrefetchScalarGridSpec(num_s...]
    pallas_call x1, Pallas kernels: 3.18 us -> 1.23 us  [inner_plane(): pl.pallas_call(inner_kernel, grid_spec=pltpu.PrefetchScalarGridSpec(num_s...]
    squeeze x3 -> x0, local copies, waits for them, and re-layouts: 1.9 us -> none  [body(): pick = lambda table: lax.dynamic_index_in_dim(table, sector, 0, False)]
  transfers between devices with their start and end apart: 5 -> 5, of which waited for: 2 -> 2; matrix products, arithmetic and copies ran while one was open for 2% -> 0% of each run, Pallas kernels for 50% -> 34%
where the time goes in v2:
time: 100 us; the launch traced here: 99 us
  waiting for transfers between devices  40 us (40%)
  Pallas kernels  38.1 us (38%)
  local copies, waits for them, and re-layouts  12.5 us (12%)
  starting transfers between devices  8.11 us (8%)
    ppermute x1, waiting for transfers between devices, body(): far_packed = lax.ppermute(far_packed, 'gx', far_pairs)  28.4 us
    pallas_call x1, Pallas kernels, bulk_update(): pl.pallas_call(functools.partial(update_kernel, cells=cells, chunk=chunk,...  19.3 us
    unnamed x20, local copies, waits for them, and re-layouts  12.5 us
    ppermute x2, waiting for transfers between devices, body(): lax.ppermute(part, 'az', [(i, (i + by) % sectors) for i in range(sectors)])  11.6 us
    pallas_call x1, Pallas kernels, inner_modes(): pl.pallas_call(functools.partial(modes_kernel, cycles=cycles, cells=cells...  9.27 us
    ppermute x1, starting transfers between devices, body(): far_flux = lax.ppermute(far_flux, 'gx', far_pairs)  4.54 us
    pallas_call x1, Pallas kernels, put_filtered(): pl.pallas_call(functools.partial(filter_kernel, cells=cells, cycles=cycle...  4.54 us
    pallas_call x1, Pallas kernels, finish_plane(): pl.pallas_call(finish_kernel, grid_spec=pltpu.PrefetchScalarGridSpec(num_...  2.8 us
  transfers between devices with their start and end apart: 5, of which 2 were waited for; matrix products, arithmetic and copies ran while one was open for 0% of the time, Pallas kernels for 34%

profile of v2, /device:TPU:1, one launch (start us, length us, event | category | flops | bytes accessed | tf_op | source)
XLA Modules:
  0.0 99.0 jit_solution(7038957084330598066)
XLA Ops:
  0.0 0.1 pad_add_fusion.odd_ref.place_ref
  0.1 7.0 %copy-done = f32[5,16,128,512]{3,2,1,0:T(8,128)S(1)} copy-done((f32[5,16,128,512]{3,2,1,0:T(8,128)S(1)}, f32[5,16,128,512]{3,2,1,0:T(8,128)}, u32[]{:S(2)}) %copy-start) | copy-done | bytes 20971544
  7.0 1.2 %inner_plane.1 = (f32[5,128,512]{2,1,0:T(8,128)S(1)}, f32[2,5,16,512]{3,2,1,0:T(8,128)S(1)}) custom-call(s32[2]{0:T(128)S(1)} %pad_add_fusion.odd_ref.place_ref, f32[5,16,128,512]{3,2,1,0:T(8,128)S(1)} %copy-done, f32[5,16,128,512]{3,2,1,0:T(8,128)S(1)} %copy-done, f32[5,16,128,512]{3,2,1,0:T(8,128)S(1)} %copy-done), custom_call_target="tpu_custom_call" | custom-call | tf_op jit(solution)/shard_map/inner_plane/pallas_call | solution.py:145
  8.3 0.0 copy-start.2
  8.3 0.0 copy-start.4
  8.3 0.0 copy-start.5
  8.3 0.0 copy-start.6
  8.3 0.0 copy-start.7
  8.3 0.0 copy-start.8
  8.4 0.1 collective-permute-start.1
  8.5 5.5 %copy-done.1 = f32[5,16,128,512]{3,2,1,0:T(8,128)S(1)} copy-done((f32[5,16,128,512]{3,2,1,0:T(8,128)S(1)}, f32[5,16,128,512]{3,2,1,0:T(8,128)}, u32[]{:S(2)}) %copy-start.1) | copy-done | bytes 20971544
  14.0 1.0 %outer_plane.1 = (f32[5,128,512]{2,1,0:T(8,128)S(1)}, f32[5,32,128]{2,1,0:T(8,128)S(1)}) custom-call(s32[2]{0:T(128)S(1)} %pad_add_fusion.odd_ref.place_ref, f32[5,16,128,512]{3,2,1,0:T(8,128)S(1)} %copy-done.1), custom_call_target="tpu_custom_call" | custom-call | tf_op jit(solution)/shard_map/outer_plane/pallas_call | solution.py:109
  15.0 4.5 %collective-permute-start = (f32[5,128,512]{2,1,0:T(8,128)S(1)}, f32[5,128,512]{2,1,0:T(8,128)S(1)}, u32[]{:S(2)}, u32[]{:S(2)}) collective-permute-start(f32[5,128,512]{2,1,0:T(8,128)S(1)} %get-tuple-element.14), channel_id=1, source_target_pairs={{2,4},{6,8},{10,12},{14,16},{18,20},{22,24},{26,28},{4,2},{8,6},{1... | collective-permute-start | bytes 3932168 | tf_op jit(solution)/shard_map/ppermute | solution.py:650
  19.6 1.9 %collective-permute-start.2 = (f32[5,32,128]{2,1,0:T(8,128)S(1)}, f32[5,32,128]{2,1,0:T(8,128)S(1)}, u32[]{:S(2)}, u32[]{:S(2)}) collective-permute-start(f32[5,32,128]{2,1,0:T(8,128)S(1)} %get-tuple-element.16), channel_id=1, source_target_pairs={{2,4},{6,8},{10,12},{14,16},{18,20},{22,24},{26,28},{4,2},{8,6},{1... | collective-permute-start | bytes 245768 | tf_op jit(solution)/shard_map/ppermute | solution.py:649
  21.5 28.4 %collective-permute-done.2.far_ref = f32[5,32,128]{2,1,0:T(8,128)S(1)} collective-permute-done((f32[5,32,128]{2,1,0:T(8,128)S(1)}, f32[5,32,128]{2,1,0:T(8,128)S(1)}, u32[]{:S(2)}, u32[]{:S(2)}) %collective-permute-start.2) | collective-permute-done | bytes 81952 | tf_op jit(solution)/shard_map/ppermute | solution.py:649
  49.9 0.0 collective-permute-done.1.near_ref
  49.9 9.3 %inner_modes.1 = (f32[1304,128]{1,0:T(8,128)S(1)}, f32[5,16,128,128]{3,2,1,0:T(8,128)S(1)}, f32[5,16,128,128]{3,2,1,0:T(8,128)S(1)}) custom-call(s32[2]{0:T(128)S(1)} %pad_add_fusion.odd_ref.place_ref, f32[16]{0:T(128)S(1)} %copy-done.8, f32[5,16,128,512]{3,2,1,0:T(8,128)} %state_ref.7, f32[5,16,128,512]{3,2,1,0:T(8,128)} %state_ref.7, ...), custom_call_target="tpu_custom_call" | custom-call | tf_op jit(solution)/shard_map/inner_modes/pallas_call | solution.py:291
  59.2 1.3 %collective-permute-start.4 = (f32[1304,128]{1,0:T(8,128)S(1)}, f32[1304,128]{1,0:T(8,128)S(1)}, u32[]{:S(2)}, u32[]{:S(2)}) collective-permute-start(f32[1304,128]{1,0:T(8,128)S(1)} %get-tuple-element.21.refs_0_), channel_id=1, source_target_pairs={{0,1},{1,0},{2,3},{3,2},{4,5},{5,4},{6,7},{7,6},{8,9},{9,8},{10,11... | collective-permute-start | bytes 2002952 | tf_op jit(solution)/shard_map/ppermute | solution.py:646
  60.5 0.3 collective-permute-start.3
  60.8 11.6 %collective-permute-done.3.halo_ref = f32[2,5,16,512]{3,2,1,0:T(8,128)S(1)} collective-permute-done((f32[2,5,16,512]{3,2,1,0:T(8,128)S(1)}, f32[2,5,16,512]{3,2,1,0:T(8,128)S(1)}, u32[]{:S(2)}, u32[]{:S(2)}) %collective-permute-start.3) | collective-permute-done | bytes 327712 | tf_op jit(solution)/shard_map/ppermute | solution.py:646
  72.4 19.3 %bulk_update.1 = (f32[5,16,128,512]{3,2,1,0:T(8,128)}, f32[5,16,128,128]{3,2,1,0:T(8,128)S(1)}) custom-call(s32[2]{0:T(128)S(1)} %pad_add_fusion.odd_ref.place_ref, f32[16]{0:T(128)S(1)} %copy-done.8, f32[1,512]{1,0:T(1,128)S(1)} %bitcast.5, f32[5,512]{1,0:T(8,128)S(1)} %copy-done.6, f32[5,128,512]{2,1,0:T(8,128)S(1)} %collective-permute-done.1.near_ref, ...), custom_call_target="tpu_custom_call" | custom-call | tf_op jit(solution)/shard_map/bulk_update/pallas_call | solution.py:484
  91.7 0.0 collective-permute-done.4.refs_1_
  91.7 4.5 %put_filtered.1.state_ref = f32[5,16,128,512]{3,2,1,0:T(8,128)} custom-call(s32[2]{0:T(128)S(1)} %pad_add_fusion.odd_ref.place_ref, s32[1,32]{1,0:T(1,128)S(1)} %bitcast.7, bf16[2,128,256]{2,1,0:T(8,128)(2,1)S(1)} %copy-done.3, f32[1,512]{1,0:T(1,128)S(1)} %bitcast.6, ...), custom_call_target="tpu_custom_call", output_to_operand_aliasing={{}: (9, {})} | custom-call | tf_op jit(solution)/shard_map/put_filtered/pallas_call | solution.py:559
  96.2 2.8 %finish_plane.1 = f32[5,16,128,512]{3,2,1,0:T(8,128)} custom-call(s32[2]{0:T(128)S(1)} %pad_add_fusion.odd_ref.place_ref, f32[16]{0:T(128)S(1)} %copy-done.8, f32[5,128,512]{2,1,0:T(8,128)S(1)} %collective-permute-done.flux_ref, f32[5,16,128,512]{3,2,1,0:T(8,128)} %put_filtered.1.state_ref), custom_call_target="tpu_custom_call", output_to_operand_aliasing={{}: (3, {})} | custom-call | tf_op jit(solution)/shard_map/finish_plane/pallas_call | solution.py:601
  (13 shorter events, 0.0 us)
Async XLA Ops:
  0.1 7.0 %copy-start = (f32[5,16,128,512]{3,2,1,0:T(8,128)S(1)}, f32[5,16,128,512]{3,2,1,0:T(8,128)}, u32[]{:S(2)}) copy-start(f32[5,16,128,512]{3,2,1,0:T(8,128)} %state_ref.7) | copy-start | bytes 62914564
  7.0 7.0 %copy-start.1 = (f32[5,16,128,512]{3,2,1,0:T(8,128)S(1)}, f32[5,16,128,512]{3,2,1,0:T(8,128)}, u32[]{:S(2)}) copy-start(f32[5,16,128,512]{3,2,1,0:T(8,128)} %state_ref.7) | copy-start | bytes 62914564
  8.3 41.6 %copy-start.2 = (s32[16,128,512]{2,1,0:T(8,128)S(1)}, s32[16,128,512]{2,1,0:T(8,128)}, u32[]{:S(2)}) copy-start(s32[16,128,512]{2,1,0:T(8,128)} %level_ref.3) | copy-start | bytes 12582916
  8.3 41.6 %copy-start.4 = (f32[2,2,64,128]{3,2,1,0:T(8,128)S(1)}, f32[2,2,64,128]{3,2,1,0:T(8,128)}, u32[]{:S(2)}) copy-start(f32[2,2,64,128]{3,2,1,0:T(8,128)} %constant.20.clone.edge_ref) | copy-start | bytes 393220
  8.3 41.6 %copy-start.5 = (bf16[2,128,256]{2,1,0:T(8,128)(2,1)S(1)}, bf16[2,128,256]{2,1,0:T(8,128)(2,1)}, u32[]{:S(2)}) copy-start(bf16[2,128,256]{2,1,0:T(8,128)(2,1)} %constant.19.clone.table_ref) | copy-start | bytes 393220
  8.3 41.6 %copy-start.6 = (f32[5,512]{1,0:T(8,128)S(1)}, f32[5,512]{1,0:T(8,128)}, u32[]{:S(2)}) copy-start(f32[5,512]{1,0:T(8,128)} %target_ref.3) | copy-start | bytes 30724
  8.3 41.6 %copy-start.7 = (f32[512]{0:T(512)S(1)}, f32[512]{0:T(512)}, u32[]{:S(2)}) copy-start(f32[512]{0:T(512)} %param.12) | copy-start | bytes 6148
  8.3 41.6 %copy-start.8 = (f32[16]{0:T(128)S(1)}, f32[16]{0:T(128)}, u32[]{:S(2)}) copy-start(f32[16]{0:T(128)} %scale_ref.5) | copy-start | bytes 196
  8.4 41.6 %collective-permute-start.1 = (f32[5,128,512]{2,1,0:T(8,128)S(1)}, f32[5,128,512]{2,1,0:T(8,128)S(1)}, u32[]{:S(2)}, u32[]{:S(2)}) collective-permute-start(f32[5,128,512]{2,1,0:T(8,128)S(1)} %get-tuple-element.15), channel_id=1, source_target_pairs={{2,0},{0,2},{6,4},{4,6},{10,8},{8,10},{14,12},{12,14},{18,16},{16,... | collective-permute-start | bytes 3932168 | tf_op jit(solution)/shard_map/ppermute | solution.py:652
  15.0 81.2 %collective-permute-start = (f32[5,128,512]{2,1,0:T(8,128)S(1)}, f32[5,128,512]{2,1,0:T(8,128)S(1)}, u32[]{:S(2)}, u32[]{:S(2)}) collective-permute-start(f32[5,128,512]{2,1,0:T(8,128)S(1)} %get-tuple-element.14), channel_id=1, source_target_pairs={{2,4},{6,8},{10,12},{14,16},{18,20},{22,24},{26,28},{4,2},{8,6},{1... | collective-permute-start | bytes 3932168 | tf_op jit(solution)/shard_map/ppermute | solution.py:650
  19.6 30.3 %collective-permute-start.2 = (f32[5,32,128]{2,1,0:T(8,128)S(1)}, f32[5,32,128]{2,1,0:T(8,128)S(1)}, u32[]{:S(2)}, u32[]{:S(2)}) collective-permute-start(f32[5,32,128]{2,1,0:T(8,128)S(1)} %get-tuple-element.16), channel_id=1, source_target_pairs={{2,4},{6,8},{10,12},{14,16},{18,20},{22,24},{26,28},{4,2},{8,6},{1... | collective-permute-start | bytes 245768 | tf_op jit(solution)/shard_map/ppermute | solution.py:649
  59.2 32.4 %collective-permute-start.4 = (f32[1304,128]{1,0:T(8,128)S(1)}, f32[1304,128]{1,0:T(8,128)S(1)}, u32[]{:S(2)}, u32[]{:S(2)}) collective-permute-start(f32[1304,128]{1,0:T(8,128)S(1)} %get-tuple-element.21.refs_0_), channel_id=1, source_target_pairs={{0,1},{1,0},{2,3},{3,2},{4,5},{5,4},{6,7},{7,6},{8,9},{9,8},{10,11... | collective-permute-start | bytes 2002952 | tf_op jit(solution)/shard_map/ppermute | solution.py:646
  60.5 11.9 %collective-permute-start.3 = (f32[2,5,16,512]{3,2,1,0:T(8,128)S(1)}, f32[2,5,16,512]{3,2,1,0:T(8,128)S(1)}, u32[]{:S(2)}, u32[]{:S(2)}) collective-permute-start(f32[2,5,16,512]{3,2,1,0:T(8,128)S(1)} %get-tuple-element.18), channel_id=1, source_target_pairs={{0,1},{1,0},{2,3},{3,2},{4,5},{5,4},{6,7},{7,6},{8,9},{9,8},{10,11... | collective-permute-start | bytes 983048 | tf_op jit(solution)/shard_map/ppermute | solution.py:646
  72.4 19.3 %copy-start.3 = (bf16[2,128,256]{2,1,0:T(8,128)(2,1)S(1)}, bf16[2,128,256]{2,1,0:T(8,128)(2,1)}, u32[]{:S(2)}) copy-start(bf16[2,128,256]{2,1,0:T(8,128)(2,1)} %constant.21.clone.table_ref) | copy-start | bytes 393220
  72.4 19.3 %copy-start.9 = (s32[32]{0:T(128)S(1)}, s32[32]{0:T(128)}, u32[]{:S(2)}) copy-start(s32[32]{0:T(128)} %param.14) | copy-start | bytes 388

commit v3 on v2

--- a/solution.py
+++ b/solution.py
@@ -89,21 +89,66 @@
     return result
 
 
-def outer_kernel(odd_ref, state_ref, flux_ref, packed_ref):
+def edge_kernel(place_ref, state_ref, first_ref, last_ref, near_ref, edge_ref, packed_ref, flux_ref):
     step = pl.program_id(0)
     rows = packed_ref.shape[1]
     blocks = state_ref.shape[2] // rows
+    low = swirl_flux([last_ref[f, :, 7, :] for f in range(5)])
+    high = swirl_flux([first_ref[f, :, 0, :] for f in range(5)])
+    planes = pl.ds(pl.multiple_of(step * 8, 8), 8)
     flux = axial_flux([state_ref[f, 0] for f in range(5)])
     lane = lax.broadcasted_iota(jnp.int32, packed_ref.shape[1:], 1)
     for f in range(5):
-        flux_ref[f, pl.ds(pl.multiple_of(step * state_ref.shape[2], 8), state_ref.shape[2])] = flux[f]
+        edge_ref[0, f, planes] = low[f]
+        edge_ref[1, f, planes] = high[f]
         for i in range(blocks):
             block = step * blocks + i
-            turned = pltpu.roll(flux[f][i * rows : (i + 1) * rows, :LANES], block * CYCLE, 1)
+            turned = pltpu.roll(flux[f][i * rows : (i + 1) * rows], block * CYCLE, 1)
             packed_ref[f] = jnp.where(lane // CYCLE == block, turned, packed_ref[f])
-
-
-def outer_plane(odd, state):
+    flux = axial_flux([near_ref[f, 0] for f in range(5)])
+    count = near_ref.shape[2]
+    for f in range(5):
+        flux_ref[f, pl.ds(pl.multiple_of(step * count, 8), count)] = flux[f]
+
+
+def edge_cells(place, state):
+    _, planes, columns, cycles = state.shape
+    steps = planes // 8
+    return pl.pallas_call(
+        edge_kernel,
+        grid_spec=pltpu.PrefetchScalarGridSpec(
+            num_scalar_prefetch=1,
+            grid=(steps,),
+            in_specs=[
+                pl.BlockSpec((5, 1, columns // steps, LANES), lambda b, place: (0, place[0] * (planes - 1), b, 0)),
+                pl.BlockSpec((5, 8, 8, cycles), lambda b, place: (0, b, 0, 0)),
+                pl.BlockSpec((5, 8, 8, cycles), lambda b, place: (0, b, columns // 8 - 1, 0)),
+                pl.BlockSpec(
+                    (5, 1, columns // steps, cycles), lambda b, place: (0, (1 - place[0]) * (planes - 1), b, 0)
+                ),
+            ],
+            out_specs=[VMEM_SPEC, VMEM_SPEC, VMEM_SPEC],
+        ),
+        out_shape=[
+            pltpu.VMEM((2, 5, planes, cycles), jnp.float32),
+            pltpu.VMEM((5, columns // PACK, LANES), jnp.float32),
+            pltpu.VMEM((5, columns, cycles), jnp.float32),
+        ],
+        compiler_params=params(1, 8),
+        name="edge_cells",
+    )(place, state, state, state, state)
+
+
+def outer_kernel(place_ref, state_ref, *refs):
+    flux_ref = refs[-1]
+    count = state_ref.shape[2]
+    rows = pl.ds(pl.multiple_of(pl.program_id(0) * count, 8), count)
+    flux = axial_flux([state_ref[f, 0] for f in range(5)])
+    for f in range(5):
+        flux_ref[f, rows] = flux[f]
+
+
+def outer_plane(place, state, after):
     _, planes, columns, cycles = state.shape
     steps = 2
     return pl.pallas_call(
@@ -112,69 +157,29 @@
             num_scalar_prefetch=1,
             grid=(steps,),
             in_specs=[
-                pl.BlockSpec((5, 1, columns // steps, cycles), lambda b, odd: (0, odd[0] * (planes - 1), b, 0))
-            ],
-            out_specs=[VMEM_SPEC, VMEM_SPEC],
+                pl.BlockSpec((5, 1, columns // steps, cycles), lambda b, place: (0, place[0] * (planes - 1), b, 0)),
+            ]
+            + [VMEM_SPEC] * len(after),
+            out_specs=VMEM_SPEC,
         ),
-        out_shape=[
-            pltpu.VMEM((5, columns, cycles), jnp.float32),
-            pltpu.VMEM((5, columns // PACK, LANES), jnp.float32),
-        ],
+        out_shape=pltpu.VMEM((5, columns, cycles), jnp.float32),
         compiler_params=params(1, 8),
         name="outer_plane",
-    )(odd, state)
-
-
-def inner_kernel(odd_ref, state_ref, first_ref, last_ref, flux_ref, edge_ref):
-    step = pl.program_id(0)
-    rows = state_ref.shape[2]
-    flux = axial_flux([state_ref[f, 0] for f in range(5)])
-    for f in range(5):
-        flux_ref[f, pl.ds(pl.multiple_of(step * rows, 8), rows)] = flux[f]
-    low = swirl_flux([last_ref[f, :, 7, :] for f in range(5)])
-    high = swirl_flux([first_ref[f, :, 0, :] for f in range(5)])
-    planes = pl.ds(pl.multiple_of(step * 8, 8), 8)
-    for f in range(5):
-        edge_ref[0, f, planes] = low[f]
-        edge_ref[1, f, planes] = high[f]
-
-
-def inner_plane(odd, state):
-    _, planes, columns, cycles = state.shape
-    steps = planes // 8
-    return pl.pallas_call(
-        inner_kernel,
-        grid_spec=pltpu.PrefetchScalarGridSpec(
-            num_scalar_prefetch=1,
-            grid=(steps,),
-            in_specs=[
-                pl.BlockSpec((5, 1, columns // steps, cycles), lambda b, odd: (0, (1 - odd[0]) * (planes - 1), b, 0)),
-                pl.BlockSpec((5, 8, 8, cycles), lambda b, odd: (0, b, 0, 0)),
-                pl.BlockSpec((5, 8, 8, cycles), lambda b, odd: (0, b, columns // 8 - 1, 0)),
-            ],
-            out_specs=[VMEM_SPEC, VMEM_SPEC],
-        ),
-        out_shape=[
-            pltpu.VMEM((5, columns, cycles), jnp.float32),
-            pltpu.VMEM((2, 5, planes, cycles), jnp.float32),
-        ],
-        compiler_params=params(1, 12),
-        name="inner_plane",
-    )(odd, state, state, state)
+    )(place, state, *(resident(part) for part in after))
 
 
 def modes_kernel(
     place_ref, scale_ref, state_ref, before_ref, after_ref, level_ref, inv_dr_ref, target_ref, table_ref, edge_ref,
-    near_ref, far_ref, sums_ref, tile_ref, behind_ref, rows_ref, axial_ref, swirl_ref, base_ref, split_ref,
-    *, cycles, cells, chunk,
+    *refs, cycles, cells, chunk, pick, steps, outside,
 ):
-    step = pl.program_id(0)
-    steps = pl.num_programs(0)
+    if outside:
+        near_ref, far_ref = refs[:2]
+    sums_ref, tile_ref, behind_ref, rows_ref, axial_ref, swirl_ref, base_ref, split_ref = refs[-8:]
+    step = pick(pl.program_id(0))
     columns = state_ref.shape[2]
     odd = place_ref[0]
-    far_rows = far_ref.shape[1]
-
-    @pl.when(step == 0)
+
+    @pl.when(pl.program_id(0) == 0)
     def _():
         fill_rows(rows_ref, inv_dr_ref[...], 0, cycles, cells)
         for f in range(5):
@@ -186,6 +191,7 @@
         return [ref[f, plane, pl.ds(start, chunk), :] for f in range(5)]
 
     def halo(slot, use_near):
+        far_rows = far_ref.shape[1]
         for f in range(5):
             for b in range(PACK):
                 away = far_ref[f]
@@ -206,10 +212,14 @@
         lax.fori_loop(0, columns // chunk, one, 0, unroll=True)
 
     lane = lax.broadcasted_iota(jnp.int32, (chunk, LANES), 1)
-    pl.when(step == 0)(lambda: halo(0, odd == 1))
-    pl.when(step > 0)(lambda: neighbour(0, before_ref))
-    pl.when(step == steps - 1)(lambda: halo(PACK + 1, odd == 0))
-    pl.when(step < steps - 1)(lambda: neighbour(PACK + 1, after_ref))
+    if outside:
+        pl.when(step == 0)(lambda: halo(0, odd == 1))
+        pl.when(step > 0)(lambda: neighbour(0, before_ref))
+        pl.when(step == steps - 1)(lambda: halo(PACK + 1, odd == 0))
+        pl.when(step < steps - 1)(lambda: neighbour(PACK + 1, after_ref))
+    else:
+        neighbour(0, before_ref)
+        neighbour(PACK + 1, after_ref)
 
     def wide(row):
         return jnp.broadcast_to(row[None], (chunk // 8, 8, LANES)).reshape(chunk, LANES)
@@ -282,32 +292,37 @@
     return groups * half + -(-groups // 8) * 8
 
 
-def inner_modes(place, scale, state, sponge, inv_dr, target, table, edge, near, far, cells):
+def inner_modes(place, scale, state, sponge, inv_dr, target, table, edge, cells, done=(), near=None, far=None):
     _, planes, columns, cycles = state.shape
     half = table.shape[1] // 2
     chunk = min(32, columns)
+    steps = planes // PACK
+    outside = bool(done)
+    pick = (lambda g: g * (steps - 1)) if outside else (lambda g: g + 1)
     whole = lambda *shape: pl.BlockSpec(shape, lambda g, place: (0,) * len(shape))
     tile = pltpu.VMEM((5, planes, columns, LANES), jnp.float32)
+    extra = [resident(part) for part in ((near, far) + tuple(done) if outside else ())]
+    before = lambda g, place: (0, jnp.maximum(pick(g) * PACK - 1, 0), 0, 0)
+    behind = lambda g, place: (0, jnp.minimum(pick(g) * PACK + PACK, planes - 1), 0, 0)
     return pl.pallas_call(
-        functools.partial(modes_kernel, cycles=cycles, cells=cells, chunk=chunk),
+        functools.partial(
+            modes_kernel, cycles=cycles, cells=cells, chunk=chunk, pick=pick, steps=steps, outside=outside
+        ),
         grid_spec=pltpu.PrefetchScalarGridSpec(
             num_scalar_prefetch=1,
-            grid=(planes // PACK,),
+            grid=(2 if outside else steps - 2,),
             in_specs=[
                 SMEM_SPEC,
-                pl.BlockSpec((5, PACK, columns, LANES), lambda g, place: (0, g, 0, 0)),
-                pl.BlockSpec((5, 1, columns, LANES), lambda g, place: (0, jnp.maximum(g * PACK - 1, 0), 0, 0)),
-                pl.BlockSpec(
-                    (5, 1, columns, LANES), lambda g, place: (0, jnp.minimum(g * PACK + PACK, planes - 1), 0, 0)
-                ),
-                pl.BlockSpec((PACK, columns, LANES), lambda g, place: (g, 0, 0)),
+                pl.BlockSpec((5, PACK, columns, LANES), lambda g, place: (0, pick(g), 0, 0)),
+                pl.BlockSpec((5, 1, columns, LANES), before),
+                pl.BlockSpec((5, 1, columns, LANES), behind),
+                pl.BlockSpec((PACK, columns, LANES), lambda g, place: (pick(g), 0, 0)),
                 whole(1, LANES),
                 whole(5, LANES),
                 pl.BlockSpec((1,) + table.shape[1:], lambda g, place: (place[1], 0, 0)),
                 pl.BlockSpec((1,) + edge.shape[1:], lambda g, place: (place[1], 0, 0, 0)),
-                VMEM_SPEC,
-                VMEM_SPEC,
-            ],
+            ]
+            + [VMEM_SPEC] * len(extra),
             out_specs=[VMEM_SPEC, VMEM_SPEC, VMEM_SPEC],
             scratch_shapes=[
                 pltpu.VMEM((3, 8, LANES), jnp.float32),
@@ -318,9 +333,10 @@
             ],
         ),
         out_shape=[pltpu.VMEM((mode_rows(planes, half), LANES), jnp.float32), tile, tile],
+        input_output_aliases={12 + k: k for k in range(3)} if outside else {},
         compiler_params=params(1, 20),
-        name="inner_modes",
-    )(place, scale, state, state, state, sponge, inv_dr, target, table, edge, resident(near), resident(far))
+        name="end_modes" if outside else "middle_modes",
+    )(place, scale, state, state, state, sponge, inv_dr, target, table, edge, *extra)
 
 
 IN_SLOTS = 3
@@ -329,7 +345,7 @@
 
 def update_kernel(
     place_ref, scale_ref, inv_dr_ref, target_ref, near_ref, halo_ref, behind_ref, state_ref, level_ref,
-    out_ref, ahead_ref, rows_ref, fields_ref, levels_ref, result_ref, axial_even_ref, axial_odd_ref, swirl_even_ref,
+    out_ref, ahead_ref, kept_ref, rows_ref, fields_ref, levels_ref, result_ref, axial_even_ref, axial_odd_ref, swirl_even_ref,
     swirl_odd_ref, base_ref, field_sem, level_sem, result_sem, *, cells, chunk, unroll,
 ):
     axial_refs = (axial_even_ref, axial_odd_ref)
@@ -350,6 +366,10 @@
     def store(plane):
         slot = lax.rem(plane, OUT_SLOTS)
         return pltpu.make_async_copy(result_ref.at[slot], out_ref.at[:, plane, :, rest], result_sem.at[slot])
+
+    def keep(plane):
+        slot = lax.rem(plane, OUT_SLOTS)
+        return pltpu.make_async_copy(result_ref.at[slot], kept_ref, result_sem.at[slot])
 
     for plane in range(IN_SLOTS):
         for copy in fetch(plane):
@@ -449,7 +469,9 @@
             return 0
 
         lax.fori_loop(0, columns // chunk, step, 0, unroll=unroll)
-        pl.when(plane > 0)(lambda: store(plane - 1).start())
+        outer = jnp.logical_and(plane == 1, odd == 0)
+        pl.when(outer)(lambda: keep(plane - 1).start())
+        pl.when(jnp.logical_and(plane > 0, jnp.logical_not(outer)))(lambda: store(plane - 1).start())
 
         @pl.when(plane + IN_SLOTS < planes)
         def _():
@@ -472,7 +494,8 @@
         return 0
 
     lax.fori_loop(0, columns // chunk, last, 0)
-    store(planes - 1).start()
+    pl.when(odd == 0)(lambda: store(planes - 1).start())
+    pl.when(odd == 1)(lambda: keep(planes - 1).start())
     for plane in range(planes - OUT_SLOTS, planes):
         store(plane).wait()
 
@@ -484,7 +507,7 @@
     return pl.pallas_call(
         functools.partial(update_kernel, cells=cells, chunk=chunk, unroll=unroll),
         in_specs=[SMEM_SPEC, SMEM_SPEC, VMEM_SPEC, VMEM_SPEC, VMEM_SPEC, VMEM_SPEC, VMEM_SPEC, HBM_SPEC, HBM_SPEC],
-        out_specs=[HBM_SPEC, VMEM_SPEC],
+        out_specs=[HBM_SPEC, VMEM_SPEC, VMEM_SPEC],
         scratch_shapes=[
             pltpu.VMEM((3, 8, width), jnp.float32),
             pltpu.VMEM((IN_SLOTS, 5, columns, width), jnp.float32),
@@ -502,6 +525,7 @@
         out_shape=[
             jax.ShapeDtypeStruct(state.shape, jnp.float32),
             pltpu.VMEM((5, planes, columns, LANES), jnp.float32),
+            pltpu.VMEM((5, columns, width), jnp.float32),
         ],
         compiler_params=pltpu.CompilerParams(vmem_limit_bytes=20 * MIB),
         name="bulk_update",
@@ -511,7 +535,7 @@
 def filter_kernel(
     place_ref, cutoff_ref, table_ref, inv_dr_ref, tile_ref, ahead_ref, halo_ref, *refs, cells, cycles
 ):
-    *sums, state_ref, out_ref, split_ref = refs
+    *sums, state_ref, out_ref, kept_ref, split_ref = refs
     step = pl.program_id(0)
     steps = pl.num_programs(0)
     half = table_ref.shape[2] // 4
@@ -553,6 +577,14 @@
             out_ref[f, i, 0:1] = out_ref[f, i, 0:1] + around * low
             out_ref[f, i, columns - 1 : columns] = out_ref[f, i, columns - 1 : columns] - around * high
 
+    def keep(i):
+        for f in range(5):
+            kept_ref[f] = out_ref[f, i]
+
+    odd = place_ref[0]
+    pl.when(jnp.logical_and(step == 0, odd == 0))(lambda: keep(0))
+    pl.when(jnp.logical_and(step == steps - 1, odd == 1))(lambda: keep(PACK - 1))
+
 
 def put_filtered(place, cutoff, table, inv_dr, tile, ahead, halo, sums, updated, cells):
     _, planes, columns, cycles = updated.shape
@@ -571,10 +603,13 @@
             ]
             + [VMEM_SPEC] * len(sums)
             + [HBM_SPEC],
-            out_specs=pl.BlockSpec((5, PACK, columns, LANES), lambda g, place: (0, g, 0, 0)),
+            out_specs=[pl.BlockSpec((5, PACK, columns, LANES), lambda g, place: (0, g, 0, 0)), VMEM_SPEC],
             scratch_shapes=[pltpu.VMEM((5, table.shape[2], LANES), jnp.bfloat16)],
         ),
-        out_shape=jax.ShapeDtypeStruct(updated.shape, jnp.float32),
+        out_shape=[
+            jax.ShapeDtypeStruct(updated.shape, jnp.float32),
+            pltpu.VMEM((5, columns, LANES), jnp.float32),
+        ],
         input_output_aliases={7 + len(sums): 0},
         compiler_params=params(1, 12),
         name="put_filtered",
@@ -582,35 +617,38 @@
       *(resident(part) for part in sums), updated)
 
 
-def finish_kernel(place_ref, scale_ref, flux_ref, state_ref, out_ref):
+def finish_kernel(place_ref, scale_ref, flux_ref, first_ref, rest_ref, state_ref, out_ref):
     odd = place_ref[0]
     planes = scale_ref.shape[0]
     rows = out_ref.shape[2]
     factor = (0.5 * time_step) * scale_ref[odd * (planes - 1)]
     factor = jnp.where(odd == 1, -factor, factor)
-    lane = lax.broadcasted_iota(jnp.int32, out_ref.shape[2:], 1)
-    start = pl.multiple_of(pl.program_id(0) * rows, 8)
+    lane = lax.broadcasted_iota(jnp.int32, (rows, LANES), 1)
+    cells = pl.ds(pl.multiple_of(pl.program_id(0) * rows, 8), rows)
     for f in range(5):
-        out_ref[f, 0] = state_ref[f, 0] + jnp.where(lane < CYCLE, 0.0, factor * flux_ref[f, pl.ds(start, rows)])
-
-
-def finish_plane(place, scale, flux, updated):
+        flux = factor * flux_ref[f, cells]
+        out_ref[f, 0, :, :LANES] = first_ref[f, cells] + jnp.where(lane < CYCLE, 0.0, flux[:, :LANES])
+        out_ref[f, 0, :, LANES:] = rest_ref[f, cells] + flux[:, LANES:]
+
+
+def finish_plane(place, scale, flux, first, rest, updated):
     _, planes, columns, cycles = updated.shape
     steps = 2
-    block = pl.BlockSpec((5, 1, columns // steps, cycles), lambda b, place: (0, place[0] * (planes - 1), b, 0))
     return pl.pallas_call(
         finish_kernel,
         grid_spec=pltpu.PrefetchScalarGridSpec(
             num_scalar_prefetch=1,
             grid=(steps,),
-            in_specs=[SMEM_SPEC, VMEM_SPEC, block],
-            out_specs=block,
+            in_specs=[SMEM_SPEC, VMEM_SPEC, VMEM_SPEC, VMEM_SPEC, HBM_SPEC],
+            out_specs=pl.BlockSpec(
+                (5, 1, columns // steps, cycles), lambda b, place: (0, place[0] * (planes - 1), b, 0)
+            ),
         ),
         out_shape=jax.ShapeDtypeStruct(updated.shape, jnp.float32),
-        input_output_aliases={3: 0},
-        compiler_params=params(1, 12),
+        input_output_aliases={5: 0},
+        compiler_params=params(1, 8),
         name="finish_plane",
-    )(place, scale, resident(flux), updated)
+    )(place, scale, resident(flux), resident(first), resident(rest), updated)
 
 
 def mode_tables(cells, sectors):
@@ -645,24 +683,26 @@
     far_pairs = [(i, i + 1) for i in range(1, rows - 1, 2)] + [(i + 1, i) for i in range(1, rows - 1, 2)]
     shifted = lambda part, by: lax.ppermute(part, "az", [(i, (i + by) % sectors) for i in range(sectors)])
 
-    far_flux, far_packed = outer_plane(place, state)
-    far_packed = lax.ppermute(far_packed, "gx", far_pairs)
-    far_flux = lax.ppermute(far_flux, "gx", far_pairs)
-    near_flux, edges = inner_plane(place, state)
+    state = pltpu.with_memory_space_constraint(state, pltpu.HBM)
+    edges, packed, near_flux = edge_cells(place, state)
+    far_packed = lax.ppermute(packed, "gx", far_pairs)
     near_flux = lax.ppermute(near_flux, "gx", near_pairs)
     if sectors == 2:
         halo = shifted(edges, 1)
     else:
         halo = jnp.stack([shifted(edges[0], 1), shifted(edges[1], sectors - 1)])
-    sums, tile, behind = inner_modes(
-        place, inv_dx, state, sponge_level, inv_dr, target, forward, edge, near_flux, far_packed, cells
+    modes = functools.partial(
+        inner_modes, place, inv_dx, state, sponge_level, inv_dr, target, forward, edge, cells
     )
+    middle = modes()
+    far_flux = lax.ppermute(outer_plane(place, state, [far_packed, halo, middle[0]]), "gx", far_pairs)
+    sums, tile, behind = modes(done=middle, near=near_flux, far=far_packed)
     others = [shifted(sums, by) for by in range(1, sectors)]
-    updated, ahead = bulk_update(
+    updated, ahead, rest = bulk_update(
         place, inv_dx, state, sponge_level, inv_dr, target, near_flux, halo, behind, cells
     )
-    updated = put_filtered(place, cutoff, inverse, inv_dr, tile, ahead, halo, [sums, *others], updated, cells)
-    return finish_plane(place, inv_dx, far_flux, updated)
+    updated, first = put_filtered(place, cutoff, inverse, inv_dr, tile, ahead, halo, [sums, *others], updated, cells)
+    return finish_plane(place, inv_dx, far_flux, first, rest, updated)
 
 
 def solution(mesh):

time: 100 us -> 53.1 us (0.53)
  waiting for transfers between devices: 40 us -> 0.01 us
  local copies, waits for them, and re-layouts: 12.5 us -> 0.03 us
  Pallas kernels: 38.1 us -> 42.3 us
  starting transfers between devices: 8.11 us -> 10.4 us
    ppermute x2, waiting for transfers between devices: 28.4 us -> 0.01 us  [the longest x1 0.01 us: body(): far_packed = lax.ppermute(packed, 'gx', far_pairs)]
    unnamed x20 -> x16, local copies, waits for them, and re-layouts: 12.5 us -> 0.03 us
    ppermute x2, waiting for transfers between devices: 11.6 us -> 0.01 us  [body(): lax.ppermute(part, 'az', [(i, (i + by) % sectors) for i in range(sectors)])]
    ppermute x2, starting transfers between devices: 1.53 us -> 3.95 us  [body(): lax.ppermute(part, 'az', [(i, (i + by) % sectors) for i in range(sectors)])]
    pallas_call x1, Pallas kernels: 1.23 us -> 3.39 us  [edge_cells(): pl.pallas_call(edge_kernel, grid_spec=pltpu.PrefetchScalarGridSpec(num_sc...]
    pallas_call x1 -> x2, Pallas kernels: 9.27 us -> 11.3 us  [inner_modes(): pl.pallas_call(functools.partial(modes_kernel, cycles=cycles, cells=cells...]
  transfers between devices with their start and end apart: 5 -> 5, of which waited for: 2 -> 0; matrix products, arithmetic and copies ran while one was open for 0% -> 0% of each run, Pallas kernels for 34% -> 69%
where the time goes in v3:
time: 53.1 us; the launch traced here: 53 us
  Pallas kernels  42.3 us (80%)
  starting transfers between devices  10.4 us (20%)
    pallas_call x1, Pallas kernels, bulk_update(): pl.pallas_call(functools.partial(update_kernel, cells=cells, chunk=chunk,...  18.9 us
    pallas_call x2, Pallas kernels, inner_modes(): pl.pallas_call(functools.partial(modes_kernel, cycles=cycles, cells=cells...  11.3 us
    pallas_call x1, Pallas kernels, put_filtered(): pl.pallas_call(functools.partial(filter_kernel, cells=cells, cycles=cycle...  4.53 us
    ppermute x2, starting transfers between devices, body(): lax.ppermute(part, 'az', [(i, (i + by) % sectors) for i in range(sectors)])  3.95 us
    pallas_call x1, Pallas kernels, edge_cells(): pl.pallas_call(edge_kernel, grid_spec=pltpu.PrefetchScalarGridSpec(num_sc...  3.39 us
    ppermute x1, starting transfers between devices, body(): far_packed = lax.ppermute(packed, 'gx', far_pairs)  3.37 us
    ppermute x1, starting transfers between devices, body(): lax.ppermute(outer_plane(place, state, [far_packed, halo, middle[0]]), 'g...  2.96 us
    pallas_call x1, Pallas kernels, finish_plane(): pl.pallas_call(finish_kernel, grid_spec=pltpu.PrefetchScalarGridSpec(num_...  2.25 us
  transfers between devices with their start and end apart: 5, of which 0 were waited for; matrix products, arithmetic and copies ran while one was open for 0% of the time, Pallas kernels for 69%

profile of v3, /device:TPU:1, one launch (start us, length us, event | category | flops | bytes accessed | tf_op | source)
XLA Modules:
  0.0 53.0 jit_solution(4536210752162845900)
XLA Ops:
  0.0 0.1 pad_add_fusion.place_ref
  0.1 0.0 copy-start.5
  0.1 0.0 copy-start.6
  0.1 3.4 %edge_cells.1 = (f32[2,5,16,512]{3,2,1,0:T(8,128)S(1)}, f32[5,32,128]{2,1,0:T(8,128)S(1)}, f32[5,128,512]{2,1,0:T(8,128)S(1)}) custom-call(s32[2]{0:T(128)S(1)} %pad_add_fusion.place_ref, f32[5,16,128,512]{3,2,1,0:T(8,128)} %state_ref.9, f32[5,16,128,512]{3,2,1,0:T(8,128)} %state_ref.9, f32[5,16,128,512]{3,2,1,0:T(8,128)} %state_ref.9, ...), custom_call_target="tpu_custom_call" | custom-call | tf_op jit(solution)/shard_map/edge_cells/pallas_call | solution.py:117
  3.5 0.1 collective-permute-start.3
  3.6 2.7 %collective-permute-start.1 = (f32[2,5,16,512]{3,2,1,0:T(8,128)S(1)}, f32[2,5,16,512]{3,2,1,0:T(8,128)S(1)}, u32[]{:S(2)}, u32[]{:S(2)}) collective-permute-start(f32[2,5,16,512]{3,2,1,0:T(8,128)S(1)} %get-tuple-element.20), channel_id=1, source_target_pairs={{0,1},{1,0},{2,3},{3,2},{4,5},{5,4},{6,7},{7,6},{8,9},{9,8},{10,11... | collective-permute-start | bytes 983048 | tf_op jit(solution)/shard_map/ppermute | solution.py:684
  6.3 3.4 %collective-permute-start = (f32[5,32,128]{2,1,0:T(8,128)S(1)}, f32[5,32,128]{2,1,0:T(8,128)S(1)}, u32[]{:S(2)}, u32[]{:S(2)}) collective-permute-start(f32[5,32,128]{2,1,0:T(8,128)S(1)} %get-tuple-element.19), channel_id=1, source_target_pairs={{2,4},{6,8},{10,12},{14,16},{18,20},{22,24},{26,28},{4,2},{8,6},{1... | collective-permute-start | bytes 245768 | tf_op jit(solution)/shard_map/ppermute | solution.py:688
  9.7 0.0 copy-done
  9.7 0.0 copy-done.1
  9.7 0.0 copy-done.2
  9.7 0.0 copy-done.3
  9.7 5.5 %middle_modes.1 = (f32[1304,128]{1,0:T(8,128)S(1)}, f32[5,16,128,128]{3,2,1,0:T(8,128)S(1)}, f32[5,16,128,128]{3,2,1,0:T(8,128)S(1)}) custom-call(s32[2]{0:T(128)S(1)} %pad_add_fusion.place_ref, f32[16]{0:T(128)S(1)} %copy-done.6, f32[5,16,128,512]{3,2,1,0:T(8,128)} %state_ref.9, f32[5,16,128,512]{3,2,1,0:T(8,128)} %state_ref.9, ...), custom_call_target="tpu_custom_call" | custom-call | tf_op jit(solution)/shard_map/middle_modes/pallas_call | solution.py:307
  15.3 0.0 collective-permute-done.refs_0_.refs_1_
  15.3 0.0 collective-permute-done.1.refs_1_.halo_ref
  15.3 2.0 %outer_plane.1 = f32[5,128,512]{2,1,0:T(8,128)S(1)} custom-call(s32[2]{0:T(128)S(1)} %pad_add_fusion.place_ref, f32[5,16,128,512]{3,2,1,0:T(8,128)} %state_ref.9, f32[5,32,128]{2,1,0:T(8,128)S(1)} %collective-permute-done.refs_0_.refs_1_, f32[2,5,16,512]{3,2,1,0:T(8,128)S(1)} %collective-permute-done.1.refs_1_.halo_ref, ...), custom_call_target="tpu_custom_call" | custom-call | tf_op jit(solution)/shard_map/outer_plane/pallas_call | solution.py:154
  17.3 3.0 %collective-permute-start.2 = (f32[5,128,512]{2,1,0:T(8,128)S(1)}, f32[5,128,512]{2,1,0:T(8,128)S(1)}, u32[]{:S(2)}, u32[]{:S(2)}) collective-permute-start(f32[5,128,512]{2,1,0:T(8,128)S(1)} %outer_plane.1), channel_id=1, source_target_pairs={{2,4},{6,8},{10,12},{14,16},{18,20},{22,24},{26,28},{4,2},{8,6},{1... | collective-permute-start | bytes 3932168 | tf_op jit(solution)/shard_map/ppermute | solution.py:698
  20.2 0.0 collective-permute-done.3.refs_0_.near_ref
  20.2 5.7 %end_modes.1 = (f32[1304,128]{1,0:T(8,128)S(1)}, f32[5,16,128,128]{3,2,1,0:T(8,128)S(1)}, f32[5,16,128,128]{3,2,1,0:T(8,128)S(1)}) custom-call(s32[2]{0:T(128)S(1)} %pad_add_fusion.place_ref, f32[16]{0:T(128)S(1)} %copy-done.6, f32[5,16,128,512]{3,2,1,0:T(8,128)} %state_ref.9, ...), custom_call_target="tpu_custom_call", output_to_operand_aliasing={{0}: (12, {}), {1}: (13, {}), {2}: (14, {})} | custom-call | tf_op jit(solution)/shard_map/end_modes/pallas_call | solution.py:307
  26.0 1.3 %collective-permute-start.4 = (f32[1304,128]{1,0:T(8,128)S(1)}, f32[1304,128]{1,0:T(8,128)S(1)}, u32[]{:S(2)}, u32[]{:S(2)}) collective-permute-start(f32[1304,128]{1,0:T(8,128)S(1)} %get-tuple-element.28.refs_0_), channel_id=1, source_target_pairs={{0,1},{1,0},{2,3},{3,2},{4,5},{5,4},{6,7},{7,6},{8,9},{9,8},{10,11... | collective-permute-start | bytes 2002952 | tf_op jit(solution)/shard_map/ppermute | solution.py:684
  27.3 18.9 %bulk_update.1 = (f32[5,16,128,512]{3,2,1,0:T(8,128)}, f32[5,16,128,128]{3,2,1,0:T(8,128)S(1)}, f32[5,128,384]{2,1,0:T(8,128)S(1)}) custom-call(s32[2]{0:T(128)S(1)} %pad_add_fusion.place_ref, f32[16]{0:T(128)S(1)} %copy-done.6, f32[1,512]{1,0:T(1,128)S(1)} %bitcast.6, f32[5,512]{1,0:T(8,128)S(1)} %copy-done.3, ...), custom_call_target="tpu_custom_call" | custom-call | tf_op jit(solution)/shard_map/bulk_update/pallas_call | solution.py:507
  46.2 0.0 collective-permute-done.4.refs_1_
  46.2 4.5 %put_filtered.1 = (f32[5,16,128,512]{3,2,1,0:T(8,128)}, f32[5,128,128]{2,1,0:T(8,128)S(1)}) custom-call(s32[2]{0:T(128)S(1)} %pad_add_fusion.place_ref, s32[1,32]{1,0:T(1,128)S(1)} %bitcast.8, bf16[2,128,256]{2,1,0:T(8,128)(2,1)S(1)} %copy-done.4, f32[1,512]{1,0:T(1,128)S(1)} %bitcast.7, ...), custom_call_target="tpu_custom_call", output_to_operand_aliasing={{0}: (9, {})} | custom-call | tf_op jit(solution)/shard_map/put_filtered/pallas_call | solution.py:591
  50.7 0.0 collective-permute-done.2.flux_ref
  50.7 2.2 %finish_plane.1 = f32[5,16,128,512]{3,2,1,0:T(8,128)} custom-call(s32[2]{0:T(128)S(1)} %pad_add_fusion.place_ref, f32[16]{0:T(128)S(1)} %copy-done.6, f32[5,128,512]{2,1,0:T(8,128)S(1)} %collective-permute-done.2.flux_ref, f32[5,128,128]{2,1,0:T(8,128)S(1)} %get-tuple-element.30.first_ref, ...), custom_call_target="tpu_custom_call", output_to_operand_aliasing={{}: (5, {})} | custom-call | tf_op jit(solution)/shard_map/finish_plane/pallas_call | solution.py:637
  (10 shorter events, 0.0 us)
Async XLA Ops:
  0.1 9.6 %copy-start = (s32[16,128,512]{2,1,0:T(8,128)S(1)}, s32[16,128,512]{2,1,0:T(8,128)}, u32[]{:S(2)}) copy-start(s32[16,128,512]{2,1,0:T(8,128)} %level_ref.5) | copy-start | bytes 12582916
  0.1 9.6 %copy-start.1 = (f32[2,2,64,128]{3,2,1,0:T(8,128)S(1)}, f32[2,2,64,128]{3,2,1,0:T(8,128)}, u32[]{:S(2)}) copy-start(f32[2,2,64,128]{3,2,1,0:T(8,128)} %constant.20.clone.edge_ref) | copy-start | bytes 393220
  0.1 9.6 %copy-start.2 = (bf16[2,128,256]{2,1,0:T(8,128)(2,1)S(1)}, bf16[2,128,256]{2,1,0:T(8,128)(2,1)}, u32[]{:S(2)}) copy-start(bf16[2,128,256]{2,1,0:T(8,128)(2,1)} %constant.19.clone.table_ref) | copy-start | bytes 393220
  0.1 9.6 %copy-start.3 = (f32[5,512]{1,0:T(8,128)S(1)}, f32[5,512]{1,0:T(8,128)}, u32[]{:S(2)}) copy-start(f32[5,512]{1,0:T(8,128)} %target_ref.5) | copy-start | bytes 30724
  0.1 9.6 %copy-start.5 = (f32[512]{0:T(512)S(1)}, f32[512]{0:T(512)}, u32[]{:S(2)}) copy-start(f32[512]{0:T(512)} %param.12) | copy-start | bytes 6148
  0.1 9.6 %copy-start.6 = (f32[16]{0:T(128)S(1)}, f32[16]{0:T(128)}, u32[]{:S(2)}) copy-start(f32[16]{0:T(128)} %scale_ref.7) | copy-start | bytes 196
  3.5 16.7 %collective-permute-start.3 = (f32[5,128,512]{2,1,0:T(8,128)S(1)}, f32[5,128,512]{2,1,0:T(8,128)S(1)}, u32[]{:S(2)}, u32[]{:S(2)}) collective-permute-start(f32[5,128,512]{2,1,0:T(8,128)S(1)} %get-tuple-element.22), channel_id=1, source_target_pairs={{2,0},{0,2},{6,4},{4,6},{10,8},{8,10},{14,12},{12,14},{18,16},{16,... | collective-permute-start | bytes 3932168 | tf_op jit(solution)/shard_map/ppermute | solution.py:689
  3.6 11.7 %collective-permute-start.1 = (f32[2,5,16,512]{3,2,1,0:T(8,128)S(1)}, f32[2,5,16,512]{3,2,1,0:T(8,128)S(1)}, u32[]{:S(2)}, u32[]{:S(2)}) collective-permute-start(f32[2,5,16,512]{3,2,1,0:T(8,128)S(1)} %get-tuple-element.20), channel_id=1, source_target_pairs={{0,1},{1,0},{2,3},{3,2},{4,5},{5,4},{6,7},{7,6},{8,9},{9,8},{10,11... | collective-permute-start | bytes 983048 | tf_op jit(solution)/shard_map/ppermute | solution.py:684
  6.3 9.0 %collective-permute-start = (f32[5,32,128]{2,1,0:T(8,128)S(1)}, f32[5,32,128]{2,1,0:T(8,128)S(1)}, u32[]{:S(2)}, u32[]{:S(2)}) collective-permute-start(f32[5,32,128]{2,1,0:T(8,128)S(1)} %get-tuple-element.19), channel_id=1, source_target_pairs={{2,4},{6,8},{10,12},{14,16},{18,20},{22,24},{26,28},{4,2},{8,6},{1... | collective-permute-start | bytes 245768 | tf_op jit(solution)/shard_map/ppermute | solution.py:688
  17.3 33.4 %collective-permute-start.2 = (f32[5,128,512]{2,1,0:T(8,128)S(1)}, f32[5,128,512]{2,1,0:T(8,128)S(1)}, u32[]{:S(2)}, u32[]{:S(2)}) collective-permute-start(f32[5,128,512]{2,1,0:T(8,128)S(1)} %outer_plane.1), channel_id=1, source_target_pairs={{2,4},{6,8},{10,12},{14,16},{18,20},{22,24},{26,28},{4,2},{8,6},{1... | collective-permute-start | bytes 3932168 | tf_op jit(solution)/shard_map/ppermute | solution.py:698
  26.0 20.2 %collective-permute-start.4 = (f32[1304,128]{1,0:T(8,128)S(1)}, f32[1304,128]{1,0:T(8,128)S(1)}, u32[]{:S(2)}, u32[]{:S(2)}) collective-permute-start(f32[1304,128]{1,0:T(8,128)S(1)} %get-tuple-element.28.refs_0_), channel_id=1, source_target_pairs={{0,1},{1,0},{2,3},{3,2},{4,5},{5,4},{6,7},{7,6},{8,9},{9,8},{10,11... | collective-permute-start | bytes 2002952 | tf_op jit(solution)/shard_map/ppermute | solution.py:684
  27.3 18.9 %copy-start.4 = (bf16[2,128,256]{2,1,0:T(8,128)(2,1)S(1)}, bf16[2,128,256]{2,1,0:T(8,128)(2,1)}, u32[]{:S(2)}) copy-start(bf16[2,128,256]{2,1,0:T(8,128)(2,1)} %constant.21.clone.table_ref) | copy-start | bytes 393220
  27.3 18.9 %copy-start.7 = (s32[32]{0:T(128)S(1)}, s32[32]{0:T(128)}, u32[]{:S(2)}) copy-start(s32[32]{0:T(128)} %param.14) | copy-start | bytes 388

commit v4 on v2

--- a/solution.py
+++ b/solution.py
@@ -25,6 +25,10 @@
     return pltpu.CompilerParams(
         dimension_semantics=("arbitrary",) * steps, vmem_limit_bytes=limit * MIB
     )
+
+
+def stored(x):
+    return pltpu.with_memory_space_constraint(x, pltpu.HBM)
 
 
 def resident(x):
@@ -89,137 +93,123 @@
     return result
 
 
-def outer_kernel(odd_ref, state_ref, flux_ref, packed_ref):
-    step = pl.program_id(0)
-    rows = packed_ref.shape[1]
-    blocks = state_ref.shape[2] // rows
-    flux = axial_flux([state_ref[f, 0] for f in range(5)])
-    lane = lax.broadcasted_iota(jnp.int32, packed_ref.shape[1:], 1)
-    for f in range(5):
-        flux_ref[f, pl.ds(pl.multiple_of(step * state_ref.shape[2], 8), state_ref.shape[2])] = flux[f]
-        for i in range(blocks):
-            block = step * blocks + i
-            turned = pltpu.roll(flux[f][i * rows : (i + 1) * rows, :LANES], block * CYCLE, 1)
-            packed_ref[f] = jnp.where(lane // CYCLE == block, turned, packed_ref[f])
-
-
-def outer_plane(odd, state):
+def edge_kernel(place_ref, state_ref, edge_ref, far_flux_ref, near_flux_ref, row_ref, plane_ref, row_sem, plane_sem):
+    _, planes, columns, cycles = state_ref.shape
+    odd = place_ref[0]
+    ends = [
+        pltpu.make_async_copy(
+            state_ref.at[:, :, pl.ds(side * (columns - 1), 1)], row_ref.at[side], row_sem.at[side]
+        )
+        for side in range(2)
+    ]
+    wholes = [
+        pltpu.make_async_copy(
+            state_ref.at[:, away * (planes - 1), pl.ds(part * (columns // 2), columns // 2)],
+            plane_ref.at[side, :, pl.ds(part * (columns // 2), columns // 2)],
+            plane_sem.at[side, part],
+        )
+        for side, away in enumerate((odd, 1 - odd))
+        for part in range(2)
+    ]
+    for copy in ends + wholes:
+        copy.start()
+    for copy in ends:
+        copy.wait()
+    for side in range(2):
+        flux = swirl_flux([row_ref[1 - side, f, :, 0, :] for f in range(5)])
+        for f in range(5):
+            edge_ref[side, f] = flux[f]
+    half = columns // 2
+    for side, flux_ref in enumerate((far_flux_ref, near_flux_ref)):
+        for part in range(2):
+            wholes[2 * side + part].wait()
+            cut = slice(part * half, (part + 1) * half)
+            flux = axial_flux([plane_ref[side, f, cut] for f in range(5)])
+            for f in range(5):
+                flux_ref[f, cut] = flux[f]
+
+
+def edge_cells(place, state):
     _, planes, columns, cycles = state.shape
-    steps = 2
+    flux = pltpu.VMEM((5, columns, cycles), jnp.float32)
     return pl.pallas_call(
-        outer_kernel,
-        grid_spec=pltpu.PrefetchScalarGridSpec(
-            num_scalar_prefetch=1,
-            grid=(steps,),
-            in_specs=[
-                pl.BlockSpec((5, 1, columns // steps, cycles), lambda b, odd: (0, odd[0] * (planes - 1), b, 0))
-            ],
-            out_specs=[VMEM_SPEC, VMEM_SPEC],
-        ),
+        edge_kernel,
+        in_specs=[SMEM_SPEC, HBM_SPEC],
+        out_specs=[VMEM_SPEC] * 3,
+        scratch_shapes=[
+            pltpu.VMEM((2, 5, planes, 1, cycles), jnp.float32),
+            pltpu.VMEM((2, 5, columns, cycles), jnp.float32),
+            pltpu.SemaphoreType.DMA((2,)),
+            pltpu.SemaphoreType.DMA((2, 2)),
+        ],
         out_shape=[
-            pltpu.VMEM((5, columns, cycles), jnp.float32),
-            pltpu.VMEM((5, columns // PACK, LANES), jnp.float32),
+            pltpu.VMEM((2, 5, planes, cycles), jnp.float32),
+            flux,
+            flux,
         ],
-        compiler_params=params(1, 8),
-        name="outer_plane",
-    )(odd, state)
-
-
-def inner_kernel(odd_ref, state_ref, first_ref, last_ref, flux_ref, edge_ref):
-    step = pl.program_id(0)
-    rows = state_ref.shape[2]
-    flux = axial_flux([state_ref[f, 0] for f in range(5)])
-    for f in range(5):
-        flux_ref[f, pl.ds(pl.multiple_of(step * rows, 8), rows)] = flux[f]
-    low = swirl_flux([last_ref[f, :, 7, :] for f in range(5)])
-    high = swirl_flux([first_ref[f, :, 0, :] for f in range(5)])
-    planes = pl.ds(pl.multiple_of(step * 8, 8), 8)
-    for f in range(5):
-        edge_ref[0, f, planes] = low[f]
-        edge_ref[1, f, planes] = high[f]
-
-
-def inner_plane(odd, state):
-    _, planes, columns, cycles = state.shape
-    steps = planes // 8
+        compiler_params=pltpu.CompilerParams(vmem_limit_bytes=8 * MIB),
+        name="edge_cells",
+    )(place, state)
+
+
+def gate_kernel(sums_ref, *refs):
+    refs[-1][0:8] = sums_ref[0:8]
+
+
+def gate(sums, after):
     return pl.pallas_call(
-        inner_kernel,
-        grid_spec=pltpu.PrefetchScalarGridSpec(
-            num_scalar_prefetch=1,
-            grid=(steps,),
-            in_specs=[
-                pl.BlockSpec((5, 1, columns // steps, cycles), lambda b, odd: (0, (1 - odd[0]) * (planes - 1), b, 0)),
-                pl.BlockSpec((5, 8, 8, cycles), lambda b, odd: (0, b, 0, 0)),
-                pl.BlockSpec((5, 8, 8, cycles), lambda b, odd: (0, b, columns // 8 - 1, 0)),
-            ],
-            out_specs=[VMEM_SPEC, VMEM_SPEC],
-        ),
-        out_shape=[
-            pltpu.VMEM((5, columns, cycles), jnp.float32),
-            pltpu.VMEM((2, 5, planes, cycles), jnp.float32),
-        ],
-        compiler_params=params(1, 12),
-        name="inner_plane",
-    )(odd, state, state, state)
+        gate_kernel,
+        in_specs=[VMEM_SPEC] * (1 + len(after)),
+        out_specs=VMEM_SPEC,
+        out_shape=pltpu.VMEM(sums.shape, jnp.float32),
+        input_output_aliases={0: 0},
+        compiler_params=pltpu.CompilerParams(vmem_limit_bytes=1 * MIB),
+        name="gate",
+    )(resident(sums), *(resident(part) for part in after))
 
 
 def modes_kernel(
-    place_ref, scale_ref, state_ref, before_ref, after_ref, level_ref, inv_dr_ref, target_ref, table_ref, edge_ref,
-    near_ref, far_ref, sums_ref, tile_ref, behind_ref, rows_ref, axial_ref, swirl_ref, base_ref, split_ref,
-    *, cycles, cells, chunk,
+    place_ref, scale_ref, level_ref, inv_dr_ref, target_ref, table_ref, edge_ref, near_ref, state_ref,
+    sums_ref, tile_ref, behind_ref, rows_ref, axial_ref, swirl_ref, base_ref, split_ref, *, cells, chunk,
 ):
     step = pl.program_id(0)
     steps = pl.num_programs(0)
-    columns = state_ref.shape[2]
+    _, planes, columns, cycles = state_ref.shape
     odd = place_ref[0]
-    far_rows = far_ref.shape[1]
+    lane = lax.broadcasted_iota(jnp.int32, (chunk, LANES), 1)
 
     @pl.when(step == 0)
     def _():
         fill_rows(rows_ref, inv_dr_ref[...], 0, cycles, cells)
         for f in range(5):
+            axial_ref[0, f] = jnp.where(odd == 1, near_ref[f, :, :LANES], 0.0)
             for i in range(PACK):
                 swirl_ref[i, f, 0:8] = jnp.zeros((8, LANES), jnp.float32)
                 swirl_ref[i, f, columns + 8 : columns + 16] = jnp.zeros((8, LANES), jnp.float32)
 
-    def load(ref, plane, start):
-        return [ref[f, plane, pl.ds(start, chunk), :] for f in range(5)]
-
-    def halo(slot, use_near):
+    @pl.when(step > 0)
+    def _():
         for f in range(5):
-            for b in range(PACK):
-                away = far_ref[f]
-                away = away if b == 0 else pltpu.roll(away, LANES - b * CYCLE, 1)
-                near = near_ref[f, b * far_rows : (b + 1) * far_rows, :LANES]
-                axial_ref[slot, f, b * far_rows : (b + 1) * far_rows] = jnp.where(
-                    use_near, near, jnp.where(lane[:far_rows] < CYCLE, away, 0.0)
-                )
-
-    def neighbour(slot, ref):
-        def one(c, _):
-            start = pl.multiple_of(c * chunk, chunk)
-            flux = axial_flux(load(ref, 0, start))
-            for f in range(5):
-                axial_ref[slot, f, pl.ds(start, chunk)] = flux[f]
-            return 0
-
-        lax.fori_loop(0, columns // chunk, one, 0, unroll=True)
-
-    lane = lax.broadcasted_iota(jnp.int32, (chunk, LANES), 1)
-    pl.when(step == 0)(lambda: halo(0, odd == 1))
-    pl.when(step > 0)(lambda: neighbour(0, before_ref))
-    pl.when(step == steps - 1)(lambda: halo(PACK + 1, odd == 0))
-    pl.when(step < steps - 1)(lambda: neighbour(PACK + 1, after_ref))
+            axial_ref[0, f] = axial_ref[PACK, f]
+
+    def load(plane, start):
+        return [state_ref[f, plane, pl.ds(start, chunk), :LANES] for f in range(5)]
+
+    def following(start):
+        flux = axial_flux(load(jnp.minimum(step * PACK + PACK, planes - 1), start))
+        final = step == steps - 1
+        for f in range(5):
+            halo = jnp.where(odd == 0, near_ref[f, pl.ds(start, chunk), :LANES], 0.0)
+            axial_ref[PACK + 1, f, pl.ds(start, chunk)] = jnp.where(final, halo, flux[f])
 
     def wide(row):
         return jnp.broadcast_to(row[None], (chunk // 8, 8, LANES)).reshape(chunk, LANES)
 
-    def first(c, _):
-        start = pl.multiple_of(c * chunk, chunk)
+    def first(start):
         up, down, around = [wide(rows_ref[k]) for k in range(3)]
         target = [jnp.broadcast_to(target_ref[f : f + 1], (chunk, LANES)) for f in range(5)]
         for i in range(PACK):
-            q = load(state_ref, i, start)
+            q = load(step * PACK + i, start)
             axial, radial, swirl = all_fluxes(q)
             sponge = level_ref[i, pl.ds(start, chunk), :].astype(jnp.float32) * (time_step * sponge_rate)
             scaled = [around * flux for flux in swirl]
@@ -232,9 +222,6 @@
                 axial_ref[i + 1, f, pl.ds(start, chunk)] = axial[f]
                 swirl_ref[i, f, pl.ds(start + 8, chunk)] = scaled[f]
                 base_ref[i, f, pl.ds(start, chunk)] = base[f]
-        return 0
-
-    lax.fori_loop(0, columns // chunk, first, 0, unroll=True)
 
     def packed(parts, rows):
         result = parts[0]
@@ -243,10 +230,10 @@
         return result
 
     factor = [(0.5 * time_step) * scale_ref[step * PACK + i] for i in range(PACK)]
-    for f in range(5):
-        total = jnp.zeros((8, LANES), jnp.float32)
-        for c in range(columns // chunk):
-            start = c * chunk
+    total = [jnp.zeros((8, LANES), jnp.float32)] * 5
+
+    def second(start):
+        for f in range(5):
             parts = []
             for i in range(PACK):
                 value = base_ref[i, f, start : start + chunk]
@@ -264,7 +251,15 @@
             split_ref[f, columns + start : columns + start + chunk] = (value - high.astype(jnp.float32)).astype(
                 jnp.bfloat16
             )
-            total = total + value.reshape(chunk // 8, 8, LANES).sum(axis=0)
+            total[f] = total[f] + value.reshape(chunk // 8, 8, LANES).sum(axis=0)
+
+    for start in range(0, columns, chunk):
+        first(start)
+        following(start)
+        if start:
+            second(start - chunk)
+    second(columns - chunk)
+    for f in range(5):
         sums = jnp.dot(table_ref[0], split_ref[f], preferred_element_type=jnp.float32)
         half = sums.shape[0] // 2
         start_row = packed([swirl_ref[i, f, 8:16] for i in range(PACK)], 8)[0:1]
@@ -273,7 +268,7 @@
         sums_ref[pl.ds(pl.multiple_of(group * half, half), half), :] = (
             sums[:half] + sums[half:] + (edge_ref[0, 1] * end_row - edge_ref[0, 0] * start_row)
         )
-        mean = total.sum(axis=0, keepdims=True) + (end_row - start_row)
+        mean = total[f].sum(axis=0, keepdims=True) + (end_row - start_row)
         sums_ref[pl.ds(steps * 5 * half + group, 1), :] = mean
 
 
@@ -282,24 +277,19 @@
     return groups * half + -(-groups // 8) * 8
 
 
-def inner_modes(place, scale, state, sponge, inv_dr, target, table, edge, near, far, cells):
+def inner_modes(place, scale, sponge, inv_dr, target, table, edge, near, state, cells):
     _, planes, columns, cycles = state.shape
     half = table.shape[1] // 2
     chunk = min(32, columns)
     whole = lambda *shape: pl.BlockSpec(shape, lambda g, place: (0,) * len(shape))
     tile = pltpu.VMEM((5, planes, columns, LANES), jnp.float32)
     return pl.pallas_call(
-        functools.partial(modes_kernel, cycles=cycles, cells=cells, chunk=chunk),
+        functools.partial(modes_kernel, cells=cells, chunk=chunk),
         grid_spec=pltpu.PrefetchScalarGridSpec(
             num_scalar_prefetch=1,
             grid=(planes // PACK,),
             in_specs=[
                 SMEM_SPEC,
-                pl.BlockSpec((5, PACK, columns, LANES), lambda g, place: (0, g, 0, 0)),
-                pl.BlockSpec((5, 1, columns, LANES), lambda g, place: (0, jnp.maximum(g * PACK - 1, 0), 0, 0)),
-                pl.BlockSpec(
-                    (5, 1, columns, LANES), lambda g, place: (0, jnp.minimum(g * PACK + PACK, planes - 1), 0, 0)
-                ),
                 pl.BlockSpec((PACK, columns, LANES), lambda g, place: (g, 0, 0)),
                 whole(1, LANES),
                 whole(5, LANES),
@@ -308,7 +298,7 @@
                 VMEM_SPEC,
                 VMEM_SPEC,
             ],
-            out_specs=[VMEM_SPEC, VMEM_SPEC, VMEM_SPEC],
+            out_specs=[VMEM_SPEC] * 3,
             scratch_shapes=[
                 pltpu.VMEM((3, 8, LANES), jnp.float32),
                 pltpu.VMEM((PACK + 2, 5, columns, LANES), jnp.float32),
@@ -318,9 +308,9 @@
             ],
         ),
         out_shape=[pltpu.VMEM((mode_rows(planes, half), LANES), jnp.float32), tile, tile],
-        compiler_params=params(1, 20),
+        compiler_params=params(1, 12),
         name="inner_modes",
-    )(place, scale, state, state, state, sponge, inv_dr, target, table, edge, resident(near), resident(far))
+    )(place, *(stored(part) for part in (scale, sponge, inv_dr, target, table, edge)), resident(near), resident(state))
 
 
 IN_SLOTS = 3
@@ -329,8 +319,8 @@
 
 def update_kernel(
     place_ref, scale_ref, inv_dr_ref, target_ref, near_ref, halo_ref, behind_ref, state_ref, level_ref,
-    out_ref, ahead_ref, rows_ref, fields_ref, levels_ref, result_ref, axial_even_ref, axial_odd_ref, swirl_even_ref,
-    swirl_odd_ref, base_ref, field_sem, level_sem, result_sem, *, cells, chunk, unroll,
+    out_ref, ahead_ref, kept_ref, rows_ref, levels_ref, result_ref, axial_even_ref, axial_odd_ref, swirl_even_ref,
+    swirl_odd_ref, base_ref, level_sem, result_sem, *, cells, chunk, unroll,
 ):
     axial_refs = (axial_even_ref, axial_odd_ref)
     swirl_refs = (swirl_even_ref, swirl_odd_ref)
@@ -342,18 +332,18 @@
 
     def fetch(plane):
         slot = lax.rem(plane, IN_SLOTS)
-        return (
-            pltpu.make_async_copy(state_ref.at[:, plane, :, rest], fields_ref.at[slot], field_sem.at[slot]),
-            pltpu.make_async_copy(level_ref.at[plane, :, rest], levels_ref.at[slot], level_sem.at[slot]),
-        )
+        return pltpu.make_async_copy(level_ref.at[plane, :, rest], levels_ref.at[slot], level_sem.at[slot])
 
     def store(plane):
         slot = lax.rem(plane, OUT_SLOTS)
         return pltpu.make_async_copy(result_ref.at[slot], out_ref.at[:, plane, :, rest], result_sem.at[slot])
 
+    def keep(plane):
+        slot = lax.rem(plane, OUT_SLOTS)
+        return pltpu.make_async_copy(result_ref.at[slot], kept_ref, result_sem.at[slot])
+
     for plane in range(IN_SLOTS):
-        for copy in fetch(plane):
-            copy.start()
+        fetch(plane).start()
 
     fill_rows(rows_ref, inv_dr_ref[:, LANES:], LANES, cycles, cells)
 
@@ -392,7 +382,7 @@
         slot = lax.rem(plane, IN_SLOTS)
 
         def open_tile(k):
-            q = [fields_ref[slot, f, rows, k * LANES : (k + 1) * LANES] for f in range(5)]
+            q = [state_ref[f, plane, rows, (k + 1) * LANES : (k + 2) * LANES] for f in range(5)]
             axial, radial, swirl = all_fluxes(q)
             ahead = [pltpu.roll(flux, LANES - 1, 1) for flux in radial]
             behind = [pltpu.roll(flux, 1, 1) for flux in radial]
@@ -434,8 +424,7 @@
             )
 
     def one_plane(plane, parity):
-        for copy in fetch(plane):
-            copy.wait()
+        fetch(plane).wait()
         for f in range(5):
             for side, row in ((0, 7), (1, columns + 8)):
                 edge = halo_ref[side, f, pl.ds(plane, 1), :]
@@ -449,12 +438,13 @@
             return 0
 
         lax.fori_loop(0, columns // chunk, step, 0, unroll=unroll)
-        pl.when(plane > 0)(lambda: store(plane - 1).start())
+        outer = jnp.logical_and(plane == 1, odd == 0)
+        pl.when(outer)(lambda: keep(plane - 1).start())
+        pl.when(jnp.logical_and(plane > 0, jnp.logical_not(outer)))(lambda: store(plane - 1).start())
 
         @pl.when(plane + IN_SLOTS < planes)
         def _():
-            for copy in fetch(plane + IN_SLOTS):
-                copy.start()
+            fetch(plane + IN_SLOTS).start()
 
     def two_planes(pair, _):
         for parity in range(2):
@@ -472,7 +462,8 @@
         return 0
 
     lax.fori_loop(0, columns // chunk, last, 0)
-    store(planes - 1).start()
+    pl.when(odd == 0)(lambda: store(planes - 1).start())
+    pl.when(odd == 1)(lambda: keep(planes - 1).start())
     for plane in range(planes - OUT_SLOTS, planes):
         store(plane).wait()
 
@@ -483,11 +474,10 @@
     width = cycles - LANES
     return pl.pallas_call(
         functools.partial(update_kernel, cells=cells, chunk=chunk, unroll=unroll),
-        in_specs=[SMEM_SPEC, SMEM_SPEC, VMEM_SPEC, VMEM_SPEC, VMEM_SPEC, VMEM_SPEC, VMEM_SPEC, HBM_SPEC, HBM_SPEC],
-        out_specs=[HBM_SPEC, VMEM_SPEC],
+        in_specs=[SMEM_SPEC, SMEM_SPEC, VMEM_SPEC, VMEM_SPEC, VMEM_SPEC, VMEM_SPEC, VMEM_SPEC, VMEM_SPEC, HBM_SPEC],
+        out_specs=[HBM_SPEC, VMEM_SPEC, VMEM_SPEC],
         scratch_shapes=[
             pltpu.VMEM((3, 8, width), jnp.float32),
-            pltpu.VMEM((IN_SLOTS, 5, columns, width), jnp.float32),
             pltpu.VMEM((IN_SLOTS, columns, width), jnp.int32),
             pltpu.VMEM((OUT_SLOTS, 5, columns, width), jnp.float32),
             pltpu.VMEM((5, tiles, columns, LANES), jnp.float32),
@@ -496,31 +486,28 @@
             pltpu.VMEM((5, tiles, columns + 16, LANES), jnp.float32),
             pltpu.VMEM((5, tiles, columns, LANES), jnp.float32),
             pltpu.SemaphoreType.DMA((IN_SLOTS,)),
-            pltpu.SemaphoreType.DMA((IN_SLOTS,)),
             pltpu.SemaphoreType.DMA((OUT_SLOTS,)),
         ],
         out_shape=[
             jax.ShapeDtypeStruct(state.shape, jnp.float32),
             pltpu.VMEM((5, planes, columns, LANES), jnp.float32),
+            pltpu.VMEM((5, columns, width), jnp.float32),
         ],
-        compiler_params=pltpu.CompilerParams(vmem_limit_bytes=20 * MIB),
+        compiler_params=pltpu.CompilerParams(vmem_limit_bytes=13 * MIB),
+        input_output_aliases={6: 1},
         name="bulk_update",
-    )(place, scale, inv_dr, target, resident(near), resident(halo), resident(behind), state, sponge)
+    )(place, scale, inv_dr, target, resident(near), resident(halo), resident(behind), resident(state), stored(sponge))
 
 
 def filter_kernel(
     place_ref, cutoff_ref, table_ref, inv_dr_ref, tile_ref, ahead_ref, halo_ref, *refs, cells, cycles
 ):
-    *sums, state_ref, out_ref, split_ref = refs
+    *sums, state_ref, out_ref, kept_ref, split_ref = refs
     step = pl.program_id(0)
     steps = pl.num_programs(0)
     half = table_ref.shape[2] // 4
-    count = half // 2
     columns = out_ref.shape[2]
-    mode = lax.broadcasted_iota(jnp.int32, (half, LANES), 0)
-    mode = jnp.where(mode >= count, mode - count, mode) + 1
-    cut = jnp.concatenate([cutoff_ref[...]] * PACK, axis=1)
-    weight = jnp.where(mode <= cut, 2.0 / cells, 0.0)
+    weight = mode_weight(cutoff_ref[...], half, cells)
     lane = lax.broadcasted_iota(jnp.int32, (columns, LANES), 1)
     spacing = 4.0 / cycles
     edge = 1.0 + spacing * (LANES - 1)
@@ -531,19 +518,10 @@
     around = jnp.where(cycle < CYCLE, 0.0, around)
     for f in range(5):
         group = step * 5 + f
-        rows = pl.ds(pl.multiple_of(group * half, half), half)
-        coefficient = sums[0][rows, :]
-        mean = sums[0][pl.ds(steps * 5 * half + group, 1), :]
-        for other in sums[1:]:
-            coefficient = coefficient + other[rows, :]
-            mean = mean + other[pl.ds(steps * 5 * half + group, 1), :]
-        coefficient = coefficient * weight
-        high = coefficient.astype(jnp.bfloat16)
-        low = (coefficient - high.astype(jnp.float32)).astype(jnp.bfloat16)
-        for k in range(2):
-            split_ref[f, 2 * k * half : (2 * k + 1) * half] = high
-            split_ref[f, (2 * k + 1) * half : (2 * k + 2) * half] = low
-        values = jnp.dot(table_ref[0], split_ref[f], preferred_element_type=jnp.float32) + mean * (1.0 / cells)
+        values = turn_back(
+            sums, pl.multiple_of(group * half, half), steps * 5 * half + group, weight, table_ref[0],
+            split_ref.at[f], cells,
+        )
         for i in range(PACK):
             turned = values if i == 0 else pltpu.roll(values, LANES - i * CYCLE, 1)
             plane = step * PACK + i
@@ -552,6 +530,14 @@
             high = halo_ref[1, f, pl.ds(plane, 1), :][:, :LANES]
             out_ref[f, i, 0:1] = out_ref[f, i, 0:1] + around * low
             out_ref[f, i, columns - 1 : columns] = out_ref[f, i, columns - 1 : columns] - around * high
+
+    def keep(i):
+        for f in range(5):
+            kept_ref[f] = out_ref[f, i]
+
+    odd = place_ref[0]
+    pl.when(jnp.logical_and(step == 0, odd == 0))(lambda: keep(0))
+    pl.when(jnp.logical_and(step == steps - 1, odd == 1))(lambda: keep(PACK - 1))
 
 
 def put_filtered(place, cutoff, table, inv_dr, tile, ahead, halo, sums, updated, cells):
@@ -571,10 +557,13 @@
             ]
             + [VMEM_SPEC] * len(sums)
             + [HBM_SPEC],
-            out_specs=pl.BlockSpec((5, PACK, columns, LANES), lambda g, place: (0, g, 0, 0)),
+            out_specs=[pl.BlockSpec((5, PACK, columns, LANES), lambda g, place: (0, g, 0, 0)), VMEM_SPEC],
             scratch_shapes=[pltpu.VMEM((5, table.shape[2], LANES), jnp.bfloat16)],
         ),
-        out_shape=jax.ShapeDtypeStruct(updated.shape, jnp.float32),
+        out_shape=[
+            jax.ShapeDtypeStruct(updated.shape, jnp.float32),
+            pltpu.VMEM((5, columns, LANES), jnp.float32),
+        ],
         input_output_aliases={7 + len(sums): 0},
         compiler_params=params(1, 12),
         name="put_filtered",
@@ -582,35 +571,110 @@
       *(resident(part) for part in sums), updated)
 
 
-def finish_kernel(place_ref, scale_ref, flux_ref, state_ref, out_ref):
+def outer_kernel(place_ref, scale_ref, table_ref, flux_ref, after_ref, sums_ref, split_ref):
     odd = place_ref[0]
     planes = scale_ref.shape[0]
-    rows = out_ref.shape[2]
+    columns = flux_ref.shape[1]
+    half = table_ref.shape[1] // 2
     factor = (0.5 * time_step) * scale_ref[odd * (planes - 1)]
     factor = jnp.where(odd == 1, -factor, factor)
-    lane = lax.broadcasted_iota(jnp.int32, out_ref.shape[2:], 1)
-    start = pl.multiple_of(pl.program_id(0) * rows, 8)
+    lane = lax.broadcasted_iota(jnp.int32, (columns, LANES), 1)
+    for group in range(2):
+        value = jnp.zeros((columns, LANES), jnp.float32)
+        for i in range(PACK):
+            if group * PACK + i < 5:
+                part = factor * flux_ref[group * PACK + i, :, :LANES]
+                part = part if i == 0 else pltpu.roll(part, i * CYCLE, 1)
+                value = jnp.where(lane // CYCLE == i, part, value)
+        high = value.astype(jnp.bfloat16)
+        split_ref[group, :columns] = high
+        split_ref[group, columns:] = (value - high.astype(jnp.float32)).astype(jnp.bfloat16)
+        sums = jnp.dot(table_ref[place_ref[1]], split_ref[group], preferred_element_type=jnp.float32)
+        sums_ref[group * half : (group + 1) * half] = sums[:half] + sums[half:]
+        sums_ref[2 * half + group : 2 * half + group + 1] = value.sum(axis=0, keepdims=True)
+
+
+def outer_modes(place, scale, table, flux, after):
+    half = table.shape[1] // 2
+    return pl.pallas_call(
+        outer_kernel,
+        in_specs=[SMEM_SPEC, SMEM_SPEC, VMEM_SPEC, VMEM_SPEC, VMEM_SPEC],
+        out_specs=VMEM_SPEC,
+        scratch_shapes=[pltpu.VMEM((2, 2 * flux.shape[1], LANES), jnp.bfloat16)],
+        out_shape=pltpu.VMEM((2 * half + 8, LANES), jnp.float32),
+        compiler_params=pltpu.CompilerParams(vmem_limit_bytes=4 * MIB),
+        name="outer_modes",
+    )(place, scale, table, resident(flux), resident(after))
+
+
+def turn_back(sums, base, mean_row, weight, table, split_ref, cells):
+    half = weight.shape[0]
+    coefficient = sums[0][pl.ds(base, half), :]
+    mean = sums[0][pl.ds(mean_row, 1), :]
+    for other in sums[1:]:
+        coefficient = coefficient + other[pl.ds(base, half), :]
+        mean = mean + other[pl.ds(mean_row, 1), :]
+    coefficient = coefficient * weight
+    high = coefficient.astype(jnp.bfloat16)
+    low = (coefficient - high.astype(jnp.float32)).astype(jnp.bfloat16)
+    for k in range(2):
+        split_ref[2 * k * half : (2 * k + 1) * half] = high
+        split_ref[(2 * k + 1) * half : (2 * k + 2) * half] = low
+    return jnp.dot(table, split_ref[...], preferred_element_type=jnp.float32) + mean * (1.0 / cells)
+
+
+def mode_weight(cutoff, half, cells):
+    count = half // 2
+    mode = lax.broadcasted_iota(jnp.int32, (half, LANES), 0)
+    mode = jnp.where(mode >= count, mode - count, mode) + 1
+    return jnp.where(mode <= jnp.concatenate([cutoff] * PACK, axis=1), 2.0 / cells, 0.0)
+
+
+def finish_kernel(place_ref, scale_ref, cutoff_ref, table_ref, flux_ref, first_ref, rest_ref, *refs, cells):
+    *sums, state_ref, out_ref, result_ref, split_ref, result_sem = refs
+    odd = place_ref[0]
+    planes = scale_ref.shape[0]
+    columns = flux_ref.shape[1]
+    half = table_ref.shape[2] // 4
+    plane = odd * (planes - 1)
+    factor = (0.5 * time_step) * scale_ref[plane]
+    factor = jnp.where(odd == 1, -factor, factor)
+    lane = lax.broadcasted_iota(jnp.int32, (columns, LANES), 1)
+    weight = mode_weight(cutoff_ref[...], half, cells)
+    table = table_ref[place_ref[1]]
+    copies = []
     for f in range(5):
-        out_ref[f, 0] = state_ref[f, 0] + jnp.where(lane < CYCLE, 0.0, factor * flux_ref[f, pl.ds(start, rows)])
-
-
-def finish_plane(place, scale, flux, updated):
-    _, planes, columns, cycles = updated.shape
-    steps = 2
-    block = pl.BlockSpec((5, 1, columns // steps, cycles), lambda b, place: (0, place[0] * (planes - 1), b, 0))
+        group, i = f // PACK, f % PACK
+        if i == 0:
+            values = turn_back(sums, group * half, 2 * half + group, weight, table, split_ref.at[group], cells)
+        turned = values if i == 0 else pltpu.roll(values, LANES - i * CYCLE, 1)
+        flux = factor * flux_ref[f]
+        result_ref[f, :, :LANES] = first_ref[f] + jnp.where(lane < CYCLE, turned, flux[:, :LANES])
+        result_ref[f, :, LANES:] = rest_ref[f] + flux[:, LANES:]
+        copies.append(pltpu.make_async_copy(result_ref.at[f], out_ref.at[f, plane], result_sem.at[f]))
+        copies[-1].start()
+    for copy in copies:
+        copy.wait()
+
+
+def finish_plane(place, scale, cutoff, table, flux, first, rest, sums, updated, cells):
     return pl.pallas_call(
-        finish_kernel,
-        grid_spec=pltpu.PrefetchScalarGridSpec(
-            num_scalar_prefetch=1,
-            grid=(steps,),
-            in_specs=[SMEM_SPEC, VMEM_SPEC, block],
-            out_specs=block,
-        ),
+        functools.partial(finish_kernel, cells=cells),
+        in_specs=[SMEM_SPEC, SMEM_SPEC] + [VMEM_SPEC] * (5 + len(sums)) + [HBM_SPEC],
+        out_specs=HBM_SPEC,
+        scratch_shapes=[
+            pltpu.VMEM(flux.shape, jnp.float32),
+            pltpu.VMEM((2, table.shape[2], LANES), jnp.bfloat16),
+            pltpu.SemaphoreType.DMA((5,)),
+        ],
         out_shape=jax.ShapeDtypeStruct(updated.shape, jnp.float32),
-        input_output_aliases={3: 0},
-        compiler_params=params(1, 12),
+        input_output_aliases={7 + len(sums): 0},
+        compiler_params=pltpu.CompilerParams(vmem_limit_bytes=4 * MIB),
         name="finish_plane",
-    )(place, scale, resident(flux), updated)
+    )(
+        place, scale, cutoff, table, resident(flux), resident(first), resident(rest),
+        *(resident(part) for part in sums), updated,
+    )
 
 
 def mode_tables(cells, sectors):
@@ -645,24 +709,25 @@
     far_pairs = [(i, i + 1) for i in range(1, rows - 1, 2)] + [(i + 1, i) for i in range(1, rows - 1, 2)]
     shifted = lambda part, by: lax.ppermute(part, "az", [(i, (i + by) % sectors) for i in range(sectors)])
 
-    far_flux, far_packed = outer_plane(place, state)
-    far_packed = lax.ppermute(far_packed, "gx", far_pairs)
+    edges, far_flux, near_flux = edge_cells(place, stored(state))
     far_flux = lax.ppermute(far_flux, "gx", far_pairs)
-    near_flux, edges = inner_plane(place, state)
     near_flux = lax.ppermute(near_flux, "gx", near_pairs)
     if sectors == 2:
         halo = shifted(edges, 1)
     else:
         halo = jnp.stack([shifted(edges[0], 1), shifted(edges[1], sectors - 1)])
     sums, tile, behind = inner_modes(
-        place, inv_dx, state, sponge_level, inv_dr, target, forward, edge, near_flux, far_packed, cells
+        place, inv_dx, sponge_level, inv_dr, target, forward, edge, near_flux, state, cells
     )
+    sums = gate(sums, [halo])
     others = [shifted(sums, by) for by in range(1, sectors)]
-    updated, ahead = bulk_update(
+    updated, ahead, rest = bulk_update(
         place, inv_dx, state, sponge_level, inv_dr, target, near_flux, halo, behind, cells
     )
-    updated = put_filtered(place, cutoff, inverse, inv_dr, tile, ahead, halo, [sums, *others], updated, cells)
-    return finish_plane(place, inv_dx, far_flux, updated)
+    outer = outer_modes(place, inv_dx, forward, far_flux, rest)
+    outer = [outer] + [shifted(outer, by) for by in range(1, sectors)]
+    updated, first = put_filtered(place, cutoff, inverse, inv_dr, tile, ahead, halo, [sums, *others], updated, cells)
+    return finish_plane(place, inv_dx, cutoff, inverse, far_flux, first, rest, outer, updated, cells)
 
 
 def solution(mesh):

time: 100 us -> 45.8 us (0.46)
  waiting for transfers between devices: 40 us -> 1.06 us
  local copies, waits for them, and re-layouts: 12.5 us -> 0.03 us
  Pallas kernels: 38.1 us -> 35.2 us
    ppermute x1 -> x0, waiting for transfers between devices: 28.4 us -> none  [body(): far_packed = lax.ppermute(far_packed, 'gx', far_pairs)]
    unnamed x20 -> x14, local copies, waits for them, and re-layouts: 12.5 us -> 0.03 us
    ppermute x2 -> x3, waiting for transfers between devices: 11.6 us -> 0.01 us  [body(): lax.ppermute(part, 'az', [(i, (i + by) % sectors) for i in range(sectors)])]
    pallas_call x1, Pallas kernels: 19.3 us -> 16.9 us  [bulk_update(): pl.pallas_call(functools.partial(update_kernel, cells=cells, chunk=chunk,...]
    ppermute x2 -> x3, starting transfers between devices: 1.53 us -> 3.74 us  [body(): lax.ppermute(part, 'az', [(i, (i + by) % sectors) for i in range(sectors)])]
    ppermute x1 -> x0, starting transfers between devices: 1.92 us -> none  [body(): far_packed = lax.ppermute(far_packed, 'gx', far_pairs)]
    ppermute x1, waiting for transfers between devices: 0.01 us -> 1.05 us  [body(): far_flux = lax.ppermute(far_flux, 'gx', far_pairs)]
    pallas_call x4 -> x5, Pallas kernels: 14.3 us -> 13.7 us  [the longest x1 8.17 us: inner_modes(): pl.pallas_call(functools.partial(modes_kernel, cells=cells, chunk=chunk),...]
  transfers between devices with their start and end apart: 5 -> 5, of which waited for: 2 -> 1; matrix products, arithmetic and copies ran while one was open for 0% -> 0% of each run, Pallas kernels for 34% -> 68%
where the time goes in v4:
time: 45.8 us; the launch traced here: 45.1 us
  Pallas kernels  35.2 us (77%)
  starting transfers between devices  8.62 us (19%)
  waiting for transfers between devices  1.06 us (2%)
    pallas_call x1, Pallas kernels, bulk_update(): pl.pallas_call(functools.partial(update_kernel, cells=cells, chunk=chunk,...  16.9 us
    pallas_call x1, Pallas kernels, inner_modes(): pl.pallas_call(functools.partial(modes_kernel, cells=cells, chunk=chunk),...  8.17 us
    ppermute x1, starting transfers between devices, body(): far_flux = lax.ppermute(far_flux, 'gx', far_pairs)  4.76 us
    pallas_call x1, Pallas kernels, put_filtered(): pl.pallas_call(functools.partial(filter_kernel, cells=cells, cycles=cycle...  4.57 us
    ppermute x3, starting transfers between devices, body(): lax.ppermute(part, 'az', [(i, (i + by) % sectors) for i in range(sectors)])  3.74 us
    pallas_call x1, Pallas kernels, edge_cells(): pl.pallas_call(edge_kernel, in_specs=[SMEM_SPEC, HBM_SPEC], out_specs=[VM...  2.77 us
    pallas_call x1, Pallas kernels, finish_plane(): pl.pallas_call(functools.partial(finish_kernel, cells=cells), in_specs=[S...  1.94 us
    ppermute x1, waiting for transfers between devices, body(): far_flux = lax.ppermute(far_flux, 'gx', far_pairs)  1.05 us
  transfers between devices with their start and end apart: 5, of which 1 were waited for; matrix products, arithmetic and copies ran while one was open for 0% of the time, Pallas kernels for 68%

profile of v4, /device:TPU:1, one launch (start us, length us, event | category | flops | bytes accessed | tf_op | source)
XLA Modules:
  0.0 45.1 jit_solution(9938744793078958601)
XLA Ops:
  0.0 0.1 pad_add_fusion.place_ref
  0.1 2.8 %edge_cells.1 = (f32[2,5,16,512]{3,2,1,0:T(8,128)S(1)}, f32[5,128,512]{2,1,0:T(8,128)S(1)}, f32[5,128,512]{2,1,0:T(8,128)S(1)}) custom-call(s32[2]{0:T(128)S(1)} %pad_add_fusion.place_ref, f32[5,16,128,512]{3,2,1,0:T(8,128)} %state_ref.5), custom_call_target="tpu_custom_call" | custom-call | tf_op jit(solution)/shard_map/edge_cells/pallas_call | solution.py:135
  2.9 0.1 collective-permute-start.1
  3.0 4.8 %collective-permute-start = (f32[5,128,512]{2,1,0:T(8,128)S(1)}, f32[5,128,512]{2,1,0:T(8,128)S(1)}, u32[]{:S(2)}, u32[]{:S(2)}) collective-permute-start(f32[5,128,512]{2,1,0:T(8,128)S(1)} %get-tuple-element.16), channel_id=1, source_target_pairs={{2,4},{6,8},{10,12},{14,16},{18,20},{22,24},{26,28},{4,2},{8,6},{1... | collective-permute-start | bytes 3932168 | tf_op jit(solution)/shard_map/ppermute | solution.py:713
  7.7 1.4 %collective-permute-start.2 = (f32[2,5,16,512]{3,2,1,0:T(8,128)S(1)}, f32[2,5,16,512]{3,2,1,0:T(8,128)S(1)}, u32[]{:S(2)}, u32[]{:S(2)}) collective-permute-start(f32[2,5,16,512]{3,2,1,0:T(8,128)S(1)} %get-tuple-element.19), channel_id=1, source_target_pairs={{0,1},{1,0},{2,3},{3,2},{4,5},{5,4},{6,7},{7,6},{8,9},{9,8},{10,11... | collective-permute-start | bytes 983048 | tf_op jit(solution)/shard_map/ppermute | solution.py:710
  9.1 0.0 collective-permute-done.1.near_ref
  9.2 0.0 copy-done
  9.2 0.0 copy-start.5
  9.2 8.2 %inner_modes.1 = (f32[1304,128]{1,0:T(8,128)S(1)}, f32[5,16,128,128]{3,2,1,0:T(8,128)S(1)}, f32[5,16,128,128]{3,2,1,0:T(8,128)S(1)}) custom-call(s32[2]{0:T(128)S(1)} %pad_add_fusion.place_ref, f32[16]{0:T(128)} %scale_ref.7, s32[16,128,512]{2,1,0:T(8,128)} %level_ref.3, f32[1,512]{1,0:T(1,128)} %bitcast.4, f32[5,512]{1,0:T(8,128)} %target_ref.3, ...), custom_call_target="tpu_custom_call" | custom-call | tf_op jit(solution)/shard_map/inner_modes/pallas_call | solution.py:286
  17.4 0.0 collective-permute-done.2.halo_ref.refs_0_
  17.4 0.9 %collective-permute-start.3 = (f32[1304,128]{1,0:T(8,128)S(1)}, f32[1304,128]{1,0:T(8,128)S(1)}, u32[]{:S(2)}, u32[]{:S(2)}) collective-permute-start(f32[1304,128]{1,0:T(8,128)S(1)} %gate.1.refs_0_), channel_id=1, source_target_pairs={{0,1},{1,0},{2,3},{3,2},{4,5},{5,4},{6,7},{7,6},{8,9},{9,8},{10,11... | collective-permute-start | bytes 2002952 | tf_op jit(solution)/shard_map/ppermute | solution.py:710
  18.3 0.0 copy-done.3
  18.3 0.0 copy-done.4
  18.3 0.0 copy-done.5
  18.3 0.0 copy-start.1
  18.3 0.0 copy-start.6
  18.3 16.9 %bulk_update.1 = (f32[5,16,128,512]{3,2,1,0:T(8,128)}, f32[5,16,128,128]{3,2,1,0:T(8,128)S(1)}, f32[5,128,384]{2,1,0:T(8,128)S(1)}) custom-call(s32[2]{0:T(128)S(1)} %pad_add_fusion.place_ref, f32[16]{0:T(128)S(1)} %copy-done.5, f32[1,512]{1,0:T(1,128)S(1)} %bitcast.5, f32[5,512]{1,0:T(8,128)S(1)} %copy-done.3, ...), custom_call_target="tpu_custom_call", output_to_operand_aliasing={{1}: (6, {})} | custom-call | tf_op jit(solution)/shard_map/bulk_update/pallas_call | solution.py:475
  35.3 1.1 %collective-permute-done.flux_ref = f32[5,128,512]{2,1,0:T(8,128)S(1)} collective-permute-done((f32[5,128,512]{2,1,0:T(8,128)S(1)}, f32[5,128,512]{2,1,0:T(8,128)S(1)}, u32[]{:S(2)}, u32[]{:S(2)}) %collective-permute-start) | collective-permute-done | bytes 1310752 | tf_op jit(solution)/shard_map/ppermute | solution.py:713
  36.3 0.8 %outer_modes.1.refs_0_ = f32[136,128]{1,0:T(8,128)S(1)} custom-call(s32[2]{0:T(128)S(1)} %pad_add_fusion.place_ref, f32[16]{0:T(128)S(1)} %copy-done.5, bf16[2,128,256]{2,1,0:T(8,128)(2,1)S(1)} %copy-done.2, f32[5,128,512]{2,1,0:T(8,128)S(1)} %collective-permute-done.flux_ref, f32[5,128,384]{2,1,0:T(8,128)S(1)} %get-tuple-element.25.after_ref.rest_ref), custom_call_target="tpu_custom_call" | custom-call | tf_op jit(solution)/shard_map/outer_modes/pallas_call | solution.py:599
  37.2 1.4 %collective-permute-start.4 = (f32[136,128]{1,0:T(8,128)S(1)}, f32[136,128]{1,0:T(8,128)S(1)}, u32[]{:S(2)}, u32[]{:S(2)}) collective-permute-start(f32[136,128]{1,0:T(8,128)S(1)} %outer_modes.1.refs_0_), channel_id=1, source_target_pairs={{0,1},{1,0},{2,3},{3,2},{4,5},{5,4},{6,7},{7,6},{8,9},{9,8},{10,11... | collective-permute-start | bytes 208904 | tf_op jit(solution)/shard_map/ppermute | solution.py:710
  38.6 0.0 collective-permute-done.3.refs_1_
  38.6 4.6 %put_filtered.1 = (f32[5,16,128,512]{3,2,1,0:T(8,128)}, f32[5,128,128]{2,1,0:T(8,128)S(1)}) custom-call(s32[2]{0:T(128)S(1)} %pad_add_fusion.place_ref, s32[1,32]{1,0:T(1,128)S(1)} %bitcast.7, bf16[2,128,256]{2,1,0:T(8,128)(2,1)S(1)} %copy-done.1, f32[1,512]{1,0:T(1,128)S(1)} %bitcast.6, ...), custom_call_target="tpu_custom_call", output_to_operand_aliasing={{0}: (9, {})} | custom-call | tf_op jit(solution)/shard_map/put_filtered/pallas_call | solution.py:545
  43.2 0.0 collective-permute-done.4.refs_1_
  43.2 1.9 %finish_plane.1 = f32[5,16,128,512]{3,2,1,0:T(8,128)} custom-call(s32[2]{0:T(128)S(1)} %pad_add_fusion.place_ref, f32[16]{0:T(128)S(1)} %copy-done.5, s32[1,32]{1,0:T(1,128)S(1)} %bitcast.8, bf16[2,128,256]{2,1,0:T(8,128)(2,1)S(1)} %copy-done.1, f32[5,128,512]{2,1,0:T(8,128)S(1)} %collective-permute-done.flux_ref, ...), custom_call_target="tpu_custom_call", output_to_operand_aliasing={{}: (9, {})} | custom-call | tf_op jit(solution)/shard_map/finish_plane/pallas_call | solution.py:661
  (8 shorter events, 0.0 us)
Async XLA Ops:
  0.1 9.1 %copy-start = (f32[5,16,128,512]{3,2,1,0:T(8,128)S(1)}, f32[5,16,128,512]{3,2,1,0:T(8,128)}, u32[]{:S(2)}) copy-start(f32[5,16,128,512]{3,2,1,0:T(8,128)} %state_ref.5) | copy-start | bytes 62914564
  2.9 6.3 %collective-permute-start.1 = (f32[5,128,512]{2,1,0:T(8,128)S(1)}, f32[5,128,512]{2,1,0:T(8,128)S(1)}, u32[]{:S(2)}, u32[]{:S(2)}) collective-permute-start(f32[5,128,512]{2,1,0:T(8,128)S(1)} %get-tuple-element.17), channel_id=1, source_target_pairs={{2,0},{0,2},{6,4},{4,6},{10,8},{8,10},{14,12},{12,14},{18,16},{16,... | collective-permute-start | bytes 3932168 | tf_op jit(solution)/shard_map/ppermute | solution.py:714
  3.0 33.3 %collective-permute-start = (f32[5,128,512]{2,1,0:T(8,128)S(1)}, f32[5,128,512]{2,1,0:T(8,128)S(1)}, u32[]{:S(2)}, u32[]{:S(2)}) collective-permute-start(f32[5,128,512]{2,1,0:T(8,128)S(1)} %get-tuple-element.16), channel_id=1, source_target_pairs={{2,4},{6,8},{10,12},{14,16},{18,20},{22,24},{26,28},{4,2},{8,6},{1... | collective-permute-start | bytes 3932168 | tf_op jit(solution)/shard_map/ppermute | solution.py:713
  7.7 9.6 %collective-permute-start.2 = (f32[2,5,16,512]{3,2,1,0:T(8,128)S(1)}, f32[2,5,16,512]{3,2,1,0:T(8,128)S(1)}, u32[]{:S(2)}, u32[]{:S(2)}) collective-permute-start(f32[2,5,16,512]{3,2,1,0:T(8,128)S(1)} %get-tuple-element.19), channel_id=1, source_target_pairs={{0,1},{1,0},{2,3},{3,2},{4,5},{5,4},{6,7},{7,6},{8,9},{9,8},{10,11... | collective-permute-start | bytes 983048 | tf_op jit(solution)/shard_map/ppermute | solution.py:710
  9.2 9.1 %copy-start.3 = (f32[5,512]{1,0:T(8,128)S(1)}, f32[5,512]{1,0:T(8,128)}, u32[]{:S(2)}) copy-start(f32[5,512]{1,0:T(8,128)} %target_ref.3) | copy-start | bytes 30724
  9.2 9.1 %copy-start.4 = (f32[512]{0:T(512)S(1)}, f32[512]{0:T(512)}, u32[]{:S(2)}) copy-start(f32[512]{0:T(512)} %param.12) | copy-start | bytes 6148
  9.2 9.1 %copy-start.5 = (f32[16]{0:T(128)S(1)}, f32[16]{0:T(128)}, u32[]{:S(2)}) copy-start(f32[16]{0:T(128)} %scale_ref.7) | copy-start | bytes 196
  17.4 21.2 %collective-permute-start.3 = (f32[1304,128]{1,0:T(8,128)S(1)}, f32[1304,128]{1,0:T(8,128)S(1)}, u32[]{:S(2)}, u32[]{:S(2)}) collective-permute-start(f32[1304,128]{1,0:T(8,128)S(1)} %gate.1.refs_0_), channel_id=1, source_target_pairs={{0,1},{1,0},{2,3},{3,2},{4,5},{5,4},{6,7},{7,6},{8,9},{9,8},{10,11... | collective-permute-start | bytes 2002952 | tf_op jit(solution)/shard_map/ppermute | solution.py:710
  18.3 18.0 %copy-start.2 = (bf16[2,128,256]{2,1,0:T(8,128)(2,1)S(1)}, bf16[2,128,256]{2,1,0:T(8,128)(2,1)}, u32[]{:S(2)}) copy-start(bf16[2,128,256]{2,1,0:T(8,128)(2,1)} %constant.19.clone.table_ref) | copy-start | bytes 393220
  18.3 20.3 %copy-start.1 = (bf16[2,128,256]{2,1,0:T(8,128)(2,1)S(1)}, bf16[2,128,256]{2,1,0:T(8,128)(2,1)}, u32[]{:S(2)}) copy-start(bf16[2,128,256]{2,1,0:T(8,128)(2,1)} %constant.21.clone.table_ref) | copy-start | bytes 393220
  18.3 20.3 %copy-start.6 = (s32[32]{0:T(128)S(1)}, s32[32]{0:T(128)}, u32[]{:S(2)}) copy-start(s32[32]{0:T(128)} %param.14) | copy-start | bytes 388
  37.2 6.0 %collective-permute-start.4 = (f32[136,128]{1,0:T(8,128)S(1)}, f32[136,128]{1,0:T(8,128)S(1)}, u32[]{:S(2)}, u32[]{:S(2)}) collective-permute-start(f32[136,128]{1,0:T(8,128)S(1)} %outer_modes.1.refs_0_), channel_id=1, source_target_pairs={{0,1},{1,0},{2,3},{3,2},{4,5},{5,4},{6,7},{7,6},{8,9},{9,8},{10,11... | collective-permute-start | bytes 208904 | tf_op jit(solution)/shard_map/ppermute | solution.py:710

commit v5 on v4

--- a/solution.py
+++ b/solution.py
@@ -25,6 +25,10 @@
     return pltpu.CompilerParams(
         dimension_semantics=("arbitrary",) * steps, vmem_limit_bytes=limit * MIB
     )
+
+
+def place():
+    return lax.rem(lax.axis_index("gx"), 2), lax.axis_index("az")
 
 
 def stored(x):
@@ -93,114 +97,138 @@
     return result
 
 
-def edge_kernel(place_ref, state_ref, edge_ref, far_flux_ref, near_flux_ref, row_ref, plane_ref, row_sem, plane_sem):
+PARTS = 2
+
+
+def plane_copies(state_ref, plane, plane_ref, sem):
+    rows = state_ref.shape[2] // PARTS
+    return [
+        pltpu.make_async_copy(
+            state_ref.at[:, plane, pl.ds(part * rows, rows)], plane_ref.at[:, pl.ds(part * rows, rows)], sem.at[part]
+        )
+        for part in range(PARTS)
+    ]
+
+
+def edge_kernel(
+    state_ref, scale_ref, edge_ref, first_ref, rest_ref, near_ref, factor_ref, row_ref, far_plane_ref, near_plane_ref,
+    held_ref, row_sem, plane_sem, held_sem,
+):
     _, planes, columns, cycles = state_ref.shape
-    odd = place_ref[0]
+    odd, _ = place()
+    scales = pltpu.make_async_copy(scale_ref, held_ref, held_sem.at[0])
     ends = [
         pltpu.make_async_copy(
             state_ref.at[:, :, pl.ds(side * (columns - 1), 1)], row_ref.at[side], row_sem.at[side]
         )
         for side in range(2)
     ]
-    wholes = [
-        pltpu.make_async_copy(
-            state_ref.at[:, away * (planes - 1), pl.ds(part * (columns // 2), columns // 2)],
-            plane_ref.at[side, :, pl.ds(part * (columns // 2), columns // 2)],
-            plane_sem.at[side, part],
-        )
-        for side, away in enumerate((odd, 1 - odd))
-        for part in range(2)
-    ]
-    for copy in ends + wholes:
+    far = plane_copies(state_ref, odd * (planes - 1), far_plane_ref, plane_sem.at[0])
+    near = plane_copies(state_ref, (1 - odd) * (planes - 1), near_plane_ref, plane_sem.at[1])
+    for copy in far + near + ends + [scales]:
         copy.start()
+    rows = columns // PARTS
+    for part, copy in enumerate(far):
+        copy.wait()
+        cut = slice(part * rows, (part + 1) * rows)
+        flux = axial_flux([far_plane_ref[f, cut] for f in range(5)])
+        for f in range(5):
+            first_ref[f, cut] = flux[f][:, :LANES]
+            rest_ref[f, cut] = flux[f][:, LANES:]
+    for part, copy in enumerate(near):
+        copy.wait()
+        cut = slice(part * rows, (part + 1) * rows)
+        flux = axial_flux([near_plane_ref[f, cut] for f in range(5)])
+        for f in range(5):
+            near_ref[f, cut] = flux[f]
     for copy in ends:
         copy.wait()
     for side in range(2):
         flux = swirl_flux([row_ref[1 - side, f, :, 0, :] for f in range(5)])
         for f in range(5):
             edge_ref[side, f] = flux[f]
-    half = columns // 2
-    for side, flux_ref in enumerate((far_flux_ref, near_flux_ref)):
-        for part in range(2):
-            wholes[2 * side + part].wait()
-            cut = slice(part * half, (part + 1) * half)
-            flux = axial_flux([plane_ref[side, f, cut] for f in range(5)])
-            for f in range(5):
-                flux_ref[f, cut] = flux[f]
-
-
-def edge_cells(place, state):
+    scales.wait()
+    for plane in range(planes):
+        factor_ref[plane] = jnp.full((8, LANES), (0.5 * time_step) * held_ref[plane], jnp.float32)
+
+
+def edge_cells(state, scale):
     _, planes, columns, cycles = state.shape
-    flux = pltpu.VMEM((5, columns, cycles), jnp.float32)
+    plane = pltpu.VMEM((5, columns, cycles), jnp.float32)
     return pl.pallas_call(
         edge_kernel,
-        in_specs=[SMEM_SPEC, HBM_SPEC],
-        out_specs=[VMEM_SPEC] * 3,
+        in_specs=[HBM_SPEC, HBM_SPEC],
+        out_specs=[VMEM_SPEC] * 5,
         scratch_shapes=[
             pltpu.VMEM((2, 5, planes, 1, cycles), jnp.float32),
-            pltpu.VMEM((2, 5, columns, cycles), jnp.float32),
+            plane,
+            plane,
+            pltpu.SMEM(scale.shape, jnp.float32),
             pltpu.SemaphoreType.DMA((2,)),
-            pltpu.SemaphoreType.DMA((2, 2)),
+            pltpu.SemaphoreType.DMA((2, PARTS)),
+            pltpu.SemaphoreType.DMA((1,)),
         ],
         out_shape=[
             pltpu.VMEM((2, 5, planes, cycles), jnp.float32),
-            flux,
-            flux,
+            pltpu.VMEM((5, columns, LANES), jnp.float32),
+            pltpu.VMEM((5, columns, cycles - LANES), jnp.float32),
+            plane,
+            pltpu.VMEM((planes, 8, LANES), jnp.float32),
         ],
-        compiler_params=pltpu.CompilerParams(vmem_limit_bytes=8 * MIB),
+        compiler_params=pltpu.CompilerParams(vmem_limit_bytes=6 * MIB),
         name="edge_cells",
-    )(place, state)
-
-
-def gate_kernel(sums_ref, *refs):
-    refs[-1][0:8] = sums_ref[0:8]
-
-
-def gate(sums, after):
+    )(stored(state), stored(scale))
+
+
+def gate_kernel(flux_ref, after_ref, out_ref):
+    out_ref[0, 0:8, 0:LANES] = flux_ref[0, 0:8, 0:LANES]
+
+
+def gate(flux, after):
     return pl.pallas_call(
         gate_kernel,
-        in_specs=[VMEM_SPEC] * (1 + len(after)),
+        in_specs=[VMEM_SPEC, VMEM_SPEC],
         out_specs=VMEM_SPEC,
-        out_shape=pltpu.VMEM(sums.shape, jnp.float32),
+        out_shape=pltpu.VMEM(flux.shape, jnp.float32),
         input_output_aliases={0: 0},
         compiler_params=pltpu.CompilerParams(vmem_limit_bytes=1 * MIB),
         name="gate",
-    )(resident(sums), *(resident(part) for part in after))
+    )(resident(flux), resident(after))
 
 
 def modes_kernel(
-    place_ref, scale_ref, level_ref, inv_dr_ref, target_ref, table_ref, edge_ref, near_ref, state_ref,
-    sums_ref, tile_ref, behind_ref, rows_ref, axial_ref, swirl_ref, base_ref, split_ref, *, cells, chunk,
+    level_ref, inv_dr_ref, target_ref, factor_ref, table_ref, edge_ref, state_ref, *refs,
+    cells, chunk, pick, steps, ends,
 ):
-    step = pl.program_id(0)
-    steps = pl.num_programs(0)
+    sums_ref, tile_ref, behind_ref, rows_ref, axial_ref, swirl_ref, base_ref, split_ref = refs[-8:]
+    step = pick(pl.program_id(0))
     _, planes, columns, cycles = state_ref.shape
-    odd = place_ref[0]
+    odd, sector = place()
     lane = lax.broadcasted_iota(jnp.int32, (chunk, LANES), 1)
 
-    @pl.when(step == 0)
+    @pl.when(pl.program_id(0) == 0)
     def _():
         fill_rows(rows_ref, inv_dr_ref[...], 0, cycles, cells)
         for f in range(5):
-            axial_ref[0, f] = jnp.where(odd == 1, near_ref[f, :, :LANES], 0.0)
             for i in range(PACK):
                 swirl_ref[i, f, 0:8] = jnp.zeros((8, LANES), jnp.float32)
                 swirl_ref[i, f, columns + 8 : columns + 16] = jnp.zeros((8, LANES), jnp.float32)
 
-    @pl.when(step > 0)
-    def _():
-        for f in range(5):
-            axial_ref[0, f] = axial_ref[PACK, f]
-
     def load(plane, start):
         return [state_ref[f, plane, pl.ds(start, chunk), :LANES] for f in range(5)]
 
-    def following(start):
-        flux = axial_flux(load(jnp.minimum(step * PACK + PACK, planes - 1), start))
-        final = step == steps - 1
-        for f in range(5):
-            halo = jnp.where(odd == 0, near_ref[f, pl.ds(start, chunk), :LANES], 0.0)
-            axial_ref[PACK + 1, f, pl.ds(start, chunk)] = jnp.where(final, halo, flux[f])
+    def beside(start):
+        for slot, plane, at_end, use in (
+            (0, step * PACK - 1, step == 0, odd == 1),
+            (PACK + 1, step * PACK + PACK, step == steps - 1, odd == 0),
+        ):
+            flux = axial_flux(load(jnp.clip(plane, 0, planes - 1), start))
+            for f in range(5):
+                value = flux[f]
+                if ends:
+                    halo = jnp.where(use, refs[0][f, pl.ds(start, chunk), :LANES], refs[1][f, pl.ds(start, chunk)])
+                    value = jnp.where(at_end, halo, value)
+                axial_ref[slot, f, pl.ds(start, chunk)] = value
 
     def wide(row):
         return jnp.broadcast_to(row[None], (chunk // 8, 8, LANES)).reshape(chunk, LANES)
@@ -229,7 +257,7 @@
             result = jnp.where(lane[:rows] // CYCLE == i, pltpu.roll(parts[i], i * CYCLE, 1), result)
         return result
 
-    factor = [(0.5 * time_step) * scale_ref[step * PACK + i] for i in range(PACK)]
+    factor = [wide(factor_ref[step * PACK + i]) for i in range(PACK)]
     total = [jnp.zeros((8, LANES), jnp.float32)] * 5
 
     def second(start):
@@ -255,18 +283,18 @@
 
     for start in range(0, columns, chunk):
         first(start)
-        following(start)
+        beside(start)
         if start:
             second(start - chunk)
     second(columns - chunk)
     for f in range(5):
-        sums = jnp.dot(table_ref[0], split_ref[f], preferred_element_type=jnp.float32)
+        sums = jnp.dot(table_ref[sector], split_ref[f], preferred_element_type=jnp.float32)
         half = sums.shape[0] // 2
         start_row = packed([swirl_ref[i, f, 8:16] for i in range(PACK)], 8)[0:1]
         end_row = packed([swirl_ref[i, f, columns : columns + 8] for i in range(PACK)], 8)[7:8]
         group = step * 5 + f
         sums_ref[pl.ds(pl.multiple_of(group * half, half), half), :] = (
-            sums[:half] + sums[half:] + (edge_ref[0, 1] * end_row - edge_ref[0, 0] * start_row)
+            sums[:half] + sums[half:] + (edge_ref[sector, 1] * end_row - edge_ref[sector, 0] * start_row)
         )
         mean = total[f].sum(axis=0, keepdims=True) + (end_row - start_row)
         sums_ref[pl.ds(steps * 5 * half + group, 1), :] = mean
@@ -277,40 +305,45 @@
     return groups * half + -(-groups // 8) * 8
 
 
-def inner_modes(place, scale, sponge, inv_dr, target, table, edge, near, state, cells):
+def inner_modes(sponge, inv_dr, target, factor, table, edge, state, cells, near=None, far=None, after=None, done=()):
     _, planes, columns, cycles = state.shape
     half = table.shape[1] // 2
-    chunk = min(32, columns)
-    whole = lambda *shape: pl.BlockSpec(shape, lambda g, place: (0,) * len(shape))
+    chunk = min(16, columns)
+    steps = planes // PACK
+    ends = bool(done)
+    pick = (lambda g: g * (steps - 1)) if ends else (lambda g: g + 1)
+    whole = lambda *shape: pl.BlockSpec(shape, lambda g: (0,) * len(shape))
     tile = pltpu.VMEM((5, planes, columns, LANES), jnp.float32)
+    extra = [resident(part) for part in ((near, far, after) + tuple(done) if ends else ())]
     return pl.pallas_call(
-        functools.partial(modes_kernel, cells=cells, chunk=chunk),
-        grid_spec=pltpu.PrefetchScalarGridSpec(
-            num_scalar_prefetch=1,
-            grid=(planes // PACK,),
-            in_specs=[
-                SMEM_SPEC,
-                pl.BlockSpec((PACK, columns, LANES), lambda g, place: (g, 0, 0)),
-                whole(1, LANES),
-                whole(5, LANES),
-                pl.BlockSpec((1,) + table.shape[1:], lambda g, place: (place[1], 0, 0)),
-                pl.BlockSpec((1,) + edge.shape[1:], lambda g, place: (place[1], 0, 0, 0)),
-                VMEM_SPEC,
-                VMEM_SPEC,
-            ],
-            out_specs=[VMEM_SPEC] * 3,
-            scratch_shapes=[
-                pltpu.VMEM((3, 8, LANES), jnp.float32),
-                pltpu.VMEM((PACK + 2, 5, columns, LANES), jnp.float32),
-                pltpu.VMEM((PACK, 5, columns + 16, LANES), jnp.float32),
-                pltpu.VMEM((PACK, 5, columns, LANES), jnp.float32),
-                pltpu.VMEM((5, 2 * columns, LANES), jnp.bfloat16),
-            ],
-        ),
+        functools.partial(modes_kernel, cells=cells, chunk=chunk, pick=pick, steps=steps, ends=ends),
+        grid=(2 if ends else steps - 2,),
+        in_specs=[
+            pl.BlockSpec((PACK, columns, LANES), lambda g: (pick(g), 0, 0)),
+            whole(1, LANES),
+            whole(5, LANES),
+            VMEM_SPEC,
+            whole(*table.shape),
+            whole(*edge.shape),
+            VMEM_SPEC,
+        ]
+        + [VMEM_SPEC] * len(extra),
+        out_specs=[VMEM_SPEC, VMEM_SPEC, VMEM_SPEC],
+        scratch_shapes=[
+            pltpu.VMEM((3, 8, LANES), jnp.float32),
+            pltpu.VMEM((PACK + 2, 5, columns, LANES), jnp.float32),
+            pltpu.VMEM((PACK, 5, columns + 16, LANES), jnp.float32),
+            pltpu.VMEM((PACK, 5, columns, LANES), jnp.float32),
+            pltpu.VMEM((5, 2 * columns, LANES), jnp.bfloat16),
+        ],
         out_shape=[pltpu.VMEM((mode_rows(planes, half), LANES), jnp.float32), tile, tile],
-        compiler_params=params(1, 12),
-        name="inner_modes",
-    )(place, *(stored(part) for part in (scale, sponge, inv_dr, target, table, edge)), resident(near), resident(state))
+        input_output_aliases={10 + k: k for k in range(3)} if ends else {},
+        compiler_params=params(1, 8),
+        name="end_modes" if ends else "middle_modes",
+    )(
+        *(stored(part) for part in (sponge, inv_dr, target)), resident(factor), stored(table), stored(edge),
+        resident(state), *extra,
+    )
 
 
 IN_SLOTS = 3
@@ -318,7 +351,7 @@
 
 
 def update_kernel(
-    place_ref, scale_ref, inv_dr_ref, target_ref, near_ref, halo_ref, behind_ref, state_ref, level_ref,
+    inv_dr_ref, target_ref, factor_ref, near_ref, halo_ref, behind_ref, state_ref, level_ref,
     out_ref, ahead_ref, kept_ref, rows_ref, levels_ref, result_ref, axial_even_ref, axial_odd_ref, swirl_even_ref,
     swirl_odd_ref, base_ref, level_sem, result_sem, *, cells, chunk, unroll,
 ):
@@ -326,7 +359,7 @@
     swirl_refs = (swirl_even_ref, swirl_odd_ref)
     planes, columns, cycles = level_ref.shape
     tiles = cycles // LANES - 1
-    odd = place_ref[0]
+    odd, _ = place()
     rest = pl.ds(LANES, cycles - LANES)
     lane = lax.broadcasted_iota(jnp.int32, (chunk, LANES), 1)
 
@@ -366,7 +399,8 @@
 
     def finish(plane, parity, start, k, axial):
         rows = pl.ds(start, chunk)
-        factor = (0.5 * time_step) * scale_ref[jnp.maximum(plane - 1, 0)]
+        factor = factor_ref[jnp.maximum(plane - 1, 0)]
+        factor = jnp.broadcast_to(factor[None], (chunk // 8, 8, LANES)).reshape(chunk, LANES)
         axial_ref, swirl_ref = axial_refs[parity], swirl_refs[1 - parity]
         slot = lax.rem(plane + OUT_SLOTS - 1, OUT_SLOTS)
         for f in range(5):
@@ -468,13 +502,13 @@
         store(plane).wait()
 
 
-def bulk_update(place, scale, state, sponge, inv_dr, target, near, halo, behind, cells, chunk=8, unroll=16):
+def bulk_update(state, sponge, inv_dr, target, factor, near, halo, behind, cells, chunk=8, unroll=16):
     _, planes, columns, cycles = state.shape
     tiles = cycles // LANES - 1
     width = cycles - LANES
     return pl.pallas_call(
         functools.partial(update_kernel, cells=cells, chunk=chunk, unroll=unroll),
-        in_specs=[SMEM_SPEC, SMEM_SPEC, VMEM_SPEC, VMEM_SPEC, VMEM_SPEC, VMEM_SPEC, VMEM_SPEC, VMEM_SPEC, HBM_SPEC],
+        in_specs=[VMEM_SPEC] * 7 + [HBM_SPEC],
         out_specs=[HBM_SPEC, VMEM_SPEC, VMEM_SPEC],
         scratch_shapes=[
             pltpu.VMEM((3, 8, width), jnp.float32),
@@ -493,118 +527,96 @@
             pltpu.VMEM((5, planes, columns, LANES), jnp.float32),
             pltpu.VMEM((5, columns, width), jnp.float32),
         ],
-        compiler_params=pltpu.CompilerParams(vmem_limit_bytes=13 * MIB),
-        input_output_aliases={6: 1},
+        compiler_params=pltpu.CompilerParams(vmem_limit_bytes=10 * MIB),
+        input_output_aliases={5: 1},
         name="bulk_update",
-    )(place, scale, inv_dr, target, resident(near), resident(halo), resident(behind), resident(state), stored(sponge))
+    )(inv_dr, target, resident(factor), resident(near), resident(halo), resident(behind), resident(state), stored(sponge))
 
 
 def filter_kernel(
-    place_ref, cutoff_ref, table_ref, inv_dr_ref, tile_ref, ahead_ref, halo_ref, *refs, cells, cycles
+    cutoff_ref, table_ref, inv_dr_ref, factor_ref, tile_ref, ahead_ref, halo_ref, flux_ref, rest_ref, *refs, cells,
 ):
-    *sums, state_ref, out_ref, kept_ref, split_ref = refs
-    step = pl.program_id(0)
-    steps = pl.num_programs(0)
+    *sums, state_ref, out_ref, result_ref, outer_ref, split_ref, result_sem, outer_sem = refs
+    _, planes, columns, cycles = out_ref.shape
+    steps = planes // PACK
     half = table_ref.shape[2] // 4
-    columns = out_ref.shape[2]
+    odd, sector = place()
+    table = table_ref[sector]
+
+    factor = factor_ref[odd * (planes - 1)][0:1]
+    factor = jnp.where(odd == 1, -factor, factor)
+    for f in range(5):
+        for k in range(cycles // LANES - 1):
+            cut = slice(k * LANES, (k + 1) * LANES)
+            outer_ref[f, :, cut] = rest_ref[f, :, cut] + factor * flux_ref[f, :, cut]
+    outer = pltpu.make_async_copy(
+        outer_ref, out_ref.at[:, odd * (planes - 1), :, pl.ds(LANES, cycles - LANES)], outer_sem.at[0]
+    )
+    outer.start()
+
     weight = mode_weight(cutoff_ref[...], half, cells)
     lane = lax.broadcasted_iota(jnp.int32, (columns, LANES), 1)
     spacing = 4.0 / cycles
     edge = 1.0 + spacing * (LANES - 1)
-    up = (0.5 * time_step) * inv_dr_ref[...] * ((edge + spacing) / edge)
+    up = (0.5 * time_step) * inv_dr_ref[0:1, :LANES] * ((edge + spacing) / edge)
     up = jnp.where(lane == LANES - 1, up, 0.0)
     cycle = lax.broadcasted_iota(jnp.int32, (1, LANES), 1)
     around = (time_step * cells / (4.0 * math.pi)) / (1.0 + spacing * cycle.astype(jnp.float32))
     around = jnp.where(cycle < CYCLE, 0.0, around)
-    for f in range(5):
-        group = step * 5 + f
-        values = turn_back(
-            sums, pl.multiple_of(group * half, half), steps * 5 * half + group, weight, table_ref[0],
-            split_ref.at[f], cells,
+
+    def put(step, f):
+        return pltpu.make_async_copy(
+            result_ref.at[step % 2, f],
+            out_ref.at[f, pl.ds(step * PACK, PACK), :, pl.ds(0, LANES)],
+            result_sem.at[step % 2, f],
         )
-        for i in range(PACK):
-            turned = values if i == 0 else pltpu.roll(values, LANES - i * CYCLE, 1)
-            plane = step * PACK + i
-            out_ref[f, i] = jnp.where(lane < CYCLE, turned, tile_ref[f, plane] - up * ahead_ref[f, plane])
-            low = halo_ref[0, f, pl.ds(plane, 1), :][:, :LANES]
-            high = halo_ref[1, f, pl.ds(plane, 1), :][:, :LANES]
-            out_ref[f, i, 0:1] = out_ref[f, i, 0:1] + around * low
-            out_ref[f, i, columns - 1 : columns] = out_ref[f, i, columns - 1 : columns] - around * high
-
-    def keep(i):
-        for f in range(5):
-            kept_ref[f] = out_ref[f, i]
-
-    odd = place_ref[0]
-    pl.when(jnp.logical_and(step == 0, odd == 0))(lambda: keep(0))
-    pl.when(jnp.logical_and(step == steps - 1, odd == 1))(lambda: keep(PACK - 1))
-
-
-def put_filtered(place, cutoff, table, inv_dr, tile, ahead, halo, sums, updated, cells):
+
+    for step in range(steps):
+        for f in range(5):
+            group = step * 5 + f
+            values = turn_back(
+                sums, group * half, steps * 5 * half + group, weight, table, split_ref.at[group % 2], cells
+            )
+            if step >= 2:
+                put(step - 2, f).wait()
+            for i in range(PACK):
+                turned = values if i == 0 else pltpu.roll(values, LANES - i * CYCLE, 1)
+                plane = step * PACK + i
+                value = tile_ref[f, plane] - up * ahead_ref[f, plane]
+                value = jnp.where(lane < CYCLE, turned, value)
+                low = value[0:1] + around * halo_ref[0, f, plane : plane + 1, :LANES]
+                high = value[columns - 1 : columns] - around * halo_ref[1, f, plane : plane + 1, :LANES]
+                result_ref[step % 2, f, i] = value
+                result_ref[step % 2, f, i, 0:1] = low
+                result_ref[step % 2, f, i, columns - 1 : columns] = high
+            put(step, f).start()
+    for step in range(max(steps - 2, 0), steps):
+        for f in range(5):
+            put(step, f).wait()
+    outer.wait()
+
+
+def put_filtered(cutoff, table, inv_dr, factor, tile, ahead, halo, flux, rest, sums, updated, cells):
     _, planes, columns, cycles = updated.shape
     return pl.pallas_call(
-        functools.partial(filter_kernel, cells=cells, cycles=cycles),
-        grid_spec=pltpu.PrefetchScalarGridSpec(
-            num_scalar_prefetch=1,
-            grid=(planes // PACK,),
-            in_specs=[
-                pl.BlockSpec(cutoff.shape, lambda g, place: (0, 0)),
-                pl.BlockSpec((1,) + table.shape[1:], lambda g, place: (place[1], 0, 0)),
-                pl.BlockSpec((1, LANES), lambda g, place: (0, 0)),
-                VMEM_SPEC,
-                VMEM_SPEC,
-                VMEM_SPEC,
-            ]
-            + [VMEM_SPEC] * len(sums)
-            + [HBM_SPEC],
-            out_specs=[pl.BlockSpec((5, PACK, columns, LANES), lambda g, place: (0, g, 0, 0)), VMEM_SPEC],
-            scratch_shapes=[pltpu.VMEM((5, table.shape[2], LANES), jnp.bfloat16)],
-        ),
-        out_shape=[
-            jax.ShapeDtypeStruct(updated.shape, jnp.float32),
-            pltpu.VMEM((5, columns, LANES), jnp.float32),
+        functools.partial(filter_kernel, cells=cells),
+        in_specs=[VMEM_SPEC] * (9 + len(sums)) + [HBM_SPEC],
+        out_specs=HBM_SPEC,
+        scratch_shapes=[
+            pltpu.VMEM((2, 5, PACK, columns, LANES), jnp.float32),
+            pltpu.VMEM((5, columns, cycles - LANES), jnp.float32),
+            pltpu.VMEM((2, table.shape[2], LANES), jnp.bfloat16),
+            pltpu.SemaphoreType.DMA((2, 5)),
+            pltpu.SemaphoreType.DMA((1,)),
         ],
-        input_output_aliases={7 + len(sums): 0},
-        compiler_params=params(1, 12),
+        out_shape=jax.ShapeDtypeStruct(updated.shape, jnp.float32),
+        input_output_aliases={9 + len(sums): 0},
+        compiler_params=pltpu.CompilerParams(vmem_limit_bytes=6 * MIB),
         name="put_filtered",
-    )(place, cutoff, table, inv_dr, resident(tile), resident(ahead), resident(halo),
-      *(resident(part) for part in sums), updated)
-
-
-def outer_kernel(place_ref, scale_ref, table_ref, flux_ref, after_ref, sums_ref, split_ref):
-    odd = place_ref[0]
-    planes = scale_ref.shape[0]
-    columns = flux_ref.shape[1]
-    half = table_ref.shape[1] // 2
-    factor = (0.5 * time_step) * scale_ref[odd * (planes - 1)]
-    factor = jnp.where(odd == 1, -factor, factor)
-    lane = lax.broadcasted_iota(jnp.int32, (columns, LANES), 1)
-    for group in range(2):
-        value = jnp.zeros((columns, LANES), jnp.float32)
-        for i in range(PACK):
-            if group * PACK + i < 5:
-                part = factor * flux_ref[group * PACK + i, :, :LANES]
-                part = part if i == 0 else pltpu.roll(part, i * CYCLE, 1)
-                value = jnp.where(lane // CYCLE == i, part, value)
-        high = value.astype(jnp.bfloat16)
-        split_ref[group, :columns] = high
-        split_ref[group, columns:] = (value - high.astype(jnp.float32)).astype(jnp.bfloat16)
-        sums = jnp.dot(table_ref[place_ref[1]], split_ref[group], preferred_element_type=jnp.float32)
-        sums_ref[group * half : (group + 1) * half] = sums[:half] + sums[half:]
-        sums_ref[2 * half + group : 2 * half + group + 1] = value.sum(axis=0, keepdims=True)
-
-
-def outer_modes(place, scale, table, flux, after):
-    half = table.shape[1] // 2
-    return pl.pallas_call(
-        outer_kernel,
-        in_specs=[SMEM_SPEC, SMEM_SPEC, VMEM_SPEC, VMEM_SPEC, VMEM_SPEC],
-        out_specs=VMEM_SPEC,
-        scratch_shapes=[pltpu.VMEM((2, 2 * flux.shape[1], LANES), jnp.bfloat16)],
-        out_shape=pltpu.VMEM((2 * half + 8, LANES), jnp.float32),
-        compiler_params=pltpu.CompilerParams(vmem_limit_bytes=4 * MIB),
-        name="outer_modes",
-    )(place, scale, table, resident(flux), resident(after))
+    )(
+        cutoff, table, inv_dr, resident(factor), resident(tile), resident(ahead), resident(halo), resident(flux),
+        resident(rest), *(resident(part) for part in sums), updated,
+    )
 
 
 def turn_back(sums, base, mean_row, weight, table, split_ref, cells):
@@ -630,53 +642,6 @@
     return jnp.where(mode <= jnp.concatenate([cutoff] * PACK, axis=1), 2.0 / cells, 0.0)
 
 
-def finish_kernel(place_ref, scale_ref, cutoff_ref, table_ref, flux_ref, first_ref, rest_ref, *refs, cells):
-    *sums, state_ref, out_ref, result_ref, split_ref, result_sem = refs
-    odd = place_ref[0]
-    planes = scale_ref.shape[0]
-    columns = flux_ref.shape[1]
-    half = table_ref.shape[2] // 4
-    plane = odd * (planes - 1)
-    factor = (0.5 * time_step) * scale_ref[plane]
-    factor = jnp.where(odd == 1, -factor, factor)
-    lane = lax.broadcasted_iota(jnp.int32, (columns, LANES), 1)
-    weight = mode_weight(cutoff_ref[...], half, cells)
-    table = table_ref[place_ref[1]]
-    copies = []
-    for f in range(5):
-        group, i = f // PACK, f % PACK
-        if i == 0:
-            values = turn_back(sums, group * half, 2 * half + group, weight, table, split_ref.at[group], cells)
-        turned = values if i == 0 else pltpu.roll(values, LANES - i * CYCLE, 1)
-        flux = factor * flux_ref[f]
-        result_ref[f, :, :LANES] = first_ref[f] + jnp.where(lane < CYCLE, turned, flux[:, :LANES])
-        result_ref[f, :, LANES:] = rest_ref[f] + flux[:, LANES:]
-        copies.append(pltpu.make_async_copy(result_ref.at[f], out_ref.at[f, plane], result_sem.at[f]))
-        copies[-1].start()
-    for copy in copies:
-        copy.wait()
-
-
-def finish_plane(place, scale, cutoff, table, flux, first, rest, sums, updated, cells):
-    return pl.pallas_call(
-        functools.partial(finish_kernel, cells=cells),
-        in_specs=[SMEM_SPEC, SMEM_SPEC] + [VMEM_SPEC] * (5 + len(sums)) + [HBM_SPEC],
-        out_specs=HBM_SPEC,
-        scratch_shapes=[
-            pltpu.VMEM(flux.shape, jnp.float32),
-            pltpu.VMEM((2, table.shape[2], LANES), jnp.bfloat16),
-            pltpu.SemaphoreType.DMA((5,)),
-        ],
-        out_shape=jax.ShapeDtypeStruct(updated.shape, jnp.float32),
-        input_output_aliases={7 + len(sums): 0},
-        compiler_params=pltpu.CompilerParams(vmem_limit_bytes=4 * MIB),
-        name="finish_plane",
-    )(
-        place, scale, cutoff, table, resident(flux), resident(first), resident(rest),
-        *(resident(part) for part in sums), updated,
-    )
-
-
 def mode_tables(cells, sectors):
     columns = cells // sectors
     mode = np.arange(1, cells // 8 + 1)
@@ -700,7 +665,6 @@
 def body(forward, inverse, edge, cells, state, sponge_level, inv_dx, inv_dr, target, cutoff):
     sectors = lax.axis_size("az")
     rows = lax.axis_size("gx")
-    place = jnp.stack([lax.rem(lax.axis_index("gx"), 2), lax.axis_index("az")]).astype(jnp.int32)
     cycles = state.shape[3]
     inv_dr = inv_dr.reshape(1, cycles)
     cutoff = cutoff.reshape(1, CYCLE)
@@ -709,25 +673,27 @@
     far_pairs = [(i, i + 1) for i in range(1, rows - 1, 2)] + [(i + 1, i) for i in range(1, rows - 1, 2)]
     shifted = lambda part, by: lax.ppermute(part, "az", [(i, (i + by) % sectors) for i in range(sectors)])
 
-    edges, far_flux, near_flux = edge_cells(place, stored(state))
-    far_flux = lax.ppermute(far_flux, "gx", far_pairs)
+    edges, far_first, far_rest, near_flux, factor = edge_cells(state, inv_dx)
+    far_first = lax.ppermute(far_first, "gx", far_pairs)
     near_flux = lax.ppermute(near_flux, "gx", near_pairs)
     if sectors == 2:
         halo = shifted(edges, 1)
     else:
         halo = jnp.stack([shifted(edges[0], 1), shifted(edges[1], sectors - 1)])
-    sums, tile, behind = inner_modes(
-        place, inv_dx, sponge_level, inv_dr, target, forward, edge, near_flux, state, cells
+    modes = functools.partial(
+        inner_modes, sponge_level, inv_dr, target, factor, forward, edge, state, cells
     )
-    sums = gate(sums, [halo])
+    middle = modes()
+    far_rest = lax.ppermute(gate(far_rest, middle[0]), "gx", far_pairs)
+    sums, tile, behind = modes(near=near_flux, far=far_first, after=halo, done=middle)
     others = [shifted(sums, by) for by in range(1, sectors)]
     updated, ahead, rest = bulk_update(
-        place, inv_dx, state, sponge_level, inv_dr, target, near_flux, halo, behind, cells
+        state, sponge_level, inv_dr, target, factor, near_flux, halo, behind, cells
     )
-    outer = outer_modes(place, inv_dx, forward, far_flux, rest)
-    outer = [outer] + [shifted(outer, by) for by in range(1, sectors)]
-    updated, first = put_filtered(place, cutoff, inverse, inv_dr, tile, ahead, halo, [sums, *others], updated, cells)
-    return finish_plane(place, inv_dx, cutoff, inverse, far_flux, first, rest, outer, updated, cells)
+    return put_filtered(
+        cutoff, inverse, inv_dr, factor, tile, ahead, halo, far_rest, rest, [sums, *others],
+        updated, cells,
+    )
 
 
 def solution(mesh):

time: 45.8 us -> 43.8 us (0.956); the launches traced: 45.1 us -> 43.6 us
  Pallas kernels: 35.2 us -> 31.9 us
  starting transfers between devices: 8.62 us -> 11.5 us
  waiting for transfers between devices: 1.06 us -> 0.01 us
    ppermute x1 -> x2, starting transfers between devices: 4.76 us -> 8.83 us  [the longest x1 4.89 us: body(): far_first = lax.ppermute(far_first, 'gx', far_pairs)]
    pallas_call x6 -> x5, Pallas kernels: 18.3 us -> 15.2 us  [the longest x2 9.2 us: inner_modes(): pl.pallas_call(functools.partial(modes_kernel, cells=cells, chunk=chunk,...]
    ppermute x3 -> x2, starting transfers between devices: 3.74 us -> 2.55 us  [body(): lax.ppermute(part, 'az', [(i, (i + by) % sectors) for i in range(sectors)])]
    ppermute x1 -> x2, waiting for transfers between devices: 1.05 us -> 0.01 us  [the longest x1 0.01 us: body(): far_first = lax.ppermute(far_first, 'gx', far_pairs)]
  transfers between devices with their start and end apart: 5 -> 5, of which waited for: 1 -> 0; matrix products, arithmetic and copies ran while one was open for 0% -> 0% of each run, Pallas kernels for 68% -> 60%
where the time goes in v5:
time: 43.8 us; the launch traced here: 43.6 us
  Pallas kernels  31.9 us (73%)
  starting transfers between devices  11.5 us (26%)
    pallas_call x1, Pallas kernels, bulk_update(): pl.pallas_call(functools.partial(update_kernel, cells=cells, chunk=chunk,...  16.8 us
    pallas_call x2, Pallas kernels, inner_modes(): pl.pallas_call(functools.partial(modes_kernel, cells=cells, chunk=chunk,...  9.2 us
    ppermute x1, starting transfers between devices, body(): far_first = lax.ppermute(far_first, 'gx', far_pairs)  4.89 us
    ppermute x1, starting transfers between devices, body(): far_rest = lax.ppermute(gate(far_rest, middle[0]), 'gx', far_pairs)  3.94 us
    pallas_call x1, Pallas kernels, put_filtered(): pl.pallas_call(functools.partial(filter_kernel, cells=cells), in_specs=[V...  3.81 us
    ppermute x2, starting transfers between devices, body(): lax.ppermute(part, 'az', [(i, (i + by) % sectors) for i in range(sectors)])  2.55 us
    pallas_call x1, Pallas kernels, edge_cells(): pl.pallas_call(edge_kernel, in_specs=[HBM_SPEC, HBM_SPEC], out_specs=[VME...  2.15 us
  transfers between devices with their start and end apart: 5, of which 0 were waited for; matrix products, arithmetic and copies ran while one was open for 0% of the time, Pallas kernels for 60%

profile of v5, /device:TPU:1, one launch (start us, length us, event | category | flops | bytes accessed | tf_op | source)
XLA Modules:
  0.0 43.6 jit_solution(7578624484863675468)
XLA Ops:
  0.0 0.0 copy-start
  0.0 2.1 %edge_cells.1 = (f32[2,5,16,512]{3,2,1,0:T(8,128)S(1)}, f32[5,128,128]{2,1,0:T(8,128)S(1)}, f32[5,128,384]{2,1,0:T(8,128)S(1)}, f32[5,128,512]{2,1,0:T(8,128)S(1)}, f32[16,8,128]{2,1,0:T(8,128)S(1)}) custom-call(f32[5,16,128,512]{3,2,1,0:T(8,128)} %state_ref.7, f32[16]{0:T(128)} %scale_ref.1), custom_call_target="tpu_custom_call" | custom-call | tf_op jit(solution)/shard_map/edge_cells/pallas_call | solution.py:158
  2.2 0.1 collective-permute-start
  2.3 4.9 %collective-permute-start.1 = (f32[5,128,128]{2,1,0:T(8,128)S(1)}, f32[5,128,128]{2,1,0:T(8,128)S(1)}, u32[]{:S(2)}, u32[]{:S(2)}) collective-permute-start(f32[5,128,128]{2,1,0:T(8,128)S(1)} %get-tuple-element.21), channel_id=1, source_target_pairs={{2,4},{6,8},{10,12},{14,16},{18,20},{22,24},{26,28},{4,2},{8,6},{1... | collective-permute-start | bytes 983048 | tf_op jit(solution)/shard_map/ppermute | solution.py:677
  7.2 1.3 %collective-permute-start.2 = (f32[2,5,16,512]{3,2,1,0:T(8,128)S(1)}, f32[2,5,16,512]{3,2,1,0:T(8,128)S(1)}, u32[]{:S(2)}, u32[]{:S(2)}) collective-permute-start(f32[2,5,16,512]{3,2,1,0:T(8,128)S(1)} %get-tuple-element.22), channel_id=1, source_target_pairs={{0,1},{1,0},{2,3},{3,2},{4,5},{5,4},{6,7},{7,6},{8,9},{9,8},{10,11... | collective-permute-start | bytes 983048 | tf_op jit(solution)/shard_map/ppermute | solution.py:674
  8.5 0.0 copy-done
  8.5 4.5 %middle_modes.1 = (f32[1304,128]{1,0:T(8,128)S(1)}, f32[5,16,128,128]{3,2,1,0:T(8,128)S(1)}, f32[5,16,128,128]{3,2,1,0:T(8,128)S(1)}) custom-call(s32[16,128,512]{2,1,0:T(8,128)} %level_ref.5, f32[1,512]{1,0:T(1,128)} %bitcast.2, f32[5,512]{1,0:T(8,128)} %target_ref.5, f32[16,8,128]{2,1,0:T(8,128)S(1)} %get-tuple-element.19.factor_ref, ...), custom_call_target="tpu_custom_call" | custom-call | tf_op jit(solution)/shard_map/middle_modes/pallas_call | solution.py:318
  13.0 3.9 %collective-permute-start.3 = (f32[5,128,384]{2,1,0:T(8,128)S(1)}, f32[5,128,384]{2,1,0:T(8,128)S(1)}, u32[]{:S(2)}, u32[]{:S(2)}) collective-permute-start(f32[5,128,384]{2,1,0:T(8,128)S(1)} %gate.1), channel_id=1, source_target_pairs={{2,4},{6,8},{10,12},{14,16},{18,20},{22,24},{26,28},{4,2},{8,6},{1... | collective-permute-start | bytes 2949128 | tf_op jit(solution)/shard_map/ppermute | solution.py:687
  17.0 0.0 collective-permute-done.1.refs_1_
  17.0 0.0 collective-permute-done.2.refs_2_.halo_ref
  17.0 0.0 collective-permute-done.refs_0_.near_ref
  17.0 0.0 copy-start.1
  17.0 0.0 copy-start.3
  17.0 4.7 %end_modes.1 = (f32[1304,128]{1,0:T(8,128)S(1)}, f32[5,16,128,128]{3,2,1,0:T(8,128)S(1)}, f32[5,16,128,128]{3,2,1,0:T(8,128)S(1)}) custom-call(s32[16,128,512]{2,1,0:T(8,128)} %level_ref.5, f32[1,512]{1,0:T(1,128)} %bitcast.3, f32[5,512]{1,0:T(8,128)} %target_ref.5, ...), custom_call_target="tpu_custom_call", output_to_operand_aliasing={{0}: (10, {}), {1}: (11, {}), {2}: (12, {})} | custom-call | tf_op jit(solution)/shard_map/end_modes/pallas_call | solution.py:318
  21.7 1.3 %collective-permute-start.4 = (f32[1304,128]{1,0:T(8,128)S(1)}, f32[1304,128]{1,0:T(8,128)S(1)}, u32[]{:S(2)}, u32[]{:S(2)}) collective-permute-start(f32[1304,128]{1,0:T(8,128)S(1)} %get-tuple-element.31.refs_0_), channel_id=1, source_target_pairs={{0,1},{1,0},{2,3},{3,2},{4,5},{5,4},{6,7},{7,6},{8,9},{9,8},{10,11... | collective-permute-start | bytes 2002952 | tf_op jit(solution)/shard_map/ppermute | solution.py:674
  23.0 0.0 copy-done.1
  23.0 0.0 copy-done.3
  23.0 0.0 copy-start.2
  23.0 16.8 %bulk_update.1 = (f32[5,16,128,512]{3,2,1,0:T(8,128)}, f32[5,16,128,128]{3,2,1,0:T(8,128)S(1)}, f32[5,128,384]{2,1,0:T(8,128)S(1)}) custom-call(f32[1,512]{1,0:T(1,128)S(1)} %bitcast.4, f32[5,512]{1,0:T(8,128)S(1)} %copy-done.1, f32[16,8,128]{2,1,0:T(8,128)S(1)} %get-tuple-element.19.factor_ref, ...), custom_call_target="tpu_custom_call", output_to_operand_aliasing={{1}: (5, {})} | custom-call | tf_op jit(solution)/shard_map/bulk_update/pallas_call | solution.py:509
  39.8 0.0 collective-permute-done.3.flux_ref
  39.8 0.0 collective-permute-done.4.refs_1_
  39.8 0.0 copy-done.2
  39.8 0.0 copy-done.4
  39.8 3.8 %put_filtered.1 = f32[5,16,128,512]{3,2,1,0:T(8,128)} custom-call(s32[1,32]{1,0:T(1,128)S(1)} %bitcast.6, bf16[2,128,256]{2,1,0:T(8,128)(2,1)S(1)} %copy-done.2, f32[1,512]{1,0:T(1,128)S(1)} %bitcast.5, f32[16,8,128]{2,1,0:T(8,128)S(1)} %get-tuple-element.19.factor_ref, ...), custom_call_target="tpu_custom_call", output_to_operand_aliasing={{}: (11, {})} | custom-call | tf_op jit(solution)/shard_map/put_filtered/pallas_call | solution.py:601
  (2 shorter events, 0.0 us)
Async XLA Ops:
  0.0 8.5 %copy-start = (f32[5,16,128,512]{3,2,1,0:T(8,128)S(1)}, f32[5,16,128,512]{3,2,1,0:T(8,128)}, u32[]{:S(2)}) copy-start(f32[5,16,128,512]{3,2,1,0:T(8,128)} %state_ref.7) | copy-start | bytes 62914564
  2.2 14.8 %collective-permute-start = (f32[5,128,512]{2,1,0:T(8,128)S(1)}, f32[5,128,512]{2,1,0:T(8,128)S(1)}, u32[]{:S(2)}, u32[]{:S(2)}) collective-permute-start(f32[5,128,512]{2,1,0:T(8,128)S(1)} %get-tuple-element.20), channel_id=1, source_target_pairs={{2,0},{0,2},{6,4},{4,6},{10,8},{8,10},{14,12},{12,14},{18,16},{16,... | collective-permute-start | bytes 3932168 | tf_op jit(solution)/shard_map/ppermute | solution.py:678
  2.3 14.7 %collective-permute-start.1 = (f32[5,128,128]{2,1,0:T(8,128)S(1)}, f32[5,128,128]{2,1,0:T(8,128)S(1)}, u32[]{:S(2)}, u32[]{:S(2)}) collective-permute-start(f32[5,128,128]{2,1,0:T(8,128)S(1)} %get-tuple-element.21), channel_id=1, source_target_pairs={{2,4},{6,8},{10,12},{14,16},{18,20},{22,24},{26,28},{4,2},{8,6},{1... | collective-permute-start | bytes 983048 | tf_op jit(solution)/shard_map/ppermute | solution.py:677
  7.2 9.8 %collective-permute-start.2 = (f32[2,5,16,512]{3,2,1,0:T(8,128)S(1)}, f32[2,5,16,512]{3,2,1,0:T(8,128)S(1)}, u32[]{:S(2)}, u32[]{:S(2)}) collective-permute-start(f32[2,5,16,512]{3,2,1,0:T(8,128)S(1)} %get-tuple-element.22), channel_id=1, source_target_pairs={{0,1},{1,0},{2,3},{3,2},{4,5},{5,4},{6,7},{7,6},{8,9},{9,8},{10,11... | collective-permute-start | bytes 983048 | tf_op jit(solution)/shard_map/ppermute | solution.py:674
  13.0 26.8 %collective-permute-start.3 = (f32[5,128,384]{2,1,0:T(8,128)S(1)}, f32[5,128,384]{2,1,0:T(8,128)S(1)}, u32[]{:S(2)}, u32[]{:S(2)}) collective-permute-start(f32[5,128,384]{2,1,0:T(8,128)S(1)} %gate.1), channel_id=1, source_target_pairs={{2,4},{6,8},{10,12},{14,16},{18,20},{22,24},{26,28},{4,2},{8,6},{1... | collective-permute-start | bytes 2949128 | tf_op jit(solution)/shard_map/ppermute | solution.py:687
  17.0 6.0 %copy-start.1 = (f32[5,512]{1,0:T(8,128)S(1)}, f32[5,512]{1,0:T(8,128)}, u32[]{:S(2)}) copy-start(f32[5,512]{1,0:T(8,128)} %target_ref.5) | copy-start | bytes 30724
  17.0 6.0 %copy-start.3 = (f32[512]{0:T(512)S(1)}, f32[512]{0:T(512)}, u32[]{:S(2)}) copy-start(f32[512]{0:T(512)} %param.12) | copy-start | bytes 6148
  21.7 18.1 %collective-permute-start.4 = (f32[1304,128]{1,0:T(8,128)S(1)}, f32[1304,128]{1,0:T(8,128)S(1)}, u32[]{:S(2)}, u32[]{:S(2)}) collective-permute-start(f32[1304,128]{1,0:T(8,128)S(1)} %get-tuple-element.31.refs_0_), channel_id=1, source_target_pairs={{0,1},{1,0},{2,3},{3,2},{4,5},{5,4},{6,7},{7,6},{8,9},{9,8},{10,11... | collective-permute-start | bytes 2002952 | tf_op jit(solution)/shard_map/ppermute | solution.py:674
  23.0 16.8 %copy-start.2 = (bf16[2,128,256]{2,1,0:T(8,128)(2,1)S(1)}, bf16[2,128,256]{2,1,0:T(8,128)(2,1)}, u32[]{:S(2)}) copy-start(bf16[2,128,256]{2,1,0:T(8,128)(2,1)} %constant.8.clone.table_ref) | copy-start | bytes 393220
  23.0 16.8 %copy-start.4 = (s32[32]{0:T(128)S(1)}, s32[32]{0:T(128)}, u32[]{:S(2)}) copy-start(s32[32]{0:T(128)} %param.14) | copy-start | bytes 388
